TPU v7x, 512 devices: a whole 4x8x8 slice. The times are simulated.
512 devices in a mesh: dp: 8 (over y_hi, core), expert: 64 (over z, y_lo, x).
Axes of the slice: x: 4, y: 8 (y_hi: 4, y_lo: 2; y = y_hi * 2 + y_lo), z: 8, core: 2. Of those that a mesh axis runs over, the one named last changes fastest.
Arguments:
- tokens: bfloat16 [4096, 2048], P('expert', 'dp'), may hold values from -6 to 6
- expert_ids: int32 [4096, 8], P('expert'), may hold values from 0 to 63, as said below
- router_probs: float32 [4096, 8], P('expert'), may hold values from 0.05 to 1
- w_gate: bfloat16 [64, 2048, 3072], P('expert', None, 'dp'), may hold values from -0.125 to 0.125
- w_up: bfloat16 [64, 2048, 3072], P('expert', None, 'dp'), may hold values from -0.125 to 0.125
- w_down: bfloat16 [64, 3072, 2048], P('expert', 'dp'), may hold values from -0.109375 to 0.109375
Outputs:
- mixed: bfloat16 [4096, 2048], P('expert', 'dp')
Inputs may be any that keep to these rules, and one draw needn't show every extreme that they name: `expert_ids`: A row's 8 ids differ. In each aligned block of 64 rows (the rows of one device) no expert is named more than 12 times; 8 experts, the same in all blocks and chosen by the seed, are named exactly 12 times in every block; every expert is named somewhere.
All inputs are finite; a program needn't handle non-finite values.
Results may differ from a plain program's by a relative error of at most 0.02.
Values may be sent and summed in bfloat16 or wider, within the bound.
No kernel may reach another device: no remote copies, remote signals or barrier semaphores. Data moves between devices by JAX's collectives and lax.ppermute only.
A program may use at most 64 MiB of HBM per device.

v0:
```python
import jax
import jax.numpy as jnp
from jax import lax
from jax.sharding import PartitionSpec as P


def seat_numbers(expert_ids, capacity, experts):
    row_count, fanout = expert_ids.shape
    flat_ids = expert_ids.reshape(row_count * fanout)
    labels = jnp.arange(experts, dtype=jnp.int32)
    onehot = (flat_ids[:, None] == labels[None, :]).astype(jnp.int32)
    before = jnp.cumsum(onehot, axis=0) - onehot
    slot_no = jnp.sum(before * onehot, axis=1)
    return (flat_ids * capacity + slot_no).reshape(row_count, fanout)


def body(tokens, expert_ids, router_probs, w_gate, w_up, w_down):
    tok_rows = tokens.shape[0]
    fanout = expert_ids.shape[1]
    local_experts = w_gate.shape[0]
    features = w_gate.shape[1]
    owners = lax.axis_size("expert")
    groups = lax.axis_size("dp")
    experts = local_experts * owners
    capacity = 3 * tok_rows * fanout // (2 * experts)
    seat_count = experts * capacity
    band = features // groups
    places = seat_numbers(expert_ids, capacity, experts)
    seat_ids = jnp.arange(seat_count, dtype=jnp.int32)
    chooser = jnp.any(places[None, :, :] == seat_ids[:, None, None], axis=2).astype(jnp.bfloat16)
    full_tokens = lax.all_gather(tokens, "dp", axis=1, tiled=True)
    dispatched = jnp.dot(chooser, full_tokens, preferred_element_type=jnp.float32).astype(
        jnp.bfloat16
    )
    dispatched = dispatched.reshape(experts, capacity, features)
    arrived = lax.all_to_all(dispatched, "expert", split_axis=0, concat_axis=0, tiled=True)
    arrived = arrived.reshape(owners, local_experts, capacity, features)
    gate_part = jnp.einsum("ojcd,jdf->ojcf", arrived, w_gate, preferred_element_type=jnp.float32)
    up_part = jnp.einsum("ojcd,jdf->ojcf", arrived, w_up, preferred_element_type=jnp.float32)
    hidden = (jax.nn.silu(gate_part) * up_part).astype(jnp.bfloat16)
    partial_terms = jnp.einsum("ojcf,jfd->ojcd", hidden, w_down, preferred_element_type=jnp.float32)
    summed = lax.psum(partial_terms.astype(jnp.bfloat16), "dp")
    returned = summed.reshape(experts, capacity, features)
    at_home = lax.all_to_all(returned, "expert", split_axis=0, concat_axis=0, tiled=True)
    at_home = at_home.reshape(seat_count, features)
    at_home = lax.dynamic_slice_in_dim(at_home, lax.axis_index("dp") * band, band, 1)
    shares = (router_probs / jnp.sum(router_probs, axis=1, keepdims=True)).astype(jnp.bfloat16)
    mixing = jnp.sum(
        jnp.where(
            places[:, :, None] == seat_ids[None, None, :],
            shares[:, :, None],
            jnp.zeros((), jnp.bfloat16),
        ),
        axis=1,
    )
    return jnp.dot(mixing, at_home, preferred_element_type=jnp.float32).astype(jnp.bfloat16)


def solution(mesh):
    return jax.shard_map(
        body,
        mesh=mesh,
        in_specs=(
            P("expert", "dp"),
            P("expert", None),
            P("expert", None),
            P("expert", None, "dp"),
            P("expert", None, "dp"),
            P("expert", "dp", None),
        ),
        out_specs=P("expert", "dp"),
        check_vma=False,
    )
```

profile of v0, /device:TPU:133, one launch (start us, length us, event | category | flops | bytes accessed | tf_op | source)
XLA Modules:
  0.0 394.0 jit_solution(8653412462759266420)
XLA Ops:
  6.5 0.0 copy-start
  6.5 0.0 all-reduce.2.cloned.1.call-start
  6.5 0.9 copy.37
  7.4 0.1 eq.55
  7.5 0.1 eq.51
  7.6 1.2 reduce-window.6
  8.8 0.2 slice_reduce_fusion
  9.1 0.1 fusion.43
  9.2 0.1 reduce_sum.33
  9.3 0.1 copy.40
  9.4 0.7 multiply_add_fusion
  10.1 0.1 copy.41
  10.2 0.5 fusion.8
  10.7 17.8 %all_gather.3 = bf16[64,2048]{1,0:T(8,128)(2,1)S(1)} all-gather(bf16[64,256]{1,0:T(8,128)(2,1)} %param.6), channel_id=1, replica_groups=mesh['dp'=8,'expert'=64] {'dp'}, dimensions={1}, use_global_device_ids=true | all-gather | bytes 294912 | tf_op jit(solution)/shard_map/all_gather | solution.py:31
  28.5 2.7 convolution_convert_fusion.1
  31.2 6.1 %reshape.63 = bf16[64,12,2048]{2,1,0:T(8,128)(2,1)} reshape(bf16[768,2048]{1,0:T(8,128)(2,1)} %convolution_convert_fusion.1) | data formatting | bytes 6291456 | tf_op jit(solution)/shard_map/reshape | solution.py:35
  37.3 0.0 copy-start.3
  37.3 107.4 %all_to_all.10 = bf16[64,12,2048]{2,1,0:T(8,128)(2,1)S(1)} all-to-all(bf16[64,12,2048]{2,1,0:T(8,128)(2,1)} %reshape.63), channel_id=1, replica_groups=mesh['dp'=8,'expert'=64] {'expert'}, dimensions={0} | all-to-all | bytes 6291456 | tf_op jit(solution)/shard_map/all_to_all | solution.py:36
  144.7 0.0 copy-start.1
  144.7 1.9 copy-done.1
  146.6 0.0 copy-done.3
  146.6 0.0 copy-start.4
  146.6 3.0 fusion.9
  149.6 0.0 copy-done
  149.6 0.0 copy-done.4
  149.6 7.9 %convolution_convert_fusion = bf16[64,12,2048]{2,0,1:T(8,128)(2,1)} fusion(bf16[1,384,2048]{2,1,0:T(8,128)(2,1)S(1)} %copy-done, bf16[1,2048,384]{2,1,0:T(8,128)(2,1)S(1)} %copy-done.4, bf16[64,12,2048]{2,1,0:T(8,128)(2,1)} %copy-done.1, f32[64,1,12,384]{3,0,2,1:T(8,128)} %fusion.9), kind=kOutput, calls=%fused_computation | convolution fusion | flops 2419261440 | bytes 10616832 | tf_op jit(solution)/shard_map/ojcf,jfd->ojcd/dot_general | solution.py:41
  157.5 0.0 all-reduce.2.cloned.1.call-update
  157.5 103.0 %all-reduce.2.cloned.1.call-done = bf16[64,12,2048]{2,0,1:T(8,128)(2,1)} async-done(((bf16[64,12,2048]{2,0,1:T(8,128)(2,1)}), bf16[64,12,2048]{2,0,1:T(8,128)(2,1)}) %all-reduce.2.cloned.1.call-update) | async-done | bytes 3145744 | tf_op jit(solution)/shard_map/psum | solution.py:42
  260.5 5.7 %copy.46 = bf16[64,12,2048]{2,1,0:T(8,128)(2,1)} copy(bf16[64,12,2048]{2,0,1:T(8,128)(2,1)} %all-reduce.2.cloned.1.call-done) | data formatting | bytes 6291456 | tf_op jit(solution)/shard_map/psum | solution.py:42
  266.2 0.0 copy-start.2
  266.2 12.0 %all-to-all-start.1 = ((bf16[64,12,2048]{2,1,0:T(8,128)(2,1)}), bf16[64,12,2048]{2,1,0:T(8,128)(2,1)}, u32[]{:S(2)}, u32[]{:S(2)}) async-start(bf16[64,12,2048]{2,1,0:T(8,128)(2,1)} %copy.46), calls=%async_computation.1 | async-start | bytes 8388608 | tf_op jit(solution)/shard_map/all_to_all | solution.py:44
  278.2 0.0 copy-done.2
  278.2 0.1 copy.42
  278.3 0.6 fusion.38
  278.9 100.2 %all-to-all-done.1 = bf16[64,12,2048]{2,1,0:T(8,128)(2,1)} async-done(((bf16[64,12,2048]{2,1,0:T(8,128)(2,1)}), bf16[64,12,2048]{2,1,0:T(8,128)(2,1)}, u32[]{:S(2)}, u32[]{:S(2)}) %all-to-all-start.1) | async-done | bytes 3145760 | tf_op jit(solution)/shard_map/all_to_all | solution.py:44
  379.1 6.2 %reshape.69 = bf16[768,2048]{1,0:T(8,128)(2,1)} reshape(bf16[64,12,2048]{2,1,0:T(8,128)(2,1)} %all-to-all-done.1) | data formatting | bytes 6291456 | tf_op jit(solution)/shard_map/reshape | solution.py:45
  385.3 1.8 convolution_convert_fusion.2
  (5 shorter events, 0.1 us)
Async XLA Ops:
  6.5 143.1 %copy-start = (bf16[1,384,2048]{2,1,0:T(8,128)(2,1)S(1)}, bf16[1,384,2048]{2,1,0:T(8,128)(2,1)}, u32[]{:S(2)}) copy-start(bf16[1,384,2048]{2,1,0:T(8,128)(2,1)} %param.11) | copy-start | bytes 4718596
  6.5 254.0 %all-reduce.2.cloned.1.call-start = ((), (), s32[]{:S(2)}) async-start(), calls=%async_computation.2 | async-start | bytes 6291456 | tf_op jit(solution)/shard_map/psum | solution.py:42
  37.3 109.4 %copy-start.3 = (bf16[1,2048,384]{2,1,0:T(8,128)(2,1)S(1)}, bf16[1,2048,384]{2,1,0:T(8,128)(2,1)}, u32[]{:S(2)}) copy-start(bf16[1,2048,384]{2,1,0:T(8,128)(2,1)} %param.9) | copy-start | bytes 4718596
  144.7 1.9 copy-start.1
  146.6 3.0 copy-start.4
  266.2 12.0 %copy-start.2 = (f32[64,8]{0,1:T(8,128)S(1)}, f32[64,8]{0,1:T(8,128)}, u32[]{:S(2)}) copy-start(f32[64,8]{0,1:T(8,128)} %param.8) | copy-start | bytes 6148
  266.2 113.0 %all-to-all-start.1 = ((bf16[64,12,2048]{2,1,0:T(8,128)(2,1)}), bf16[64,12,2048]{2,1,0:T(8,128)(2,1)}, u32[]{:S(2)}, u32[]{:S(2)}) async-start(bf16[64,12,2048]{2,1,0:T(8,128)(2,1)} %copy.46), calls=%async_computation.1 | async-start | bytes 8388608 | tf_op jit(solution)/shard_map/all_to_all | solution.py:44
Sparse Core Ops, SparseCore 0:
  157.7 102.7 all-reduce.1
where the time goes:
time: 395 us; the launch traced here: 394 us
  waiting for transfers between devices  203 us (51%)
  blocking collectives  125 us (32%)
  local copies, waits for them, and re-layouts  21.5 us (5%)
  matrix products  15.4 us (4%)
  between operations  13.5 us (3%)
  starting transfers between devices  12 us (3%)
    all_to_all x1, blocking collectives, body(): lax.all_to_all(dispatched, 'expert', split_axis=0, concat_axis=0, tiled=T...  107 us
    psum x1, waiting for transfers between devices, body(): summed = lax.psum(partial_terms.astype(jnp.bfloat16), 'dp')  103 us
    all_to_all x1, waiting for transfers between devices, body(): lax.all_to_all(returned, 'expert', split_axis=0, concat_axis=0, tiled=True)  100 us
    all_gather x1, blocking collectives, body(): full_tokens = lax.all_gather(tokens, 'dp', axis=1, tiled=True)  17.8 us
    all_to_all x1, starting transfers between devices, body(): lax.all_to_all(returned, 'expert', split_axis=0, concat_axis=0, tiled=True)  12 us
    dot_general x1, matrix products, body(): jnp.einsum('ojcf,jfd->ojcd', hidden, w_down, preferred_element_type=jnp.f...  7.9 us
  transfers between devices with their start and end apart: 2, of which 2 were waited for; matrix products, arithmetic and copies ran while one was open for 0% of the time, Pallas kernels for 0%

commit v1 on v0

v1 whole, which is shorter than its diff:
```python
import functools

import jax
import jax.numpy as jnp
from jax import lax
from jax.experimental import pallas as pl
from jax.experimental.pallas import tpu as pltpu
from jax.sharding import PartitionSpec as P

BF = jnp.bfloat16
F32 = jnp.float32
NEAR = 8
FAR = 4
VM = pl.BlockSpec(memory_space=pltpu.VMEM)


def call(kernel, outs, name, limit=48 << 20, flops=0, moved=0, smem=False):
    def run(*args):
        specs = [VM] * len(args)
        if smem:
            specs[0] = pl.BlockSpec(memory_space=pltpu.SMEM)
        return pl.pallas_call(
            kernel,
            out_shape=[jax.ShapeDtypeStruct(s, t) for s, t in outs],
            in_specs=specs,
            out_specs=[VM] * len(outs),
            compiler_params=pltpu.CompilerParams(vmem_limit_bytes=limit),
            cost_estimate=pl.CostEstimate(flops=flops, bytes_accessed=moved, transcendentals=0),
            name=name,
        )(*args)

    return run


def dot(a, b):
    return jnp.dot(a, b, preferred_element_type=F32)


def dot_t(a, b):
    return lax.dot_general(a, b, (((0,), (0,)), ((), ())), preferred_element_type=F32)


def pick_kernel(ids, probs, tokens, wire1, pick2, mix1, mix2):
    rows, fanout = ids.shape
    experts = wire1.shape[0] // NEAR
    label = lax.broadcasted_iota(jnp.int32, (rows, experts), 1)
    p = probs[...]
    shares = (p / jnp.sum(p, axis=1, keepdims=True)).astype(BF).astype(F32)
    named = jnp.zeros((rows, experts), F32)
    share = jnp.zeros((rows, experts), F32)
    for k in range(fanout):
        hit = ids[:, k : k + 1] == label
        named = jnp.where(hit, 1.0, named)
        share = jnp.where(hit, shares[:, k : k + 1], share)
    i0 = lax.broadcasted_iota(jnp.int32, (rows, rows), 0)
    i1 = lax.broadcasted_iota(jnp.int32, (rows, rows), 1)
    eye = (i0 == i1).astype(BF)
    earlier = (i0 < i1).astype(BF)
    named = named.astype(BF)
    named_t = dot_t(named, eye)
    before_t = dot_t(named, earlier)
    share_t = dot_t(share.astype(BF), eye)
    seat = jnp.where(named_t > 0.5, before_t, -1.0).astype(jnp.int32)

    def spread(values, count):
        return jnp.broadcast_to(values[:, None, :], (experts, count, rows)).reshape(
            experts * count, rows
        )

    place = lax.broadcasted_iota(jnp.int32, (experts * NEAR, rows), 0) % NEAR
    hit1 = spread(seat, NEAR) == place
    one1 = hit1.astype(F32).astype(BF)
    mix1[...] = jnp.where(hit1, spread(share_t, NEAR), 0.0).astype(BF)
    hit2 = spread(seat, 2 * FAR) == (place % FAR) + NEAR
    pick = hit2.astype(F32)
    mix = jnp.where(hit2, spread(share_t, 2 * FAR), 0.0)
    low = place < FAR
    pick2[:, :rows] = jnp.where(low, pick, 0.0).astype(BF)
    pick2[:, rows:] = jnp.where(low, 0.0, pick).astype(BF)
    mix2[:, :rows] = jnp.where(low, mix, 0.0).astype(BF)
    mix2[:, rows:] = jnp.where(low, 0.0, mix).astype(BF)
    wire1[...] = dot(one1, tokens[...]).astype(BF)


def wire2_kernel(pick2, t0, t1, t2, t3, wire2):
    rows, band = t0.shape
    low = pick2[:, :rows]
    high = pick2[:, rows:]
    wire2[:, :band] = (dot(low, t0[...]) + dot(high, t2[...])).astype(BF)
    wire2[:, band:] = (dot(low, t1[...]) + dot(high, t3[...])).astype(BF)


def order(count):
    half = count // 2
    i = lax.broadcasted_iota(jnp.int32, (count, count), 0)
    j = lax.broadcasted_iota(jnp.int32, (count, count), 1)
    r = i % half
    return (j == (r // FAR) * (2 * FAR) + (i // half) * FAR + r % FAR).astype(F32).astype(BF)


def expert_kernel(where, *refs):
    own1, sib1 = refs[0:4], refs[4:8]
    own2, sib2, wg, wu, wd = refs[8:13]
    keep1, give1, keep2, give2 = refs[13:17]
    yh, core = where[0], where[1]
    band = own1[0].shape[1]
    rows1 = own1[0].shape[0]
    rows2 = own2.shape[0] // 2
    step = 256

    def offset(k, parity):
        return pl.multiple_of((2 * (k % 4) + parity) * band, band)

    seq = order(own2.shape[0])
    a_own = dot(seq, own2[...]).astype(BF)
    a_sib = dot(seq, sib2[...]).astype(BF)

    def chunk(pieces):
        g = None
        for piece, at in pieces:
            pg = dot(piece, wg[pl.ds(at, band), :])
            pu = dot(piece, wu[pl.ds(at, band), :])
            g, u = (pg, pu) if g is None else (g + pg, u + pu)
        return (g / (1.0 + jnp.exp(-g)) * u).astype(BF)

    far = []
    for k in range(4):
        r = slice((k // 2) * rows2, (k // 2 + 1) * rows2)
        c = slice((k % 2) * band, (k % 2 + 1) * band)
        far.append((a_own[r, c], offset(yh + 4 - k, core)))
        far.append((a_sib[r, c], offset(yh + 4 - k, 1 - core)))
    h2 = chunk(far)
    for k in range(4):
        at = offset(yh + k, 1 - core)
        give2[k] = dot(h2, wd[:, pl.ds(at, band)]).astype(BF)
        at = offset(yh + k, core)
        keep2[k] = dot(h2, wd[:, pl.ds(at, band)]).astype(BF)
    for m in range(0, rows1, step):
        near = []
        for k in range(4):
            near.append((own1[k][m : m + step, :], offset(yh + 4 - k, core)))
            near.append((sib1[k][m : m + step, :], offset(yh + 4 - k, 1 - core)))
        h1 = chunk(near)
        for k in range(4):
            at = offset(yh + k, 1 - core)
            give1[k, m : m + step, :] = dot(h1, wd[:, pl.ds(at, band)]).astype(BF)
            at = offset(yh + k, core)
            keep1[k, m : m + step, :] = dot(h1, wd[:, pl.ds(at, band)]).astype(BF)


def far_sum_kernel(keep2, give2, wire):
    rows, band = keep2.shape[1:]
    seq = order(2 * rows)
    for col in range(2):
        parts = []
        for half in range(2):
            k = 2 * half + col
            s = keep2[k].astype(F32) + give2[k].astype(F32)
            parts.append(s.astype(BF))
        both = jnp.concatenate(parts, axis=0)
        wire[:, col * band : (col + 1) * band] = dot_t(seq, both).astype(BF)


def far_mix_kernel(mix2, home, out):
    rows = out.shape[1]
    band = out.shape[2]
    for k in range(4):
        half, col = k // 2, k % 2
        out[k] = dot_t(
            mix2[:, half * rows : (half + 1) * rows], home[:, col * band : (col + 1) * band]
        ).astype(BF)


def last_kernel(mix1, home, f0, f1, f2, f3, out):
    total = dot_t(mix1[...], home[...])
    for f in (f0, f1, f2, f3):
        total = total + f[...].astype(F32)
    out[...] = total.astype(BF)


def body(tokens, expert_ids, router_probs, w_gate, w_up, w_down):
    rows, band = tokens.shape
    owners = lax.axis_size("expert")
    groups = lax.axis_size("dp")
    experts = owners
    features = w_gate.shape[1]
    seats1, seats2 = experts * NEAR, experts * FAR
    me = lax.axis_index("dp")
    where = jnp.stack([me // 2, me % 2]).astype(jnp.int32)

    def shift(x, k):
        return lax.ppermute(x, "dp", [(i, (i + 2 * k) % groups) for i in range(groups)])

    def swap(x):
        return lax.ppermute(x, "dp", [(i, i ^ 1) for i in range(groups)])

    def trade(x):
        x = x.reshape(experts, x.shape[0] // experts, x.shape[1])
        x = lax.all_to_all(x, "expert", split_axis=0, concat_axis=0, tiled=True)
        return x.reshape(-1, x.shape[2])

    bands = [tokens] + [shift(tokens, k) for k in (1, 2, 3)]
    wire1, pick2, mix1, mix2 = call(
        pick_kernel,
        [((seats1, band), BF), ((seats1, 2 * rows), BF), ((seats1, rows), BF), ((seats1, 2 * rows), BF)],
        "pick",
    )(expert_ids, router_probs, tokens)
    got1 = trade(wire1)
    (wire2,) = call(wire2_kernel, [((seats1, 2 * band), BF)], "wire2")(pick2, *bands)
    got2 = trade(wire2)
    own1 = [got1] + [shift(got1, k) for k in (1, 2, 3)]
    sib1 = [swap(x) for x in own1]
    sib2 = swap(got2)
    keep1, give1, keep2, give2 = call(
        expert_kernel,
        [
            ((4, seats1, band), BF),
            ((4, seats1, band), BF),
            ((4, seats2, band), BF),
            ((4, seats2, band), BF),
        ],
        "expert",
        smem=True,
        flops=6 * (seats1 + seats2) * features * w_gate.shape[2],
        moved=12 << 20,
    )(where, *own1, *sib1, got2, sib2, w_gate[0], w_up[0], w_down[0])
    give2 = swap(give2)
    give1 = swap(give1)
    (back2,) = call(far_sum_kernel, [((seats1, 2 * band), BF)], "far_sum")(keep2, give2)
    home2 = trade(back2)
    pair1 = [(keep1[k].astype(F32) + give1[k].astype(F32)) for k in range(4)]
    sent = [shift(pair1[k].astype(BF), k) for k in (1, 2, 3)]
    back1 = pair1[0]
    for s in sent:
        back1 = back1 + s.astype(F32)
    home1 = trade(back1.astype(BF))
    (part2,) = call(far_mix_kernel, [((4, rows, band), BF)], "far_mix")(mix2, home2)
    fars = [part2[0]] + [shift(part2[k], k) for k in (1, 2, 3)]
    (out,) = call(last_kernel, [((rows, band), BF)], "last")(mix1, home1, *fars)
    return out


def solution(mesh):
    return jax.shard_map(
        body,
        mesh=mesh,
        in_specs=(
            P("expert", "dp"),
            P("expert", None),
            P("expert", None),
            P("expert", None, "dp"),
            P("expert", None, "dp"),
            P("expert", "dp", None),
        ),
        out_specs=P("expert", "dp"),
        check_vma=False,
    )
```

time: 395 us -> 181 us (0.46)
  the two profiles are of different devices: /device:TPU:133 before, /device:TPU:8 now
where the time goes in v1:
time: 181 us; the launch traced here: 179 us
  starting transfers between devices  114 us (63%)
  waiting for transfers between devices  39.8 us (22%)
  Pallas kernels  14.5 us (8%)
  local copies, waits for them, and re-layouts  9.69 us (5%)
    ppermute x12, starting transfers between devices, shift(): lax.ppermute(x, 'dp', [(i, (i + 2 * k) % groups) for i in range(groups)])  52.5 us
    all_to_all x4, starting transfers between devices, trade(): x = lax.all_to_all(x, 'expert', split_axis=0, concat_axis=0, tiled=True)  47.1 us
    ppermute x12, waiting for transfers between devices, shift(): lax.ppermute(x, 'dp', [(i, (i + 2 * k) % groups) for i in range(groups)])  34.2 us
    pallas_call x6, Pallas kernels, run(): pl.pallas_call(kernel, out_shape=[jax.ShapeDtypeStruct(s, t) for s, t in...  14.5 us
    ppermute x7, starting transfers between devices, swap(): return lax.ppermute(x, 'dp', [(i, i ^ 1) for i in range(groups)])  14.4 us
    unnamed x22, local copies, waits for them, and re-layouts  9.68 us
    all_to_all x4, waiting for transfers between devices, trade(): x = lax.all_to_all(x, 'expert', split_axis=0, concat_axis=0, tiled=True)  3.8 us
  transfers between devices with their start and end apart: 23, of which 11 were waited for; matrix products, arithmetic and copies ran while one was open for 1% of the time, Pallas kernels for 2%

profile of v1, /device:TPU:8, one launch (start us, length us, event | category | flops | bytes accessed | tf_op | source)
XLA Modules:
  0.0 179.4 jit_solution(793407706873141704)
XLA Ops:
  0.0 0.8 copy.7.ids
  0.8 0.8 copy.8.probs
  1.5 0.8 copy-done
  2.3 1.4 pick.1
  3.7 14.8 %all-to-all-start = ((bf16[64,8,256]{2,1,0:T(8,128)(2,1)}), bf16[64,8,256]{2,1,0:T(8,128)(2,1)S(1)}, u32[]{:S(2)}, u32[]{:S(2)}) async-start(bf16[64,8,256]{2,1,0:T(8,128)(2,1)} %bitcast.2), calls=%async_computation | async-start | bytes 524288 | tf_op jit(solution)/shard_map/all_to_all | solution.py:199
  18.5 6.8 %collective-permute-start.8 = (bf16[64,256]{1,0:T(8,128)(2,1)}, bf16[64,256]{1,0:T(8,128)(2,1)S(1)}, u32[]{:S(2)}, u32[]{:S(2)}) collective-permute-start(bf16[64,256]{1,0:T(8,128)(2,1)} %t0.1), channel_id=1, source_target_pairs={{0,256},{64,320},{128,384},{192,448},{256,0},{320,64},{384,128},{4... | collective-permute-start | bytes 98312 | tf_op jit(solution)/shard_map/ppermute | solution.py:192
  25.4 2.7 %collective-permute-start.7 = (bf16[64,256]{1,0:T(8,128)(2,1)}, bf16[64,256]{1,0:T(8,128)(2,1)S(1)}, u32[]{:S(2)}, u32[]{:S(2)}) collective-permute-start(bf16[64,256]{1,0:T(8,128)(2,1)} %t0.1), channel_id=1, source_target_pairs={{0,128},{64,192},{128,256},{192,320},{256,384},{320,448},{384,0},{... | collective-permute-start | bytes 98312 | tf_op jit(solution)/shard_map/ppermute | solution.py:192
  28.1 5.3 %collective-permute-start.9 = (bf16[64,256]{1,0:T(8,128)(2,1)}, bf16[64,256]{1,0:T(8,128)(2,1)S(1)}, u32[]{:S(2)}, u32[]{:S(2)}) collective-permute-start(bf16[64,256]{1,0:T(8,128)(2,1)} %t0.1), channel_id=1, source_target_pairs={{0,384},{64,448},{128,0},{192,64},{256,128},{320,192},{384,256},{4... | collective-permute-start | bytes 98312 | tf_op jit(solution)/shard_map/ppermute | solution.py:192
  33.8 1.4 collective-permute-done.9.t3
  35.2 0.8 copy-done.1
  36.0 1.3 wire2.1
  37.3 11.2 %all-to-all-start.1 = ((bf16[64,8,512]{2,1,0:T(8,128)(2,1)}), bf16[64,8,512]{2,1,0:T(8,128)(2,1)S(1)}, u32[]{:S(2)}, u32[]{:S(2)}) async-start(bf16[64,8,512]{2,1,0:T(8,128)(2,1)} %bitcast.4), calls=%async_computation.1 | async-start | bytes 1048576 | tf_op jit(solution)/shard_map/all_to_all | solution.py:199
  48.5 6.2 %collective-permute-start.2 = (bf16[512,256]{1,0:T(8,128)(2,1)S(1)}, bf16[512,256]{1,0:T(8,128)(2,1)S(1)}, u32[]{:S(2)}, u32[]{:S(2)}) collective-permute-start(bf16[512,256]{1,0:T(8,128)(2,1)S(1)} %bitcast.42), channel_id=1, source_target_pairs={{0,384},{64,448},{128,0},{192,64},{256,128},{320,192},{384,256},{4... | collective-permute-start | bytes 786440 | tf_op jit(solution)/shard_map/ppermute | solution.py:192
  54.7 3.1 %collective-permute-start.1 = (bf16[512,256]{1,0:T(8,128)(2,1)S(1)}, bf16[512,256]{1,0:T(8,128)(2,1)S(1)}, u32[]{:S(2)}, u32[]{:S(2)}) collective-permute-start(bf16[512,256]{1,0:T(8,128)(2,1)S(1)} %bitcast.43), channel_id=1, source_target_pairs={{0,256},{64,320},{128,384},{192,448},{256,0},{320,64},{384,128},{4... | collective-permute-start | bytes 786440 | tf_op jit(solution)/shard_map/ppermute | solution.py:192
  57.9 3.0 %collective-permute-start = (bf16[512,256]{1,0:T(8,128)(2,1)S(1)}, bf16[512,256]{1,0:T(8,128)(2,1)S(1)}, u32[]{:S(2)}, u32[]{:S(2)}) collective-permute-start(bf16[512,256]{1,0:T(8,128)(2,1)S(1)} %bitcast.44), channel_id=1, source_target_pairs={{0,128},{64,192},{128,256},{192,320},{256,384},{320,448},{384,0},{... | collective-permute-start | bytes 786440 | tf_op jit(solution)/shard_map/ppermute | solution.py:192
  60.9 3.8 %all-to-all-done.1 = bf16[64,8,512]{2,1,0:T(8,128)(2,1)S(1)} async-done(((bf16[64,8,512]{2,1,0:T(8,128)(2,1)}), bf16[64,8,512]{2,1,0:T(8,128)(2,1)S(1)}, u32[]{:S(2)}, u32[]{:S(2)}) %all-to-all-start.1) | async-done | bytes 524320 | tf_op jit(solution)/shard_map/all_to_all | solution.py:199
  64.7 1.9 %collective-permute-start.10 = (bf16[512,512]{1,0:T(8,128)(2,1)S(1)}, bf16[512,512]{1,0:T(8,128)(2,1)S(1)}, u32[]{:S(2)}, u32[]{:S(2)}) collective-permute-start(bf16[512,512]{1,0:T(8,128)(2,1)S(1)} %bitcast.40), channel_id=1, source_target_pairs={{0,64},{64,0},{128,192},{192,128},{256,320},{320,256},{384,448},{4... | collective-permute-start | bytes 1572872 | tf_op jit(solution)/shard_map/ppermute | solution.py:195
  66.6 2.4 %collective-permute-start.3 = (bf16[512,256]{1,0:T(8,128)(2,1)S(1)}, bf16[512,256]{1,0:T(8,128)(2,1)S(1)}, u32[]{:S(2)}, u32[]{:S(2)}) collective-permute-start(bf16[512,256]{1,0:T(8,128)(2,1)S(1)} %bitcast.45), channel_id=1, source_target_pairs={{0,64},{64,0},{128,192},{192,128},{256,320},{320,256},{384,448},{4... | collective-permute-start | bytes 786440 | tf_op jit(solution)/shard_map/ppermute | solution.py:195
  69.3 1.9 %collective-permute-start.6 = (bf16[512,256]{1,0:T(8,128)(2,1)S(1)}, bf16[512,256]{1,0:T(8,128)(2,1)S(1)}, u32[]{:S(2)}, u32[]{:S(2)}) collective-permute-start(bf16[512,256]{1,0:T(8,128)(2,1)S(1)} %collective-permute-done.2.refs_3_), channel_id=1, source_target_pairs={{0,64},{64,0},{128,192},{192,128},{256,320},{320,256},{384,448},{4... | collective-permute-start | bytes 786440 | tf_op jit(solution)/shard_map/ppermute | solution.py:195
  71.2 4.8 %collective-permute-done.1.refs_2_ = bf16[512,256]{1,0:T(8,128)(2,1)S(1)} collective-permute-done((bf16[512,256]{1,0:T(8,128)(2,1)S(1)}, bf16[512,256]{1,0:T(8,128)(2,1)S(1)}, u32[]{:S(2)}, u32[]{:S(2)}) %collective-permute-start.1) | collective-permute-done | bytes 262176 | tf_op jit(solution)/shard_map/ppermute | solution.py:192
  76.0 1.9 %collective-permute-start.5 = (bf16[512,256]{1,0:T(8,128)(2,1)S(1)}, bf16[512,256]{1,0:T(8,128)(2,1)S(1)}, u32[]{:S(2)}, u32[]{:S(2)}) collective-permute-start(bf16[512,256]{1,0:T(8,128)(2,1)S(1)} %collective-permute-done.1.refs_2_), channel_id=1, source_target_pairs={{0,64},{64,0},{128,192},{192,128},{256,320},{320,256},{384,448},{4... | collective-permute-start | bytes 786440 | tf_op jit(solution)/shard_map/ppermute | solution.py:195
  77.9 1.9 %collective-permute-done.refs_1_ = bf16[512,256]{1,0:T(8,128)(2,1)S(1)} collective-permute-done((bf16[512,256]{1,0:T(8,128)(2,1)S(1)}, bf16[512,256]{1,0:T(8,128)(2,1)S(1)}, u32[]{:S(2)}, u32[]{:S(2)}) %collective-permute-start) | collective-permute-done | bytes 262176 | tf_op jit(solution)/shard_map/ppermute | solution.py:192
  79.9 1.9 %collective-permute-start.4 = (bf16[512,256]{1,0:T(8,128)(2,1)S(1)}, bf16[512,256]{1,0:T(8,128)(2,1)S(1)}, u32[]{:S(2)}, u32[]{:S(2)}) collective-permute-start(bf16[512,256]{1,0:T(8,128)(2,1)S(1)} %collective-permute-done.refs_1_), channel_id=1, source_target_pairs={{0,64},{64,0},{128,192},{192,128},{256,320},{320,256},{384,448},{4... | collective-permute-start | bytes 786440 | tf_op jit(solution)/shard_map/ppermute | solution.py:195
  81.9 0.7 copy-done.2
  83.3 0.7 copy-done.6
  84.7 0.9 copy-done.3
  85.7 0.9 copy-done.5
  86.6 0.9 copy-done.7
  87.6 0.9 copy-done.9
  88.5 9.2 %expert.1 = (bf16[4,512,256]{2,1,0:T(8,128)(2,1)S(1)}, bf16[4,512,256]{2,1,0:T(8,128)(2,1)}, bf16[4,256,256]{2,1,0:T(8,128)(2,1)S(1)}, bf16[4,256,256]{2,1,0:T(8,128)(2,1)S(1)}) custom-call(s32[2]{0:T(128)S(1)} %pad_add_fusion.where, bf16[512,256]{1,0:T(8,128)(2,1)S(1)} %bitcast.46, bf16[512,256]{1,0:T(8,128)(2,1)S(1)} %collective-permute-done.refs_1_, ...), custom_call_target="tpu_custom_call" | custom-call | flops 3623878656 | bytes 12582912 | tf_op jit(solution)/shard_map/expert/pallas_call | solution.py:22
  97.8 2.4 %collective-permute-start.11 = (bf16[4,512,256]{2,1,0:T(8,128)(2,1)}, bf16[4,512,256]{2,1,0:T(8,128)(2,1)S(1)}, u32[]{:S(2)}, u32[]{:S(2)}) collective-permute-start(bf16[4,512,256]{2,1,0:T(8,128)(2,1)} %get-tuple-element.17), channel_id=1, source_target_pairs={{0,64},{64,0},{128,192},{192,128},{256,320},{320,256},{384,448},{4... | collective-permute-start | bytes 3145736 | tf_op jit(solution)/shard_map/ppermute | solution.py:195
  100.1 1.9 %collective-permute-start.15 = (bf16[4,256,256]{2,1,0:T(8,128)(2,1)S(1)}, bf16[4,256,256]{2,1,0:T(8,128)(2,1)S(1)}, u32[]{:S(2)}, u32[]{:S(2)}) collective-permute-start(bf16[4,256,256]{2,1,0:T(8,128)(2,1)S(1)} %get-tuple-element.20), channel_id=1, source_target_pairs={{0,64},{64,0},{128,192},{192,128},{256,320},{320,256},{384,448},{4... | collective-permute-start | bytes 1572872 | tf_op jit(solution)/shard_map/ppermute | solution.py:195
  102.1 1.8 %collective-permute-done.15.give2 = bf16[4,256,256]{2,1,0:T(8,128)(2,1)S(1)} collective-permute-done((bf16[4,256,256]{2,1,0:T(8,128)(2,1)S(1)}, bf16[4,256,256]{2,1,0:T(8,128)(2,1)S(1)}, u32[]{:S(2)}, u32[]{:S(2)}) %collective-permute-start.15) | collective-permute-done | bytes 524320 | tf_op jit(solution)/shard_map/ppermute | solution.py:195
  103.9 1.4 far_sum.1
  105.3 11.3 %all-to-all-start.3 = ((bf16[64,8,512]{2,1,0:T(8,128)(2,1)}), bf16[64,8,512]{2,1,0:T(8,128)(2,1)S(1)}, u32[]{:S(2)}, u32[]{:S(2)}) async-start(bf16[64,8,512]{2,1,0:T(8,128)(2,1)} %bitcast.15), calls=%async_computation.3 | async-start | bytes 1048576 | tf_op jit(solution)/shard_map/all_to_all | solution.py:199
  116.8 5.0 %collective-permute-start.12 = (bf16[512,256]{1,0:T(8,128)(2,1)S(1)}, bf16[512,256]{1,0:T(8,128)(2,1)S(1)}, u32[]{:S(2)}, u32[]{:S(2)}) collective-permute-start(bf16[512,256]{1,0:T(8,128)(2,1)S(1)} %get-tuple-element.21), channel_id=1, source_target_pairs={{0,128},{64,192},{128,256},{192,320},{256,384},{320,448},{384,0},{... | collective-permute-start | bytes 786440 | tf_op jit(solution)/shard_map/ppermute | solution.py:192
  121.8 2.9 %collective-permute-start.14 = (bf16[512,256]{1,0:T(8,128)(2,1)S(1)}, bf16[512,256]{1,0:T(8,128)(2,1)S(1)}, u32[]{:S(2)}, u32[]{:S(2)}) collective-permute-start(bf16[512,256]{1,0:T(8,128)(2,1)S(1)} %get-tuple-element.22), channel_id=1, source_target_pairs={{0,384},{64,448},{128,0},{192,64},{256,128},{320,192},{384,256},{4... | collective-permute-start | bytes 786440 | tf_op jit(solution)/shard_map/ppermute | solution.py:192
  124.8 4.7 %collective-permute-start.13 = (bf16[512,256]{1,0:T(8,128)(2,1)S(1)}, bf16[512,256]{1,0:T(8,128)(2,1)S(1)}, u32[]{:S(2)}, u32[]{:S(2)}) collective-permute-start(bf16[512,256]{1,0:T(8,128)(2,1)S(1)} %get-tuple-element.23), channel_id=1, source_target_pairs={{0,256},{64,320},{128,384},{192,448},{256,0},{320,64},{384,128},{4... | collective-permute-start | bytes 786440 | tf_op jit(solution)/shard_map/ppermute | solution.py:192
  129.5 9.3 %collective-permute-done.14 = bf16[512,256]{1,0:T(8,128)(2,1)S(1)} collective-permute-done((bf16[512,256]{1,0:T(8,128)(2,1)S(1)}, bf16[512,256]{1,0:T(8,128)(2,1)S(1)}, u32[]{:S(2)}, u32[]{:S(2)}) %collective-permute-start.14) | collective-permute-done | bytes 262176 | tf_op jit(solution)/shard_map/ppermute | solution.py:192
  138.8 10.9 %collective-permute-done.13 = bf16[512,256]{1,0:T(8,128)(2,1)S(1)} collective-permute-done((bf16[512,256]{1,0:T(8,128)(2,1)S(1)}, bf16[512,256]{1,0:T(8,128)(2,1)S(1)}, u32[]{:S(2)}, u32[]{:S(2)}) %collective-permute-start.13) | collective-permute-done | bytes 262176 | tf_op jit(solution)/shard_map/ppermute | solution.py:192
  149.7 0.9 fusion.6
  150.5 9.8 %all-to-all-start.2 = ((bf16[64,8,256]{2,1,0:T(8,128)(2,1)}), bf16[64,8,256]{2,1,0:T(8,128)(2,1)S(1)}, u32[]{:S(2)}, u32[]{:S(2)}) async-start(bf16[64,8,256]{2,1,0:T(8,128)(2,1)} %fusion.6), calls=%async_computation.2 | async-start | bytes 524288 | tf_op jit(solution)/shard_map/all_to_all | solution.py:199
  160.8 6.5 %collective-permute-start.18 = (bf16[64,256]{1,0:T(8,128)(2,1)S(1)}, bf16[64,256]{1,0:T(8,128)(2,1)S(1)}, u32[]{:S(2)}, u32[]{:S(2)}) collective-permute-start(bf16[64,256]{1,0:T(8,128)(2,1)S(1)} %get-tuple-element.24), channel_id=1, source_target_pairs={{0,384},{64,448},{128,0},{192,64},{256,128},{320,192},{384,256},{4... | collective-permute-start | bytes 98312 | tf_op jit(solution)/shard_map/ppermute | solution.py:192
  167.3 3.2 %collective-permute-start.17 = (bf16[64,256]{1,0:T(8,128)(2,1)S(1)}, bf16[64,256]{1,0:T(8,128)(2,1)S(1)}, u32[]{:S(2)}, u32[]{:S(2)}) collective-permute-start(bf16[64,256]{1,0:T(8,128)(2,1)S(1)} %get-tuple-element.25), channel_id=1, source_target_pairs={{0,256},{64,320},{128,384},{192,448},{256,0},{320,64},{384,128},{4... | collective-permute-start | bytes 98312 | tf_op jit(solution)/shard_map/ppermute | solution.py:192
  170.5 3.0 %collective-permute-start.16 = (bf16[64,256]{1,0:T(8,128)(2,1)S(1)}, bf16[64,256]{1,0:T(8,128)(2,1)S(1)}, u32[]{:S(2)}, u32[]{:S(2)}) collective-permute-start(bf16[64,256]{1,0:T(8,128)(2,1)S(1)} %get-tuple-element.26), channel_id=1, source_target_pairs={{0,128},{64,192},{128,256},{192,320},{256,384},{320,448},{384,0},{... | collective-permute-start | bytes 98312 | tf_op jit(solution)/shard_map/ppermute | solution.py:192
  173.5 3.5 %collective-permute-done.17.f2 = bf16[64,256]{1,0:T(8,128)(2,1)S(1)} collective-permute-done((bf16[64,256]{1,0:T(8,128)(2,1)S(1)}, bf16[64,256]{1,0:T(8,128)(2,1)S(1)}, u32[]{:S(2)}, u32[]{:S(2)}) %collective-permute-start.17) | collective-permute-done | bytes 32800 | tf_op jit(solution)/shard_map/ppermute | solution.py:192
  177.0 1.6 collective-permute-done.16.f1
  178.6 0.8 last.1
  (30 shorter events, 2.9 us)
Async XLA Ops:
  1.5 0.8 copy-start
  3.7 33.5 %all-to-all-start = ((bf16[64,8,256]{2,1,0:T(8,128)(2,1)}), bf16[64,8,256]{2,1,0:T(8,128)(2,1)S(1)}, u32[]{:S(2)}, u32[]{:S(2)}) async-start(bf16[64,8,256]{2,1,0:T(8,128)(2,1)} %bitcast.2), calls=%async_computation | async-start | bytes 524288 | tf_op jit(solution)/shard_map/all_to_all | solution.py:199
  18.5 14.8 %collective-permute-start.8 = (bf16[64,256]{1,0:T(8,128)(2,1)}, bf16[64,256]{1,0:T(8,128)(2,1)S(1)}, u32[]{:S(2)}, u32[]{:S(2)}) collective-permute-start(bf16[64,256]{1,0:T(8,128)(2,1)} %t0.1), channel_id=1, source_target_pairs={{0,256},{64,320},{128,384},{192,448},{256,0},{320,64},{384,128},{4... | collective-permute-start | bytes 98312 | tf_op jit(solution)/shard_map/ppermute | solution.py:192
  25.4 8.5 %collective-permute-start.7 = (bf16[64,256]{1,0:T(8,128)(2,1)}, bf16[64,256]{1,0:T(8,128)(2,1)S(1)}, u32[]{:S(2)}, u32[]{:S(2)}) collective-permute-start(bf16[64,256]{1,0:T(8,128)(2,1)} %t0.1), channel_id=1, source_target_pairs={{0,128},{64,192},{128,256},{192,320},{256,384},{320,448},{384,0},{... | collective-permute-start | bytes 98312 | tf_op jit(solution)/shard_map/ppermute | solution.py:192
  28.1 7.2 %collective-permute-start.9 = (bf16[64,256]{1,0:T(8,128)(2,1)}, bf16[64,256]{1,0:T(8,128)(2,1)S(1)}, u32[]{:S(2)}, u32[]{:S(2)}) collective-permute-start(bf16[64,256]{1,0:T(8,128)(2,1)} %t0.1), channel_id=1, source_target_pairs={{0,384},{64,448},{128,0},{192,64},{256,128},{320,192},{384,256},{4... | collective-permute-start | bytes 98312 | tf_op jit(solution)/shard_map/ppermute | solution.py:192
  35.2 0.8 copy-start.1
  37.3 27.5 %all-to-all-start.1 = ((bf16[64,8,512]{2,1,0:T(8,128)(2,1)}), bf16[64,8,512]{2,1,0:T(8,128)(2,1)S(1)}, u32[]{:S(2)}, u32[]{:S(2)}) async-start(bf16[64,8,512]{2,1,0:T(8,128)(2,1)} %bitcast.4), calls=%async_computation.1 | async-start | bytes 1048576 | tf_op jit(solution)/shard_map/all_to_all | solution.py:199
  48.5 20.8 %collective-permute-start.2 = (bf16[512,256]{1,0:T(8,128)(2,1)S(1)}, bf16[512,256]{1,0:T(8,128)(2,1)S(1)}, u32[]{:S(2)}, u32[]{:S(2)}) collective-permute-start(bf16[512,256]{1,0:T(8,128)(2,1)S(1)} %bitcast.42), channel_id=1, source_target_pairs={{0,384},{64,448},{128,0},{192,64},{256,128},{320,192},{384,256},{4... | collective-permute-start | bytes 786440 | tf_op jit(solution)/shard_map/ppermute | solution.py:192
  54.7 21.3 %collective-permute-start.1 = (bf16[512,256]{1,0:T(8,128)(2,1)S(1)}, bf16[512,256]{1,0:T(8,128)(2,1)S(1)}, u32[]{:S(2)}, u32[]{:S(2)}) collective-permute-start(bf16[512,256]{1,0:T(8,128)(2,1)S(1)} %bitcast.43), channel_id=1, source_target_pairs={{0,256},{64,320},{128,384},{192,448},{256,0},{320,64},{384,128},{4... | collective-permute-start | bytes 786440 | tf_op jit(solution)/shard_map/ppermute | solution.py:192
  57.9 22.0 %collective-permute-start = (bf16[512,256]{1,0:T(8,128)(2,1)S(1)}, bf16[512,256]{1,0:T(8,128)(2,1)S(1)}, u32[]{:S(2)}, u32[]{:S(2)}) collective-permute-start(bf16[512,256]{1,0:T(8,128)(2,1)S(1)} %bitcast.44), channel_id=1, source_target_pairs={{0,128},{64,192},{128,256},{192,320},{256,384},{320,448},{384,0},{... | collective-permute-start | bytes 786440 | tf_op jit(solution)/shard_map/ppermute | solution.py:192
  64.7 20.0 %collective-permute-start.10 = (bf16[512,512]{1,0:T(8,128)(2,1)S(1)}, bf16[512,512]{1,0:T(8,128)(2,1)S(1)}, u32[]{:S(2)}, u32[]{:S(2)}) collective-permute-start(bf16[512,512]{1,0:T(8,128)(2,1)S(1)} %bitcast.40), channel_id=1, source_target_pairs={{0,64},{64,0},{128,192},{192,128},{256,320},{320,256},{384,448},{4... | collective-permute-start | bytes 1572872 | tf_op jit(solution)/shard_map/ppermute | solution.py:195
  66.6 15.2 %collective-permute-start.3 = (bf16[512,256]{1,0:T(8,128)(2,1)S(1)}, bf16[512,256]{1,0:T(8,128)(2,1)S(1)}, u32[]{:S(2)}, u32[]{:S(2)}) collective-permute-start(bf16[512,256]{1,0:T(8,128)(2,1)S(1)} %bitcast.45), channel_id=1, source_target_pairs={{0,64},{64,0},{128,192},{192,128},{256,320},{320,256},{384,448},{4... | collective-permute-start | bytes 786440 | tf_op jit(solution)/shard_map/ppermute | solution.py:195
  69.3 13.3 %collective-permute-start.6 = (bf16[512,256]{1,0:T(8,128)(2,1)S(1)}, bf16[512,256]{1,0:T(8,128)(2,1)S(1)}, u32[]{:S(2)}, u32[]{:S(2)}) collective-permute-start(bf16[512,256]{1,0:T(8,128)(2,1)S(1)} %collective-permute-done.2.refs_3_), channel_id=1, source_target_pairs={{0,64},{64,0},{128,192},{192,128},{256,320},{320,256},{384,448},{4... | collective-permute-start | bytes 786440 | tf_op jit(solution)/shard_map/ppermute | solution.py:195
  76.0 7.3 %collective-permute-start.5 = (bf16[512,256]{1,0:T(8,128)(2,1)S(1)}, bf16[512,256]{1,0:T(8,128)(2,1)S(1)}, u32[]{:S(2)}, u32[]{:S(2)}) collective-permute-start(bf16[512,256]{1,0:T(8,128)(2,1)S(1)} %collective-permute-done.1.refs_2_), channel_id=1, source_target_pairs={{0,64},{64,0},{128,192},{192,128},{256,320},{320,256},{384,448},{4... | collective-permute-start | bytes 786440 | tf_op jit(solution)/shard_map/ppermute | solution.py:195
  79.9 4.2 %collective-permute-start.4 = (bf16[512,256]{1,0:T(8,128)(2,1)S(1)}, bf16[512,256]{1,0:T(8,128)(2,1)S(1)}, u32[]{:S(2)}, u32[]{:S(2)}) collective-permute-start(bf16[512,256]{1,0:T(8,128)(2,1)S(1)} %collective-permute-done.refs_1_), channel_id=1, source_target_pairs={{0,64},{64,0},{128,192},{192,128},{256,320},{320,256},{384,448},{4... | collective-permute-start | bytes 786440 | tf_op jit(solution)/shard_map/ppermute | solution.py:195
  81.9 0.7 copy-start.2
  82.6 0.7 copy-start.4
  83.3 0.7 copy-start.6
  84.0 0.7 copy-start.8
  84.7 1.0 copy-start.3
  85.7 0.9 copy-start.5
  86.6 0.9 copy-start.7
  87.6 0.9 copy-start.9
  97.8 18.8 %collective-permute-start.11 = (bf16[4,512,256]{2,1,0:T(8,128)(2,1)}, bf16[4,512,256]{2,1,0:T(8,128)(2,1)S(1)}, u32[]{:S(2)}, u32[]{:S(2)}) collective-permute-start(bf16[4,512,256]{2,1,0:T(8,128)(2,1)} %get-tuple-element.17), channel_id=1, source_target_pairs={{0,64},{64,0},{128,192},{192,128},{256,320},{320,256},{384,448},{4... | collective-permute-start | bytes 3145736 | tf_op jit(solution)/shard_map/ppermute | solution.py:195
  100.1 3.8 %collective-permute-start.15 = (bf16[4,256,256]{2,1,0:T(8,128)(2,1)S(1)}, bf16[4,256,256]{2,1,0:T(8,128)(2,1)S(1)}, u32[]{:S(2)}, u32[]{:S(2)}) collective-permute-start(bf16[4,256,256]{2,1,0:T(8,128)(2,1)S(1)} %get-tuple-element.20), channel_id=1, source_target_pairs={{0,64},{64,0},{128,192},{192,128},{256,320},{320,256},{384,448},{4... | collective-permute-start | bytes 1572872 | tf_op jit(solution)/shard_map/ppermute | solution.py:195
  105.3 45.2 %all-to-all-start.3 = ((bf16[64,8,512]{2,1,0:T(8,128)(2,1)}), bf16[64,8,512]{2,1,0:T(8,128)(2,1)S(1)}, u32[]{:S(2)}, u32[]{:S(2)}) async-start(bf16[64,8,512]{2,1,0:T(8,128)(2,1)} %bitcast.15), calls=%async_computation.3 | async-start | bytes 1048576 | tf_op jit(solution)/shard_map/all_to_all | solution.py:199
  116.8 12.7 %collective-permute-start.12 = (bf16[512,256]{1,0:T(8,128)(2,1)S(1)}, bf16[512,256]{1,0:T(8,128)(2,1)S(1)}, u32[]{:S(2)}, u32[]{:S(2)}) collective-permute-start(bf16[512,256]{1,0:T(8,128)(2,1)S(1)} %get-tuple-element.21), channel_id=1, source_target_pairs={{0,128},{64,192},{128,256},{192,320},{256,384},{320,448},{384,0},{... | collective-permute-start | bytes 786440 | tf_op jit(solution)/shard_map/ppermute | solution.py:192
  121.8 16.9 %collective-permute-start.14 = (bf16[512,256]{1,0:T(8,128)(2,1)S(1)}, bf16[512,256]{1,0:T(8,128)(2,1)S(1)}, u32[]{:S(2)}, u32[]{:S(2)}) collective-permute-start(bf16[512,256]{1,0:T(8,128)(2,1)S(1)} %get-tuple-element.22), channel_id=1, source_target_pairs={{0,384},{64,448},{128,0},{192,64},{256,128},{320,192},{384,256},{4... | collective-permute-start | bytes 786440 | tf_op jit(solution)/shard_map/ppermute | solution.py:192
  124.8 24.9 %collective-permute-start.13 = (bf16[512,256]{1,0:T(8,128)(2,1)S(1)}, bf16[512,256]{1,0:T(8,128)(2,1)S(1)}, u32[]{:S(2)}, u32[]{:S(2)}) collective-permute-start(bf16[512,256]{1,0:T(8,128)(2,1)S(1)} %get-tuple-element.23), channel_id=1, source_target_pairs={{0,256},{64,320},{128,384},{192,448},{256,0},{320,64},{384,128},{4... | collective-permute-start | bytes 786440 | tf_op jit(solution)/shard_map/ppermute | solution.py:192
  150.5 28.1 %all-to-all-start.2 = ((bf16[64,8,256]{2,1,0:T(8,128)(2,1)}), bf16[64,8,256]{2,1,0:T(8,128)(2,1)S(1)}, u32[]{:S(2)}, u32[]{:S(2)}) async-start(bf16[64,8,256]{2,1,0:T(8,128)(2,1)} %fusion.6), calls=%async_computation.2 | async-start | bytes 524288 | tf_op jit(solution)/shard_map/all_to_all | solution.py:199
  160.8 12.7 %collective-permute-start.18 = (bf16[64,256]{1,0:T(8,128)(2,1)S(1)}, bf16[64,256]{1,0:T(8,128)(2,1)S(1)}, u32[]{:S(2)}, u32[]{:S(2)}) collective-permute-start(bf16[64,256]{1,0:T(8,128)(2,1)S(1)} %get-tuple-element.24), channel_id=1, source_target_pairs={{0,384},{64,448},{128,0},{192,64},{256,128},{320,192},{384,256},{4... | collective-permute-start | bytes 98312 | tf_op jit(solution)/shard_map/ppermute | solution.py:192
  167.3 9.7 %collective-permute-start.17 = (bf16[64,256]{1,0:T(8,128)(2,1)S(1)}, bf16[64,256]{1,0:T(8,128)(2,1)S(1)}, u32[]{:S(2)}, u32[]{:S(2)}) collective-permute-start(bf16[64,256]{1,0:T(8,128)(2,1)S(1)} %get-tuple-element.25), channel_id=1, source_target_pairs={{0,256},{64,320},{128,384},{192,448},{256,0},{320,64},{384,128},{4... | collective-permute-start | bytes 98312 | tf_op jit(solution)/shard_map/ppermute | solution.py:192
  170.5 8.2 %collective-permute-start.16 = (bf16[64,256]{1,0:T(8,128)(2,1)S(1)}, bf16[64,256]{1,0:T(8,128)(2,1)S(1)}, u32[]{:S(2)}, u32[]{:S(2)}) collective-permute-start(bf16[64,256]{1,0:T(8,128)(2,1)S(1)} %get-tuple-element.26), channel_id=1, source_target_pairs={{0,128},{64,192},{128,256},{192,320},{256,384},{320,448},{384,0},{... | collective-permute-start | bytes 98312 | tf_op jit(solution)/shard_map/ppermute | solution.py:192

commit v2 on v0

v2 whole, which is shorter than its diff:
```python
import jax
import jax.numpy as jnp
from jax import lax
from jax.experimental import pallas as pl
from jax.experimental.pallas import tpu as pltpu
from jax.sharding import PartitionSpec as P

BF = jnp.bfloat16
F32 = jnp.float32
NEAR = 8
FAR = 4
ROWS = 16
BANDS = 4
VM = pl.BlockSpec(memory_space=pltpu.VMEM)
SM = pl.BlockSpec(memory_space=pltpu.SMEM)


ANY = pl.BlockSpec(memory_space=pl.ANY)


def call(kernel, outs, name, specs, limit=8 << 20, flops=0, moved=0, scratch=()):
    return pl.pallas_call(
        kernel,
        out_shape=[jax.ShapeDtypeStruct(s, t) for s, t in outs],
        in_specs=specs,
        out_specs=[VM] * len(outs),
        scratch_shapes=list(scratch),
        compiler_params=pltpu.CompilerParams(vmem_limit_bytes=limit),
        cost_estimate=pl.CostEstimate(flops=flops, bytes_accessed=moved, transcendentals=0),
        name=name,
    )


def dot(a, b):
    return jnp.dot(a, b, preferred_element_type=F32)


def dot_t(a, b):
    return lax.dot_general(a, b, (((0,), (0,)), ((), ())), preferred_element_type=F32)


def pick_kernel(ids, probs, pick, mix):
    fanout, rows = ids.shape
    experts = pick.shape[0] // ROWS
    label = lax.broadcasted_iota(jnp.int32, (experts, rows), 0)
    p = probs[...]
    shares = (p / jnp.sum(p, axis=0, keepdims=True)).astype(BF).astype(F32)
    named = jnp.zeros((experts, rows), F32)
    share = jnp.zeros((experts, rows), F32)
    for k in range(fanout):
        hit = ids[k : k + 1, :] == label
        named = jnp.where(hit, 1.0, named)
        share = jnp.where(hit, shares[k : k + 1, :], share)
    i0 = lax.broadcasted_iota(jnp.int32, (rows, rows), 0)
    i1 = lax.broadcasted_iota(jnp.int32, (rows, rows), 1)
    before = dot(named.astype(BF), (i0 < i1).astype(F32).astype(BF))
    seat = jnp.where(named > 0.5, before, -1.0).astype(jnp.int32)

    def spread(values):
        return jnp.broadcast_to(values[:, None, :], (experts, ROWS, rows)).reshape(-1, rows)

    place = lax.broadcasted_iota(jnp.int32, (experts * ROWS, rows), 0) % ROWS
    seats = spread(seat)
    weights = spread(share)
    wanted = (
        place,
        place - NEAR,
        jnp.where((place >= NEAR) & (place < NEAR + FAR), place, 99),
        jnp.where(place >= NEAR + FAR, place - FAR, 99),
    )
    for i, want in enumerate(wanted):
        hit = seats == want
        if i == 0:
            hit = hit & (place < NEAR)
        elif i == 1:
            hit = hit & (want >= 0)
        pick[:, i * rows : (i + 1) * rows] = hit.astype(F32).astype(BF)
        mix[:, i * rows : (i + 1) * rows] = jnp.where(hit, weights, 0.0).astype(BF)


def wire_kernel(pick, toks, wire):
    rows, band = toks.shape[1:]
    low = pick[:, :rows]
    both = pick[:, : 2 * rows]
    far = pick[:, 2 * rows :]

    def pair(a, b):
        return jnp.concatenate([toks[a], toks[b]], axis=0)

    wire[:, :band] = dot(both, pair(0, 3)).astype(BF)
    wire[:, band : 2 * band] = (dot(low, toks[1]) + dot(far, pair(0, 2))).astype(BF)
    wire[:, 2 * band :] = (dot(low, toks[2]) + dot(far, pair(1, 3))).astype(BF)


def order(count):
    half = count // 2
    i = lax.broadcasted_iota(jnp.int32, (count, count), 0)
    j = lax.broadcasted_iota(jnp.int32, (count, count), 1)
    r = i % half
    return (j == (r // FAR) * (2 * FAR) + (i // half) * FAR + r % FAR).astype(F32).astype(BF)


def unpack(wire):
    band = wire.shape[1] // 3
    blocks = wire.shape[0] // ROWS
    tiles = wire[...].astype(F32).reshape(blocks, 2, NEAR, 3 * band)
    top = tiles[:, 0].reshape(blocks * NEAR, 3 * band).astype(BF)
    low = tiles[:, 1].reshape(blocks * NEAR, 3 * band).astype(BF)
    near = jnp.concatenate([top, low[:, :band]], axis=1)
    far = dot(order(blocks * NEAR), low[:, band:]).astype(BF)
    half = blocks * FAR
    far = jnp.concatenate([far[:half], far[half:]], axis=1)
    return near, far


def pack(near, far, wire):
    band = near.shape[1] // BANDS
    blocks = near.shape[0] // NEAR
    far = far.astype(BF)
    far = jnp.concatenate([far[:, : 2 * band], far[:, 2 * band :]], axis=0)
    far = dot_t(order(blocks * NEAR), far)
    low = jnp.concatenate([near[:, 3 * band :], far], axis=1)
    tiles = jnp.stack(
        [near[:, : 3 * band].reshape(blocks, NEAR, 3 * band), low.reshape(blocks, NEAR, 3 * band)],
        axis=1,
    )
    wire[...] = tiles.reshape(blocks * ROWS, 3 * band).astype(BF)


def fetch_pairs(parity, wg, wu, w, sems):
    band = w.shape[0] // BANDS
    wide = w.shape[1] // 2
    copies = []
    for k in range(BANDS):
        rows = pl.ds(pl.multiple_of((2 * k + parity) * band, band), band)
        for i, ref in enumerate((wg, wu)):
            copies.append(
                pltpu.make_async_copy(
                    ref.at[rows, :],
                    w.at[pl.ds(k * band, band), pl.ds(i * wide, wide)],
                    sems.at[2 * k + i],
                )
            )
    for c in copies:
        c.start()
    return copies


def first_kernel(where, own, wg, wu, acc, w, sems):
    copies = fetch_pairs(where[0], wg, wu, w, sems)
    near, far = unpack(own)
    n = near.shape[0]
    for c in copies:
        c.wait()
    acc[:n, :] = dot(near, w[...])
    acc[n:, :] = dot(far, w[...])


def fetch_down(parity, wd, w, sem):
    band = w.shape[1] // BANDS
    copies = []
    for k in range(BANDS):
        cols = pl.ds(pl.multiple_of((2 * k + parity) * band, band), band)
        copies.append(pltpu.make_async_copy(wd.at[:, cols], w.at[:, pl.ds(k * band, band)], sem.at[k]))
    for c in copies:
        c.start()
    return copies


def second_kernel(where, sib, acc, wg, wu, wd, h, give, w, wdown, sems, dsems):
    parity = 1 - where[0]
    copies = fetch_pairs(parity, wg, wu, w, sems)
    downs = fetch_down(parity, wd, wdown, dsems)
    near, far = unpack(sib)
    n = near.shape[0]
    wide = h.shape[1]
    for c in copies:
        c.wait()
    for x, at in ((near, slice(0, n)), (far, slice(n, acc.shape[0]))):
        both = acc[at, :] + dot(x, w[...])
        g, u = both[:, :wide], both[:, wide:]
        h[at, :] = (g / (1.0 + jnp.exp(-g)) * u).astype(BF)
    for c in downs:
        c.wait()
    pack(dot(h[:n, :], wdown[...]), dot(h[n:, :], wdown[...]), give)


def third_kernel(where, h, wd, keep, wdown, dsems):
    n = h.shape[0] // (NEAR + FAR) * NEAR
    for c in fetch_down(where[0], wd, wdown, dsems):
        c.wait()
    pack(dot(h[:n, :], wdown[...]), dot(h[n:, :], wdown[...]), keep)


def mix_kernel(mix, home, out):
    rows, band = out.shape[1:]
    parts = dot_t(mix[...], home[...])

    def at(i, j):
        return parts[i * rows : (i + 1) * rows, j * band : (j + 1) * band]

    out[0] = (at(0, 0) + at(2, 1)).astype(BF)
    out[1] = (at(0, 1) + at(2, 2)).astype(BF)
    out[2] = (at(0, 2) + at(3, 1)).astype(BF)
    out[3] = (at(1, 0) + at(3, 2)).astype(BF)


def body(tokens, expert_ids, router_probs, w_gate, w_up, w_down):
    rows, band = tokens.shape
    experts = lax.axis_size("expert")
    groups = lax.axis_size("dp")
    wide = w_gate.shape[2]
    seats = experts * (NEAR + FAR)
    core = lax.axis_index("dp") % 2
    where = core.astype(jnp.int32).reshape(1)
    lines = [list(range(c, groups, 2)) for c in range(2)]

    def swap(x):
        return lax.ppermute(x, "dp", [(i, i ^ 1) for i in range(groups)])

    def along(x):
        return lax.all_to_all(x, "dp", split_axis=0, concat_axis=0, tiled=True, axis_index_groups=lines)

    def trade(x):
        x = x.reshape(experts, ROWS, 3 * band)
        x = lax.all_to_all(x, "expert", split_axis=0, concat_axis=0, tiled=True)
        return x.reshape(experts * ROWS, 3 * band)

    toks = along(jnp.broadcast_to(tokens[None], (BANDS, rows, band)))
    square = ((experts * ROWS, BANDS * rows), BF)
    packed = ((experts * ROWS, 3 * band), BF)
    pick, mix = call(pick_kernel, [square, square], "pick", [VM, VM])(expert_ids.T, router_probs.T)
    (wire,) = call(wire_kernel, [packed], "wire", [VM, VM])(pick, toks)
    own = trade(wire)
    wg, wu, wd = w_gate[0], w_up[0], w_down[0]
    sib = swap(own)
    half = BANDS * band
    part = 2 * seats * half * wide
    pairs = [pltpu.VMEM((half, 2 * wide), BF)]
    downs = [pltpu.VMEM((wide, half), BF)]
    many, few = [pltpu.SemaphoreType.DMA((2 * BANDS,))], [pltpu.SemaphoreType.DMA((BANDS,))]
    (acc,) = call(
        first_kernel,
        [((seats, 2 * wide), F32)],
        "first",
        [SM, VM, ANY, ANY],
        limit=24 << 20,
        flops=2 * part,
        moved=6 << 20,
        scratch=pairs + many,
    )(where, own, wg, wu)
    h, give = call(
        second_kernel,
        [((seats, wide), BF), packed],
        "second",
        [SM, VM, VM, ANY, ANY, ANY],
        limit=24 << 20,
        flops=3 * part,
        moved=8 << 20,
        scratch=pairs + downs + many + few,
    )(where, sib, acc, wg, wu, wd)
    give = swap(give)
    (keep,) = call(
        third_kernel,
        [packed],
        "third",
        [SM, VM, ANY],
        limit=24 << 20,
        flops=part,
        moved=4 << 20,
        scratch=downs + few,
    )(where, h, wd)
    back = (keep.astype(F32) + give.astype(F32)).astype(BF)
    home = trade(back)
    (parts,) = call(mix_kernel, [((BANDS, rows, band), BF)], "mix", [VM, VM])(mix, home)
    parts = along(parts)
    return jnp.sum(parts.astype(F32), axis=0).astype(BF)


def solution(mesh):
    return jax.shard_map(
        body,
        mesh=mesh,
        in_specs=(
            P("expert", "dp"),
            P("expert", None),
            P("expert", None),
            P("expert", None, "dp"),
            P("expert", None, "dp"),
            P("expert", "dp", None),
        ),
        out_specs=P("expert", "dp"),
        check_vma=False,
    )
```

time: 395 us -> 147 us (0.37)
  the two profiles are of different devices: /device:TPU:133 before, /device:TPU:8 now
where the time goes in v2:
time: 147 us; the launch traced here: 146 us
  blocking collectives  111 us (76%)
  Pallas kernels  11.6 us (8%)
  starting transfers between devices  10.5 us (7%)
  waiting for transfers between devices  7.34 us (5%)
  local copies, waits for them, and re-layouts  5 us (3%)
    all_to_all x2, blocking collectives, trade(): x = lax.all_to_all(x, 'expert', split_axis=0, concat_axis=0, tiled=True)  98.8 us
    all_to_all x1, blocking collectives, along(): lax.all_to_all(x, 'dp', split_axis=0, concat_axis=0, tiled=True, axis_ind...  12.1 us
    all_to_all x1, starting transfers between devices, along(): lax.all_to_all(x, 'dp', split_axis=0, concat_axis=0, tiled=True, axis_ind...  6.19 us
    all_to_all x1, waiting for transfers between devices, along(): lax.all_to_all(x, 'dp', split_axis=0, concat_axis=0, tiled=True, axis_ind...  5.75 us
    pallas_call x1, Pallas kernels, body(): call(second_kernel, [((seats, wide), BF), packed], 'second', [SM, VM, VM,...  5.39 us
    ppermute x2, starting transfers between devices, swap(): return lax.ppermute(x, 'dp', [(i, i ^ 1) for i in range(groups)])  4.32 us
    unnamed x14, local copies, waits for them, and re-layouts  3.59 us
  transfers between devices with their start and end apart: 3, of which 2 were waited for; matrix products, arithmetic and copies ran while one was open for 0% of the time, Pallas kernels for 3%

profile of v2, /device:TPU:8, one launch (start us, length us, event | category | flops | bytes accessed | tf_op | source)
XLA Modules:
  0.0 146.5 jit_solution(16477348962966339310)
XLA Ops:
  0.0 1.4 broadcast_in_dim.2
  1.4 6.2 %all-to-all-start = ((bf16[4,64,256]{2,1,0:T(8,128)(2,1)}), bf16[4,64,256]{2,1,0:T(8,128)(2,1)S(1)}, u32[]{:S(2)}, u32[]{:S(2)}) async-start(bf16[4,64,256]{2,1,0:T(8,128)(2,1)} %broadcast_in_dim.2), calls=%async_computation | async-start | bytes 262144 | tf_op jit(solution)/shard_map/all_to_all | solution.py:222
  7.6 0.0 copy-start.5
  7.6 0.7 copy-done.5
  8.3 0.0 copy-start.6
  8.3 0.7 copy-done.6
  9.0 0.9 pick.1
  9.9 0.0 copy-start.3
  9.9 0.8 copy-done.3
  10.7 5.8 %all-to-all-done.toks = bf16[4,64,256]{2,1,0:T(8,128)(2,1)S(1)} async-done(((bf16[4,64,256]{2,1,0:T(8,128)(2,1)}), bf16[4,64,256]{2,1,0:T(8,128)(2,1)S(1)}, u32[]{:S(2)}, u32[]{:S(2)}) %all-to-all-start) | async-done | bytes 131104 | tf_op jit(solution)/shard_map/all_to_all | solution.py:222
  16.4 0.8 wire.1
  17.2 0.0 copy-start
  17.3 52.1 %all_to_all.20 = bf16[64,16,768]{2,1,0:T(8,128)(2,1)S(1)} all-to-all(bf16[64,16,768]{2,1,0:T(8,128)(2,1)S(1)} %bitcast.13), channel_id=1, replica_groups=mesh['dp'=8,'expert'=64] {'expert'}, dimensions={0} | all-to-all | bytes 3145728 | tf_op jit(solution)/shard_map/all_to_all | solution.py:226
  69.4 1.9 %collective-permute-start = (bf16[1024,768]{1,0:T(8,128)(2,1)S(1)}, bf16[1024,768]{1,0:T(8,128)(2,1)}, u32[]{:S(2)}, u32[]{:S(2)}) collective-permute-start(bf16[1024,768]{1,0:T(8,128)(2,1)S(1)} %bitcast.10), channel_id=1, source_target_pairs={{0,64},{64,0},{128,192},{192,128},{256,320},{320,256},{384,448},{4... | collective-permute-start | bytes 4718600 | tf_op jit(solution)/shard_map/ppermute | solution.py:219
  71.3 0.0 copy-done
  71.3 0.0 copy-start.1
  71.3 1.4 copy-done.1
  72.7 0.0 copy-start.2
  72.7 2.5 %first.1.acc = f32[768,768]{1,0:T(8,128)S(1)} custom-call(s32[1]{0:T(128)} %bitcast.2.where, bf16[1024,768]{1,0:T(8,128)(2,1)S(1)} %bitcast.11, bf16[2048,384]{1,0:T(8,128)(2,1)S(1)} %bitcast.14, bf16[2048,384]{1,0:T(8,128)(2,1)S(1)} %bitcast.16), custom_call_target="tpu_custom_call" | custom-call | flops 1207959552 | bytes 6291456 | tf_op jit(solution)/shard_map/first/pallas_call | solution.py:242
  75.2 0.0 collective-permute-done.sib
  75.2 0.0 copy-done.2
  75.2 5.4 %second.1 = (bf16[768,384]{1,0:T(8,128)(2,1)S(1)}, bf16[1024,768]{1,0:T(8,128)(2,1)S(1)}) custom-call(s32[1]{0:T(128)} %bitcast.2.where, bf16[1024,768]{1,0:T(8,128)(2,1)} %collective-permute-done.sib, f32[768,768]{1,0:T(8,128)S(1)} %first.1.acc, bf16[2048,384]{1,0:T(8,128)(2,1)S(1)} %bitcast.15, bf16[2048,384]{1,0:T(8,128)(2,1)S(1)} %bitcast.17, ...), custom_call_target="tpu_custom_call" | custom-call | flops 1811939328 | bytes 8388608 | tf_op jit(solution)/shard_map/second/pallas_call | solution.py:252
  80.6 2.4 %collective-permute-start.1 = (bf16[1024,768]{1,0:T(8,128)(2,1)S(1)}, bf16[1024,768]{1,0:T(8,128)(2,1)S(1)}, u32[]{:S(2)}, u32[]{:S(2)}) collective-permute-start(bf16[1024,768]{1,0:T(8,128)(2,1)S(1)} %get-tuple-element.12), channel_id=1, source_target_pairs={{0,64},{64,0},{128,192},{192,128},{256,320},{320,256},{384,448},{4... | collective-permute-start | bytes 4718600 | tf_op jit(solution)/shard_map/ppermute | solution.py:219
  83.1 1.4 third.1
  84.5 1.6 %collective-permute-done.1 = bf16[1024,768]{1,0:T(8,128)(2,1)S(1)} collective-permute-done((bf16[1024,768]{1,0:T(8,128)(2,1)S(1)}, bf16[1024,768]{1,0:T(8,128)(2,1)S(1)}, u32[]{:S(2)}, u32[]{:S(2)}) %collective-permute-start.1) | collective-permute-done | bytes 1572896 | tf_op jit(solution)/shard_map/ppermute | solution.py:219
  86.1 0.4 add_convert_fusion
  86.5 0.0 copy-start.4
  86.5 46.6 %all_to_all.21 = bf16[64,16,768]{2,1,0:T(8,128)(2,1)S(1)} all-to-all(bf16[64,16,768]{2,1,0:T(8,128)(2,1)S(1)} %bitcast.22), channel_id=1, replica_groups=mesh['dp'=8,'expert'=64] {'expert'}, dimensions={0} | all-to-all | bytes 3145728 | tf_op jit(solution)/shard_map/all_to_all | solution.py:226
  133.2 0.0 copy-done.4
  133.2 0.6 mix.1
  133.8 12.1 %all_to_all.22 = bf16[4,64,256]{2,1,0:T(8,128)(2,1)S(1)} all-to-all(bf16[4,64,256]{2,1,0:T(8,128)(2,1)S(1)} %mix.1), channel_id=1, replica_groups={{0,128,256,384},{64,192,320,448},{1,129,257,385},{65,193,321,449},{2,13..., dimensions={0} | all-to-all | bytes 262144 | tf_op jit(solution)/shard_map/all_to_all | solution.py:222
  145.8 0.6 reduce_sum.12
Async XLA Ops:
  1.4 15.0 %all-to-all-start = ((bf16[4,64,256]{2,1,0:T(8,128)(2,1)}), bf16[4,64,256]{2,1,0:T(8,128)(2,1)S(1)}, u32[]{:S(2)}, u32[]{:S(2)}) async-start(bf16[4,64,256]{2,1,0:T(8,128)(2,1)} %broadcast_in_dim.2), calls=%async_computation | async-start | bytes 262144 | tf_op jit(solution)/shard_map/all_to_all | solution.py:222
  7.6 0.7 copy-start.5
  8.3 0.7 copy-start.6
  9.9 0.8 copy-start.3
  17.2 54.1 %copy-start = (bf16[1,2048,384]{2,1,0:T(8,128)(2,1)S(1)}, bf16[1,2048,384]{2,1,0:T(8,128)(2,1)}, u32[]{:S(2)}) copy-start(bf16[1,2048,384]{2,1,0:T(8,128)(2,1)} %param.9) | copy-start | bytes 4718596
  69.4 5.8 %collective-permute-start = (bf16[1024,768]{1,0:T(8,128)(2,1)S(1)}, bf16[1024,768]{1,0:T(8,128)(2,1)}, u32[]{:S(2)}, u32[]{:S(2)}) collective-permute-start(bf16[1024,768]{1,0:T(8,128)(2,1)S(1)} %bitcast.10), channel_id=1, source_target_pairs={{0,64},{64,0},{128,192},{192,128},{256,320},{320,256},{384,448},{4... | collective-permute-start | bytes 4718600 | tf_op jit(solution)/shard_map/ppermute | solution.py:219
  71.3 1.4 copy-start.1
  72.7 2.5 %copy-start.2 = (bf16[1,384,2048]{2,1,0:T(8,128)(2,1)S(1)}, bf16[1,384,2048]{2,1,0:T(8,128)(2,1)}, u32[]{:S(2)}) copy-start(bf16[1,384,2048]{2,1,0:T(8,128)(2,1)} %param.11) | copy-start | bytes 4718596
  80.6 5.4 %collective-permute-start.1 = (bf16[1024,768]{1,0:T(8,128)(2,1)S(1)}, bf16[1024,768]{1,0:T(8,128)(2,1)S(1)}, u32[]{:S(2)}, u32[]{:S(2)}) collective-permute-start(bf16[1024,768]{1,0:T(8,128)(2,1)S(1)} %get-tuple-element.12), channel_id=1, source_target_pairs={{0,64},{64,0},{128,192},{192,128},{256,320},{320,256},{384,448},{4... | collective-permute-start | bytes 4718600 | tf_op jit(solution)/shard_map/ppermute | solution.py:219
  86.5 46.7 %copy-start.4 = (bf16[1024,256]{1,0:T(8,128)(2,1)S(1)}, bf16[1024,256]{1,0:T(8,128)(2,1)}, u32[]{:S(2)}) copy-start(bf16[1024,256]{1,0:T(8,128)(2,1)} %copy-done.3) | copy-start | bytes 1572868

commit v3 on v0

v3 whole, which is shorter than its diff:
```python
import jax
import jax.numpy as jnp
from jax import lax
from jax.experimental import pallas as pl
from jax.experimental.pallas import tpu as pltpu
from jax.sharding import Mesh
from jax.sharding import PartitionSpec as P

BF = jnp.bfloat16
F32 = jnp.float32
NEAR = 8
FAR = 4
BANDS = 4
LIMIT = 32 << 20
FIRST_LIMIT = 47 << 20
DP = {"yh": 4, "core": 2}
EXPERT = {"z": 8, "yl": 2, "x": 4}
TRADE = ("yl", "z", "x")
VM = pl.BlockSpec(memory_space=pltpu.VMEM)
SM = pl.BlockSpec(memory_space=pltpu.SMEM)
ANY = pl.BlockSpec(memory_space=pl.ANY)


def call(kernel, outs, name, specs, limit=8 << 20, flops=0, moved=0, scratch=()):
    return pl.pallas_call(
        kernel,
        out_shape=[jax.ShapeDtypeStruct(s, t) for s, t in outs],
        in_specs=specs,
        out_specs=[VM] * len(outs),
        scratch_shapes=list(scratch),
        compiler_params=pltpu.CompilerParams(vmem_limit_bytes=limit),
        cost_estimate=pl.CostEstimate(flops=flops, bytes_accessed=moved, transcendentals=0),
        name=name,
    )


def dot(a, b):
    return jnp.dot(a, b, preferred_element_type=F32)


def dot_t(a, b):
    return lax.dot_general(a, b, (((0,), (0,)), ((), ())), preferred_element_type=F32)


def pick_kernel(ids, probs, pick, mix):
    fanout, rows = ids.shape
    experts = pick.shape[0] // NEAR
    at = lax.broadcasted_iota(jnp.int32, (experts, rows), 0)
    place = {}
    for axis in TRADE[::-1]:
        place[axis] = at % EXPERT[axis]
        at = at // EXPERT[axis]
    label = jnp.zeros((experts, rows), jnp.int32)
    for axis, size in EXPERT.items():
        label = label * size + place[axis]
    p = probs[...]
    shares = (p / jnp.sum(p, axis=0, keepdims=True)).astype(BF).astype(F32)
    named = jnp.zeros((experts, rows), F32)
    share = jnp.zeros((experts, rows), F32)
    for k in range(fanout):
        hit = ids[k : k + 1, :] == label
        named = jnp.where(hit, 1.0, named)
        share = jnp.where(hit, shares[k : k + 1, :], share)
    i0 = lax.broadcasted_iota(jnp.int32, (rows, rows), 0)
    i1 = lax.broadcasted_iota(jnp.int32, (rows, rows), 1)
    before = dot(named.astype(BF), (i0 < i1).astype(F32).astype(BF))
    seat = jnp.where(named > 0.5, before, -1.0).astype(jnp.int32)

    def spread(values):
        return jnp.broadcast_to(values[:, None, :], (experts, NEAR, rows)).reshape(-1, rows)

    place = lax.broadcasted_iota(jnp.int32, (experts * NEAR, rows), 0) % NEAR
    seats = spread(seat)
    weights = spread(share)
    far = seats == place % FAR + NEAR
    for i, hit in enumerate((seats == place, far & (place < FAR), far & (place >= FAR))):
        pick[:, i * rows : (i + 1) * rows] = hit.astype(F32).astype(BF)
        mix[:, i * rows : (i + 1) * rows] = jnp.where(hit, weights, 0.0).astype(BF)


def repeat_kernel(tokens, out):
    for k in range(BANDS):
        out[k] = tokens[...]


def wire_kernel(pick, toks, wire):
    rows, band = toks.shape[1:]
    for k in range(BANDS):
        wire[:, k * band : (k + 1) * band] = dot(pick[:, :rows], toks[k]).astype(BF)
    for j in range(2):
        both = jnp.concatenate([toks[j], toks[2 + j]], axis=0)
        at = (BANDS + j) * band
        wire[:, at : at + band] = dot(pick[:, rows:], both).astype(BF)


def order(count):
    half = count // 2
    i = lax.broadcasted_iota(jnp.int32, (count, count), 0)
    j = lax.broadcasted_iota(jnp.int32, (count, count), 1)
    r = i % half
    return (j == (r // FAR) * (2 * FAR) + (i // half) * FAR + r % FAR).astype(F32).astype(BF)


def far_rows(wire):
    count = wire.shape[0]
    x = dot(order(count), wire[:, wire.shape[1] // 3 * 2 :]).astype(BF)
    return jnp.concatenate([x[: count // 2], x[count // 2 :]], axis=1)


def fill(h, down, wire):
    count, width = wire.shape
    half = width // 3 * 2
    band = half // BANDS
    far = []
    for k in range(BANDS):
        cols = slice(k * band, (k + 1) * band)
        wire[:, cols] = dot(h[:count, :], down[:, cols]).astype(BF)
        far.append(dot(h[count:, :], down[:, cols]).astype(BF))
    top = jnp.concatenate(far[:2], axis=1)
    low = jnp.concatenate(far[2:], axis=1)
    wire[:, half:] = dot_t(order(count), jnp.concatenate([top, low], axis=0)).astype(BF)


def first_kernel(where, own, wg, wu, wd, acc_near, acc_far, up_sib, down_sib, down_own, up_own, sems):
    band = up_own.shape[0] // BANDS
    wide = wg.shape[1]
    copies = []

    def copy(src, dst):
        copies.append(pltpu.make_async_copy(src, dst, sems.at[len(copies)]))
        copies[-1].start()

    sides = ((up_own, down_own, where[0]), (up_sib, down_sib, 1 - where[0]))
    for up, _, parity in sides:
        for k in range(BANDS):
            at = pl.ds(pl.multiple_of((2 * k + parity) * band, band), band)
            to = pl.ds(k * band, band)
            copy(wg.at[at, :], up.at[to, pl.ds(0, wide)])
            copy(wu.at[at, :], up.at[to, pl.ds(wide, wide)])
    for _, down, parity in sides[::-1]:
        for k in range(BANDS):
            at = pl.ds(pl.multiple_of((2 * k + parity) * band, band), band)
            copy(wd.at[:, at], down.at[:, pl.ds(k * band, band)])
    far = far_rows(own)
    for c in copies[: 2 * BANDS]:
        c.wait()
    acc_near[...] = dot(own[:, : BANDS * band], up_own[...])
    acc_far[...] = dot(far, up_own[...])
    for c in copies[2 * BANDS :]:
        c.wait()


def second_kernel(sib, acc_near, acc_far, up, down, h, give):
    count = sib.shape[0]
    wide = h.shape[1]
    parts = (
        (acc_near, lambda: sib[:, : sib.shape[1] // 3 * 2], slice(0, count)),
        (acc_far, lambda: far_rows(sib), slice(count, h.shape[0])),
    )
    for acc, rows, at in parts:
        both = acc[...] + dot(rows(), up[...])
        g, u = both[:, :wide], both[:, wide:]
        h[at, :] = (g / (1.0 + jnp.exp(-g)) * u).astype(BF)
    fill(h, down, give)


def third_kernel(h, down, keep):
    fill(h, down, keep)


def mix_kernel(mix, home, out):
    rows, band = out.shape[1:]
    near = dot_t(mix[:, :rows], home[:, : BANDS * band])
    far = dot_t(mix[:, rows:], home[:, BANDS * band :])
    for k in range(BANDS):
        half, col = k // 2, k % 2
        a = near[:, k * band : (k + 1) * band]
        b = far[half * rows : (half + 1) * rows, col * band : (col + 1) * band]
        out[k] = (a + b).astype(BF)


def body(tokens, expert_ids, router_probs, w_gate, w_up, w_down):
    rows, band = tokens.shape
    experts = lax.axis_size(TRADE)
    wide = w_gate.shape[2]
    half = BANDS * band
    lines = experts * NEAR
    where = lax.axis_index("core").astype(jnp.int32).reshape(1)

    def swap(x):
        return lax.ppermute(x, "core", [(0, 1), (1, 0)])

    def along(x):
        return lax.all_to_all(x, "yh", split_axis=0, concat_axis=0, tiled=True)

    def trade(x):
        y = x.reshape(experts, NEAR, x.shape[1])
        y = lax.all_to_all(y, TRADE, split_axis=0, concat_axis=0, tiled=True)
        return y.reshape(x.shape)

    bands = ((BANDS, rows, band), BF)
    lists = ((lines, 3 * rows), BF)
    packed = ((lines, half // 2 * 3), BF)
    (toks,) = call(repeat_kernel, [bands], "repeat", [VM], limit=58 << 20)(tokens)
    toks = along(toks)
    pick, mix = call(pick_kernel, [lists, lists], "pick", [VM] * 2)(expert_ids.T, router_probs.T)
    (wire,) = call(wire_kernel, [packed], "wire", [VM] * 2)(pick, toks)
    own = trade(wire)
    sib = swap(own)
    part = 2 * experts * (NEAR + FAR) * half * wide
    sums = [((experts * n, 2 * wide), F32) for n in (NEAR, FAR)]
    ups, downs = ((half, 2 * wide), BF), ((wide, half), BF)
    acc_near, acc_far, up_sib, down_sib, down_own = call(
        first_kernel,
        sums + [ups, downs, downs],
        "first",
        [SM, VM, ANY, ANY, ANY],
        limit=FIRST_LIMIT,
        flops=2 * part,
        moved=6 << 20,
        scratch=[pltpu.VMEM(*ups), pltpu.SemaphoreType.DMA((6 * BANDS,))],
    )(where, own, w_gate[0], w_up[0], w_down[0])
    h, give = call(
        second_kernel,
        [((experts * (NEAR + FAR), wide), BF), packed],
        "second",
        [VM] * 5,
        limit=LIMIT,
        flops=3 * part,
        moved=8 << 20,
    )(sib, acc_near, acc_far, up_sib, down_sib)
    give = swap(give)
    (keep,) = call(third_kernel, [packed], "third", [VM] * 2, limit=LIMIT, flops=part, moved=4 << 20)(
        h, down_own
    )
    home = trade((keep.astype(F32) + give.astype(F32)).astype(BF))
    (parts,) = call(mix_kernel, [bands], "mix", [VM] * 2)(mix, home)
    return jnp.sum(along(parts).astype(F32), axis=0).astype(BF)


def solution(mesh):
    sizes = DP | EXPERT
    mesh = Mesh(mesh.devices.reshape(*sizes.values()), tuple(sizes))
    dp, expert = tuple(DP), tuple(EXPERT)
    return jax.shard_map(
        body,
        mesh=mesh,
        in_specs=(
            P(expert, dp),
            P(expert, None),
            P(expert, None),
            P(expert, None, dp),
            P(expert, None, dp),
            P(expert, dp, None),
        ),
        out_specs=P(expert, dp),
        check_vma=False,
    )
```

time: 395 us -> 142 us (0.36)
  the two profiles are of different devices: /device:TPU:133 before, /device:TPU:8 now
where the time goes in v3:
time: 142 us; the launch traced here: 141 us
  blocking collectives  109 us (77%)
  starting transfers between devices  10.4 us (7%)
  Pallas kernels  10.1 us (7%)
  waiting for transfers between devices  8.91 us (6%)
    all_to_all x2, blocking collectives, trade(): y = lax.all_to_all(y, TRADE, split_axis=0, concat_axis=0, tiled=True)  97.4 us
    all_to_all x1, blocking collectives, along(): return lax.all_to_all(x, 'yh', split_axis=0, concat_axis=0, tiled=True)  11.8 us
    all_to_all x1, waiting for transfers between devices, along(): return lax.all_to_all(x, 'yh', split_axis=0, concat_axis=0, tiled=True)  7.03 us
    all_to_all x1, starting transfers between devices, along(): return lax.all_to_all(x, 'yh', split_axis=0, concat_axis=0, tiled=True)  6.19 us
    ppermute x2, starting transfers between devices, swap(): return lax.ppermute(x, 'core', [(0, 1), (1, 0)])  4.2 us
    pallas_call x1, Pallas kernels, body(): call(first_kernel, sums + [ups, downs, downs], 'first', [SM, VM, ANY, ANY...  3.24 us
    pallas_call x1, Pallas kernels, body(): call(second_kernel, [((experts * (NEAR + FAR), wide), BF), packed], 'seco...  2.84 us
  transfers between devices with their start and end apart: 3, of which 3 were waited for; matrix products, arithmetic and copies ran while one was open for 0% of the time, Pallas kernels for 3%

profile of v3, /device:TPU:8, one launch (start us, length us, event | category | flops | bytes accessed | tf_op | source)
XLA Modules:
  0.0 141.1 jit_solution(14322864888780844446)
XLA Ops:
  0.0 1.4 %repeat.1 = bf16[4,64,256]{2,1,0:T(8,128)(2,1)} custom-call(bf16[64,256]{1,0:T(8,128)(2,1)} %tokens.1), custom_call_target="tpu_custom_call" | custom-call | tf_op jit(solution)/shard_map/repeat/pallas_call | solution.py:204
  1.4 6.2 %all-to-all-start = ((bf16[4,64,256]{2,1,0:T(8,128)(2,1)}), bf16[4,64,256]{2,1,0:T(8,128)(2,1)S(1)}, u32[]{:S(2)}, u32[]{:S(2)}) async-start(bf16[4,64,256]{2,1,0:T(8,128)(2,1)} %repeat.1), calls=%async_computation | async-start | bytes 262144 | tf_op jit(solution)/shard_map/all_to_all | solution.py:194
  7.6 0.0 copy-start
  7.6 0.7 copy-done
  8.3 0.0 copy-start.1
  8.3 0.7 copy-done.1
  9.0 0.4 pick.1
  9.4 7.0 %all-to-all-done.toks = bf16[4,64,256]{2,1,0:T(8,128)(2,1)S(1)} async-done(((bf16[4,64,256]{2,1,0:T(8,128)(2,1)}), bf16[4,64,256]{2,1,0:T(8,128)(2,1)S(1)}, u32[]{:S(2)}, u32[]{:S(2)}) %all-to-all-start) | async-done | bytes 131104 | tf_op jit(solution)/shard_map/all_to_all | solution.py:194
  16.4 0.5 wire.1
  17.0 50.8 %all_to_all.20 = bf16[64,8,1536]{2,1,0:T(8,128)(2,1)S(1)} all-to-all(bf16[64,8,1536]{2,1,0:T(8,128)(2,1)S(1)} %bitcast.14), channel_id=1, replica_groups=mesh['yh'=4,'core'=2,'z'=8,'yl'=2,'x'=4] {'yl','z','x'}, dimensions={0} | all-to-all | bytes 3145728 | tf_op jit(solution)/shard_map/all_to_all | solution.py:198
  67.8 1.9 %collective-permute-start = (bf16[512,1536]{1,0:T(8,128)(2,1)S(1)}, bf16[512,1536]{1,0:T(8,128)(2,1)S(1)}, u32[]{:S(2)}, u32[]{:S(2)}) collective-permute-start(bf16[512,1536]{1,0:T(8,128)(2,1)S(1)} %bitcast.11), channel_id=1, source_target_pairs={{0,64},{64,0},{1,65},{65,1},{2,66},{66,2},{3,67},{67,3},{4,68},{68... | collective-permute-start | bytes 4718600 | tf_op jit(solution)/shard_map/ppermute | solution.py:191
  69.7 3.2 %first.1 = (f32[512,768]{1,0:T(8,128)S(1)}, f32[256,768]{1,0:T(8,128)S(1)}, bf16[1024,768]{1,0:T(8,128)(2,1)S(1)}, bf16[384,1024]{1,0:T(8,128)(2,1)S(1)}, bf16[384,1024]{1,0:T(8,128)(2,1)S(1)}) custom-call(s32[1]{0:T(128)} %bitcast.4.where, bf16[512,1536]{1,0:T(8,128)(2,1)S(1)} %bitcast.12, bf16[2048,384]{1,0:T(8,128)(2,1)} %bitcast.17, ...), custom_call_target="tpu_custom_call" | custom-call | flops 1207959552 | bytes 6291456 | tf_op jit(solution)/shard_map/first/pallas_call | solution.py:213
  73.0 0.1 collective-permute-done.sib
  73.1 2.8 %second.1 = (bf16[768,384]{1,0:T(8,128)(2,1)S(1)}, bf16[512,1536]{1,0:T(8,128)(2,1)S(1)}) custom-call(bf16[512,1536]{1,0:T(8,128)(2,1)S(1)} %collective-permute-done.sib, f32[512,768]{1,0:T(8,128)S(1)} %get-tuple-element.16.acc_near, f32[256,768]{1,0:T(8,128)S(1)} %get-tuple-element.17.acc_far, bf16[1024,768]{1,0:T(8,128)(2,1)S(1)} %get-tuple-element.18.up, ...), custom_call_target="tpu_custom_call" | custom-call | flops 1811939328 | bytes 8388608 | tf_op jit(solution)/shard_map/second/pallas_call | solution.py:223
  75.9 2.3 %collective-permute-start.1 = (bf16[512,1536]{1,0:T(8,128)(2,1)S(1)}, bf16[512,1536]{1,0:T(8,128)(2,1)S(1)}, u32[]{:S(2)}, u32[]{:S(2)}) collective-permute-start(bf16[512,1536]{1,0:T(8,128)(2,1)S(1)} %get-tuple-element.22), channel_id=1, source_target_pairs={{0,64},{64,0},{1,65},{65,1},{2,66},{66,2},{3,67},{67,3},{4,68},{68... | collective-permute-start | bytes 4718600 | tf_op jit(solution)/shard_map/ppermute | solution.py:191
  78.2 1.3 third.1
  79.5 1.8 %collective-permute-done.1 = bf16[512,1536]{1,0:T(8,128)(2,1)S(1)} collective-permute-done((bf16[512,1536]{1,0:T(8,128)(2,1)S(1)}, bf16[512,1536]{1,0:T(8,128)(2,1)S(1)}, u32[]{:S(2)}, u32[]{:S(2)}) %collective-permute-start.1) | collective-permute-done | bytes 1572896 | tf_op jit(solution)/shard_map/ppermute | solution.py:191
  81.3 0.4 fusion
  81.6 46.6 %all_to_all.21 = bf16[64,8,1536]{2,1,0:T(8,128)(2,1)S(1)} all-to-all(bf16[64,8,1536]{2,1,0:T(8,128)(2,1)S(1)} %fusion), channel_id=1, replica_groups=mesh['yh'=4,'core'=2,'z'=8,'yl'=2,'x'=4] {'yl','z','x'}, dimensions={0} | all-to-all | bytes 3145728 | tf_op jit(solution)/shard_map/all_to_all | solution.py:198
  128.2 0.4 mix.1
  128.6 11.8 %all_to_all.22 = bf16[4,64,256]{2,1,0:T(8,128)(2,1)S(1)} all-to-all(bf16[4,64,256]{2,1,0:T(8,128)(2,1)S(1)} %mix.1), channel_id=1, replica_groups=mesh['yh'=4,'core'=2,'z'=8,'yl'=2,'x'=4] {'yh'}, dimensions={0} | all-to-all | bytes 262144 | tf_op jit(solution)/shard_map/all_to_all | solution.py:194
  140.4 0.6 reduce_sum.12
Async XLA Ops:
  1.4 15.0 %all-to-all-start = ((bf16[4,64,256]{2,1,0:T(8,128)(2,1)}), bf16[4,64,256]{2,1,0:T(8,128)(2,1)S(1)}, u32[]{:S(2)}, u32[]{:S(2)}) async-start(bf16[4,64,256]{2,1,0:T(8,128)(2,1)} %repeat.1), calls=%async_computation | async-start | bytes 262144 | tf_op jit(solution)/shard_map/all_to_all | solution.py:194
  7.6 0.7 copy-start
  8.3 0.7 copy-start.1
  67.8 5.3 %collective-permute-start = (bf16[512,1536]{1,0:T(8,128)(2,1)S(1)}, bf16[512,1536]{1,0:T(8,128)(2,1)S(1)}, u32[]{:S(2)}, u32[]{:S(2)}) collective-permute-start(bf16[512,1536]{1,0:T(8,128)(2,1)S(1)} %bitcast.11), channel_id=1, source_target_pairs={{0,64},{64,0},{1,65},{65,1},{2,66},{66,2},{3,67},{67,3},{4,68},{68... | collective-permute-start | bytes 4718600 | tf_op jit(solution)/shard_map/ppermute | solution.py:191
  75.9 5.3 %collective-permute-start.1 = (bf16[512,1536]{1,0:T(8,128)(2,1)S(1)}, bf16[512,1536]{1,0:T(8,128)(2,1)S(1)}, u32[]{:S(2)}, u32[]{:S(2)}) collective-permute-start(bf16[512,1536]{1,0:T(8,128)(2,1)S(1)} %get-tuple-element.22), channel_id=1, source_target_pairs={{0,64},{64,0},{1,65},{65,1},{2,66},{66,2},{3,67},{67,3},{4,68},{68... | collective-permute-start | bytes 4718600 | tf_op jit(solution)/shard_map/ppermute | solution.py:191

commit v4 on v3

v4 whole, which is shorter than its diff:
```python
import jax
import jax.numpy as jnp
from jax import lax
from jax.experimental import pallas as pl
from jax.experimental.pallas import tpu as pltpu
from jax.sharding import Mesh
from jax.sharding import PartitionSpec as P

BF = jnp.bfloat16
F32 = jnp.float32
NEAR = 8
FAR = 4
SEATS = NEAR + FAR
LINE = 4
LONG = 40_000_000_000
SHORT = 2_000_000_000
PLUS_LIMIT = 50 << 20
LOAD_LIMIT = 49 << 20
REST_LIMIT = 50 << 20
LIMIT = 32 << 20
PICK_LIMIT = 58 << 20
DP = {"yh": 4, "core": 2}
EXPERT = {"z": 8, "yl": 2, "x": 4}
TRADE = ("yl", "z", "x")
VM = pl.BlockSpec(memory_space=pltpu.VMEM)
SM = pl.BlockSpec(memory_space=pltpu.SMEM)
ANY = pl.BlockSpec(memory_space=pl.ANY)
HBM = pl.BlockSpec(memory_space=pltpu.HBM)


def call(kernel, outs, name, specs, limit=LIMIT, flops=0, moved=0, scratch=(), out_specs=None):
    return pl.pallas_call(
        kernel,
        out_shape=[jax.ShapeDtypeStruct(s, t) for s, t in outs],
        in_specs=specs,
        out_specs=out_specs or [VM] * len(outs),
        scratch_shapes=list(scratch),
        compiler_params=pltpu.CompilerParams(vmem_limit_bytes=limit),
        cost_estimate=pl.CostEstimate(flops=flops, bytes_accessed=moved, transcendentals=0),
        name=name,
    )


def dot(a, b):
    return jnp.dot(a, b, preferred_element_type=F32)


def dot_t(a, b):
    return lax.dot_general(a, b, (((0,), (0,)), ((), ())), preferred_element_type=F32)


def fill(pick, tokens, wire):
    rows, band = tokens.shape
    t = tokens[...]
    wire[:, :band] = dot(pick[:, :rows], t).astype(BF)
    halves = jnp.concatenate([t[:, : band // 2], t[:, band // 2 :]], axis=0)
    wire[:, band:] = dot(pick[:, rows:], halves).astype(BF)


def pick_kernel(ids, probs, tokens, wire, pick, mix):
    fanout, rows = ids.shape
    experts = pick.shape[0] // NEAR
    at = lax.broadcasted_iota(jnp.int32, (experts, rows), 0)
    place = {}
    for axis in TRADE[::-1]:
        place[axis] = at % EXPERT[axis]
        at = at // EXPERT[axis]
    label = jnp.zeros((experts, rows), jnp.int32)
    for axis, size in EXPERT.items():
        label = label * size + place[axis]
    p = probs[...]
    shares = (p / jnp.sum(p, axis=0, keepdims=True)).astype(BF).astype(F32)
    named = jnp.zeros((experts, rows), F32)
    share = jnp.zeros((experts, rows), F32)
    for k in range(fanout):
        hit = ids[k : k + 1, :] == label
        named = jnp.where(hit, 1.0, named)
        share = jnp.where(hit, shares[k : k + 1, :], share)
    i0 = lax.broadcasted_iota(jnp.int32, (rows, rows), 0)
    i1 = lax.broadcasted_iota(jnp.int32, (rows, rows), 1)
    before = dot(named.astype(BF), (i0 < i1).astype(F32).astype(BF))
    seat = jnp.where(named > 0.5, before, -1.0).astype(jnp.int32)

    def spread(values):
        return jnp.broadcast_to(values[:, None, :], (experts, NEAR, rows)).reshape(-1, rows)

    place = lax.broadcasted_iota(jnp.int32, (experts * NEAR, rows), 0) % NEAR
    seats = spread(seat)
    weights = spread(share)
    far = seats == place % FAR + NEAR
    for i, hit in enumerate((seats == place, far & (place < FAR), far & (place >= FAR))):
        pick[:, i * rows : (i + 1) * rows] = hit.astype(F32).astype(BF)
        mix[:, i * rows : (i + 1) * rows] = jnp.where(hit, weights, 0.0).astype(BF)
    fill(pick, tokens, wire)


def order(count):
    half = count // 2
    i = lax.broadcasted_iota(jnp.int32, (count, count), 0)
    j = lax.broadcasted_iota(jnp.int32, (count, count), 1)
    r = i % half
    return (j == (r // FAR) * (2 * FAR) + (i // half) * FAR + r % FAR).astype(F32).astype(BF)


def spread_far(far, wide):
    half = far.shape[0] // 2
    parts = []
    for i in range(far.shape[1] // wide):
        cols = slice(i * wide, (i + 1) * wide)
        parts += [far[:half, cols], far[half:, cols]]
    return jnp.concatenate(parts, axis=1)


def unpack(wires):
    count, width = wires[0].shape
    band = width // 3 * 2
    near = jnp.concatenate([w[:, :band] for w in wires], axis=1)
    far = jnp.concatenate([w[:, band:] for w in wires], axis=1)
    far = dot(order(count), far).astype(BF)
    return near, spread_far(far, band // 2)


def pack(near, far, down, wires):
    count, width = wires[0].shape
    band = width // 3 * 2
    wide = band // 2
    top, low = [], []
    for i, wire in enumerate(wires):
        cols = slice(i * band, (i + 1) * band)
        wire[:, :band] = dot(near, down[:, cols]).astype(BF)
        part = dot(far, down[:, cols]).astype(BF)
        top.append(part[:, :wide])
        low.append(part[:, wide:])
    both = jnp.concatenate([jnp.concatenate(top, axis=1), jnp.concatenate(low, axis=1)], axis=0)
    both = dot_t(order(count), both).astype(BF)
    for i, wire in enumerate(wires):
        wire[:, band:] = both[:, i * wide : (i + 1) * wide]


def band_at(k, parity, band):
    return pl.ds(pl.multiple_of((2 * (k % LINE) + parity) * band, band), band)


class Fetch:
    def __init__(self, sems):
        self.sems, self.copies = sems, []

    def __call__(self, src, dst):
        self.copies.append(pltpu.make_async_copy(src, dst, self.sems.at[len(self.copies)]))
        self.copies[-1].start()

    def up(self, wg, wu, dst, slot, rows):
        wide, band = wg.shape[1], rows.size
        to = pl.ds(slot * band, band)
        self(wg.at[rows, :], dst.at[to, pl.ds(0, wide)])
        self(wu.at[rows, :], dst.at[to, pl.ds(wide, wide)])

    def wait(self, first=0, last=None):
        for c in self.copies[first:last]:
            c.wait()


def place():
    return lax.axis_index("yh"), lax.axis_index("core")


def plus_kernel(wg, wu, *refs):
    wires, (out_near, out_far, up, x, y, near_sum, far_sum, sems) = refs[:6], refs[6:]
    yh, core = place()
    count, width = wires[0].shape
    band = up.shape[0] // 6
    wide = band // 2
    fetch = Fetch(sems)
    for i, wire in enumerate(wires):
        fetch(wire.at[:, pl.ds(band, wide)], y.at[:, pl.ds(i * wide, wide)])
    for i, wire in enumerate(wires):
        fetch(wire.at[:, pl.ds(0, band)], x.at[:, pl.ds(i * band, band)])
    for slot, (k, parity) in enumerate((k, p) for k in (0, 1, 3) for p in (core, 1 - core)):
        fetch.up(wg, wu, up, slot, band_at(yh + LINE - k, parity, band))
    seq = order(count)
    fetch.wait(0, 6)
    far = spread_far(dot(seq, y[...]).astype(BF), wide)
    fetch.wait(6)
    near_sum[...] = dot(x[...], up[...])
    back = Fetch(sems)
    back(near_sum, out_near)
    far_sum[...] = dot(far, up[...])
    back(far_sum, out_far)
    back.wait()


def load_kernel(wg, wu, wd, acc_near, acc_far, out_top, out_low, out_far, up, give13, sems):
    yh, core = place()
    band = up.shape[0] // 2
    fetch = Fetch(sems)
    half = out_top.shape[0]
    fetch(acc_near.at[pl.ds(0, half), :], out_top)
    fetch(acc_near.at[pl.ds(half, half), :], out_low)
    fetch(acc_far, out_far)
    fetch.up(wg, wu, up, 0, band_at(yh + 2, core, band))
    fetch.up(wg, wu, up, 1, band_at(yh + 2, 1 - core, band))
    for slot, k in enumerate((1, 3)):
        fetch(wd.at[:, band_at(yh + k, 1 - core, band)], give13.at[:, pl.ds(slot * band, band)])
    fetch.wait()


def halves(ref):
    rows = ref.shape[0] // 2
    return [ref.at[pl.ds(i * rows, rows), :] for i in range(2)]


def hidden_kernel(own, sib, acc_top, acc_low, acc_far, up, down, h, give):
    near, far = unpack((own, sib))
    n = near.shape[0]
    wide = h.shape[1]
    half = n // 2
    parts = (
        (near[:half], acc_top, slice(0, half)),
        (near[half:], acc_low, slice(half, n)),
        (far, acc_far, slice(n, h.shape[0])),
    )
    for x, acc, at in parts:
        both = acc[...] + dot(x, up[...])
        g, u = both[:, :wide], both[:, wide:]
        h[at, :] = (g / (1.0 + jnp.exp(-g)) * u).astype(BF)
    pack(h[:n, :], h[n:, :], down, halves(give))


def rest_kernel(h, wd, give, keep1, keep3, keep2, keep0, give20, keep13, keep20, sems):
    yh, core = place()
    band = give20.shape[1] // 2
    fetch = Fetch(sems)
    for down, ks, parity in ((give20, (2, 0), 1 - core), (keep13, (1, 3), core), (keep20, (2, 0), core)):
        for slot, k in enumerate(ks):
            fetch(wd.at[:, band_at(yh + k, parity, band)], down.at[:, pl.ds(slot * band, band)])
    n = h.shape[0] // SEATS * NEAR
    near, far = h[:n, :], h[n:, :]
    fetch.wait()
    pack(near, far, keep13, (keep1, keep3))
    pack(near, far, give20, halves(give))
    pack(near, far, keep20, (keep2, keep0))


def pair_kernel(keep1, keep3, give, one, three):
    for a, b, out in zip((keep1, keep3), halves(give), (one, three)):
        out[...] = (a[...].astype(F32) + b[...].astype(F32)).astype(BF)


def sum_kernel(keep0, give, one, three, out):
    total = keep0[...].astype(F32) + halves(give)[1][...].astype(F32)
    out[...] = (total + one[...].astype(F32) + three[...].astype(F32)).astype(BF)


def two_sum_kernel(keep2, give, out):
    out[...] = (keep2[...].astype(F32) + halves(give)[0][...].astype(F32)).astype(BF)


def mixed(mix, home):
    rows = mix.shape[1] // 3
    band = home.shape[1] // 3 * 2
    total = dot_t(mix[:, :rows], home[:, :band])
    rest = dot_t(mix[:, rows:], home[:, band:])
    return total + jnp.concatenate([rest[:rows], rest[rows:]], axis=1)


def mix_kernel(mix, home, out):
    out[...] = mixed(mix, home).astype(BF)


def last_kernel(mix, home, other, out):
    out[...] = (mixed(mix, home) + other[...].astype(F32)).astype(BF)


def body(tokens, expert_ids, router_probs, w_gate, w_up, w_down):
    rows, band = tokens.shape
    experts = lax.axis_size(TRADE)
    wide = w_gate.shape[2]
    lines = experts * NEAR

    def swap(x):
        return lax.ppermute(x, "core", [(0, 1), (1, 0)])

    def shift(x, k):
        return lax.ppermute(x, "yh", [(i, (i + k) % LINE) for i in range(LINE)])

    def trade(x):
        y = x.reshape(experts, NEAR, x.shape[1])
        y = lax.all_to_all(y, TRADE, split_axis=0, concat_axis=0, tiled=True)
        return y.reshape(x.shape)

    tie = lax.optimization_barrier
    wg, wu, wd = w_gate[0], w_up[0], w_down[0]
    width = band // 2 * 3
    wire, two = ((lines, width), BF), ((2 * lines, width), BF)
    sums = [((experts * n, 2 * wide), F32) for n in (NEAR, FAR)]
    lists = ((lines, 3 * rows), BF)
    work = 2 * experts * SEATS * band * wide
    sems = lambda n: pltpu.SemaphoreType.DMA((n,))
    other = shift(tokens, 2)
    wire0, pick, mix = call(pick_kernel, [wire, lists, lists], "pick", [VM] * 3, limit=PICK_LIMIT)(
        expert_ids.T, router_probs.T, tokens
    )
    got0 = trade(wire0)
    (wire2,) = call(fill, [wire], "wire", [VM] * 2)(pick, other)
    got0, wire2 = tie((got0, wire2))
    got1, got3 = shift(got0, 1), shift(got0, 3)
    got2 = trade(wire2)
    sib0, sib1, sib3 = swap(got0), swap(got1), swap(got3)
    sums0 = call(
        plus_kernel,
        sums,
        "plus",
        [ANY] * 8,
        limit=PLUS_LIMIT,
        flops=SHORT,
        scratch=[
            pltpu.VMEM((6 * band, 2 * wide), BF),
            pltpu.VMEM((lines, 6 * band), BF),
            pltpu.VMEM((lines, 3 * band), BF),
        ]
        + [pltpu.VMEM(*x) for x in sums]
        + [sems(24)],
        out_specs=[HBM] * 2,
    )(wg, wu, got0, sib0, got1, sib1, got3, sib3)
    got2, sums0 = tie((got2, sums0))
    sib2 = swap(got2)
    pair = ((wide, 2 * band), BF)
    top, low, far, up2, give13 = call(
        load_kernel,
        [((experts * FAR, 2 * wide), F32)] * 3 + [((2 * band, 2 * wide), BF), pair],
        "load",
        [ANY, ANY, ANY, HBM, HBM],
        limit=LOAD_LIMIT,
        scratch=[sems(9)],
    )(wg, wu, wd, *sums0)
    h, give_a = call(
        hidden_kernel, [((experts * SEATS, wide), BF), two], "hidden", [VM] * 7, flops=6 * work
    )(got2, sib2, top, low, far, up2, give13)
    give_a = swap(give_a)
    give_b, keep1, keep3, keep2, keep0 = call(
        rest_kernel,
        [two] + [wire] * 4,
        "rest",
        [VM, ANY],
        limit=REST_LIMIT,
        flops=6 * work,
        scratch=[pltpu.VMEM(*pair)] * 3 + [sems(6)],
    )(h, wd)
    one, three = call(pair_kernel, [wire] * 2, "pair", [VM] * 3)(keep1, keep3, give_a)
    one, three, give_b = tie((one, three, give_b))
    one, three = shift(one, 1), shift(three, 3)
    give_b = swap(give_b)
    (back2,) = call(two_sum_kernel, [wire], "two_sum", [VM] * 2)(keep2, give_b)
    home2 = trade(back2)
    (back0,) = call(sum_kernel, [wire], "sum", [VM] * 4, flops=LONG)(keep0, give_b, one, three)
    home0 = trade(back0)
    (part,) = call(mix_kernel, [((rows, band), BF)], "mix", [VM] * 2)(mix, home2)
    (out,) = call(last_kernel, [((rows, band), BF)], "last", [VM] * 3)(mix, home0, shift(part, 2))
    return out


def solution(mesh):
    sizes = DP | EXPERT
    mesh = Mesh(mesh.devices.reshape(*sizes.values()), tuple(sizes))
    dp, expert = tuple(DP), tuple(EXPERT)
    return jax.shard_map(
        body,
        mesh=mesh,
        in_specs=(
            P(expert, dp),
            P(expert, None),
            P(expert, None),
            P(expert, None, dp),
            P(expert, None, dp),
            P(expert, dp, None),
        ),
        out_specs=P(expert, dp),
        check_vma=False,
    )
```

time: 142 us -> 136 us (0.958)
  blocking collectives: 109 us -> 0 us
  starting transfers between devices: 10.4 us -> 81.5 us
  waiting for transfers between devices: 8.91 us -> 33.9 us
  Pallas kernels: 10.1 us -> 18.9 us
    all_to_all x3 -> x0, blocking collectives: 109 us -> none  [the longest x2 97.4 us: trade(): y = lax.all_to_all(y, TRADE, split_axis=0, concat_axis=0, tiled=True)]
    all_to_all x1 -> x4, starting transfers between devices: 6.19 us -> 42.1 us  [trade(): y = lax.all_to_all(y, TRADE, split_axis=0, concat_axis=0, tiled=True)]
    ppermute x0 -> x6, starting transfers between devices: none -> 27.3 us  [shift(): return lax.ppermute(x, 'yh', [(i, (i + k) % LINE) for i in range(LINE)])]
    ppermute x0 -> x6, waiting for transfers between devices: none -> 15.6 us  [shift(): return lax.ppermute(x, 'yh', [(i, (i + k) % LINE) for i in range(LINE)])]
    all_to_all x1 -> x4, waiting for transfers between devices: 7.03 us -> 16.7 us  [trade(): y = lax.all_to_all(y, TRADE, split_axis=0, concat_axis=0, tiled=True)]
    pallas_call x7 -> x11, Pallas kernels: 10.1 us -> 18.9 us  [the longest x1 5.14 us: body(): call(plus_kernel, sums, 'plus', [ANY] * 8, limit=PLUS_LIMIT, flops=SHORT,...]
    ppermute x2 -> x6, starting transfers between devices: 4.2 us -> 12.1 us  [swap(): return lax.ppermute(x, 'core', [(0, 1), (1, 0)])]
  transfers between devices with their start and end apart: 3 -> 16, of which waited for: 3 -> 9; matrix products, arithmetic and copies ran while one was open for 0% -> 0% of each run, Pallas kernels for 3% -> 10%
where the time goes in v4:
time: 136 us; the launch traced here: 135 us
  starting transfers between devices  81.5 us (60%)
  waiting for transfers between devices  33.9 us (25%)
  Pallas kernels  18.9 us (14%)
    all_to_all x4, starting transfers between devices, trade(): y = lax.all_to_all(y, TRADE, split_axis=0, concat_axis=0, tiled=True)  42.1 us
    ppermute x6, starting transfers between devices, shift(): return lax.ppermute(x, 'yh', [(i, (i + k) % LINE) for i in range(LINE)])  27.3 us
    all_to_all x4, waiting for transfers between devices, trade(): y = lax.all_to_all(y, TRADE, split_axis=0, concat_axis=0, tiled=True)  16.7 us
    ppermute x6, waiting for transfers between devices, shift(): return lax.ppermute(x, 'yh', [(i, (i + k) % LINE) for i in range(LINE)])  15.6 us
    ppermute x6, starting transfers between devices, swap(): return lax.ppermute(x, 'core', [(0, 1), (1, 0)])  12.1 us
    pallas_call x1, Pallas kernels, body(): call(plus_kernel, sums, 'plus', [ANY] * 8, limit=PLUS_LIMIT, flops=SHORT,...  5.14 us
    pallas_call x1, Pallas kernels, body(): call(rest_kernel, [two] + [wire] * 4, 'rest', [VM, ANY], limit=REST_LIMIT...  3.59 us
  transfers between devices with their start and end apart: 16, of which 9 were waited for; matrix products, arithmetic and copies ran while one was open for 0% of the time, Pallas kernels for 10%

profile of v4, /device:TPU:8, one launch (start us, length us, event | category | flops | bytes accessed | tf_op | source)
XLA Modules:
  0.0 135.4 jit_solution(17049961243556400279)
XLA Ops:
  0.0 2.2 %pick.1 = (bf16[512,384]{1,0:T(8,128)(2,1)}, bf16[512,192]{1,0:T(8,128)(2,1)}, bf16[512,192]{1,0:T(8,128)(2,1)}) custom-call(s32[8,64]{1,0:T(8,128)} %bitcast.28, f32[8,64]{1,0:T(8,128)} %bitcast.29, bf16[64,256]{1,0:T(8,128)(2,1)} %tokens.1), custom_call_target="tpu_custom_call" | custom-call | tf_op jit(solution)/shard_map/pick/pallas_call | solution.py:300
  2.3 14.9 %all-to-all-start = ((bf16[64,8,384]{2,1,0:T(8,128)(2,1)}), bf16[64,8,384]{2,1,0:T(8,128)(2,1)S(1)}, u32[]{:S(2)}, u32[]{:S(2)}) async-start(bf16[64,8,384]{2,1,0:T(8,128)(2,1)} %bitcast.27), calls=%async_computation | async-start | bytes 786432 | tf_op jit(solution)/shard_map/all_to_all | solution.py:288
  17.2 6.8 %collective-permute-start = (bf16[64,256]{1,0:T(8,128)(2,1)}, bf16[64,256]{1,0:T(8,128)(2,1)S(1)}, u32[]{:S(2)}, u32[]{:S(2)}) collective-permute-start(bf16[64,256]{1,0:T(8,128)(2,1)} %tokens.1), channel_id=1, source_target_pairs={{0,256},{128,384},{256,0},{384,128},{1,257},{129,385},{257,1},{385... | collective-permute-start | bytes 98312 | tf_op jit(solution)/shard_map/ppermute | solution.py:284
  24.0 3.2 %collective-permute-done.tokens = bf16[64,256]{1,0:T(8,128)(2,1)S(1)} collective-permute-done((bf16[64,256]{1,0:T(8,128)(2,1)}, bf16[64,256]{1,0:T(8,128)(2,1)S(1)}, u32[]{:S(2)}, u32[]{:S(2)}) %collective-permute-start) | collective-permute-done | bytes 32800 | tf_op jit(solution)/shard_map/ppermute | solution.py:284
  27.2 0.0 copy-start.1
  27.2 0.9 copy-done.1
  28.1 1.1 wire.1
  29.2 2.3 %all-to-all-done = bf16[64,8,384]{2,1,0:T(8,128)(2,1)S(1)} async-done(((bf16[64,8,384]{2,1,0:T(8,128)(2,1)}), bf16[64,8,384]{2,1,0:T(8,128)(2,1)S(1)}, u32[]{:S(2)}, u32[]{:S(2)}) %all-to-all-start) | async-done | bytes 393248 | tf_op jit(solution)/shard_map/all_to_all | solution.py:288
  31.5 4.5 %collective-permute-start.2 = (bf16[512,384]{1,0:T(8,128)(2,1)S(1)}, bf16[512,384]{1,0:T(8,128)(2,1)S(1)}, u32[]{:S(2)}, u32[]{:S(2)}) collective-permute-start(bf16[512,384]{1,0:T(8,128)(2,1)S(1)} %bitcast.17), channel_id=1, source_target_pairs={{0,128},{128,256},{256,384},{384,0},{1,129},{129,257},{257,385},{3... | collective-permute-start | bytes 1179656 | tf_op jit(solution)/shard_map/ppermute | solution.py:284
  36.0 3.5 %collective-permute-start.4 = (bf16[512,384]{1,0:T(8,128)(2,1)S(1)}, bf16[512,384]{1,0:T(8,128)(2,1)S(1)}, u32[]{:S(2)}, u32[]{:S(2)}) collective-permute-start(bf16[512,384]{1,0:T(8,128)(2,1)S(1)} %bitcast.18), channel_id=1, source_target_pairs={{0,384},{128,0},{256,128},{384,256},{1,385},{129,1},{257,129},{385... | collective-permute-start | bytes 1179656 | tf_op jit(solution)/shard_map/ppermute | solution.py:284
  39.5 9.0 %all-to-all-start.1 = ((bf16[64,8,384]{2,1,0:T(8,128)(2,1)}), bf16[64,8,384]{2,1,0:T(8,128)(2,1)S(1)}, u32[]{:S(2)}, u32[]{:S(2)}) async-start(bf16[64,8,384]{2,1,0:T(8,128)(2,1)} %bitcast.4), calls=%async_computation.1 | async-start | bytes 786432 | tf_op jit(solution)/shard_map/all_to_all | solution.py:288
  48.5 1.9 %collective-permute-start.1 = (bf16[512,384]{1,0:T(8,128)(2,1)S(1)}, bf16[512,384]{1,0:T(8,128)(2,1)S(1)}, u32[]{:S(2)}, u32[]{:S(2)}) collective-permute-start(bf16[512,384]{1,0:T(8,128)(2,1)S(1)} %bitcast.19), channel_id=1, source_target_pairs={{0,64},{64,0},{1,65},{65,1},{2,66},{66,2},{3,67},{67,3},{4,68},{68... | collective-permute-start | bytes 1179656 | tf_op jit(solution)/shard_map/ppermute | solution.py:281
  50.4 1.1 collective-permute-done.2.refs_2_
  51.5 1.9 %collective-permute-start.3 = (bf16[512,384]{1,0:T(8,128)(2,1)S(1)}, bf16[512,384]{1,0:T(8,128)(2,1)S(1)}, u32[]{:S(2)}, u32[]{:S(2)}) collective-permute-start(bf16[512,384]{1,0:T(8,128)(2,1)S(1)} %collective-permute-done.2.refs_2_), channel_id=1, source_target_pairs={{0,64},{64,0},{1,65},{65,1},{2,66},{66,2},{3,67},{67,3},{4,68},{68... | collective-permute-start | bytes 1179656 | tf_op jit(solution)/shard_map/ppermute | solution.py:281
  53.5 3.4 %collective-permute-done.4.refs_4_ = bf16[512,384]{1,0:T(8,128)(2,1)S(1)} collective-permute-done((bf16[512,384]{1,0:T(8,128)(2,1)S(1)}, bf16[512,384]{1,0:T(8,128)(2,1)S(1)}, u32[]{:S(2)}, u32[]{:S(2)}) %collective-permute-start.4) | collective-permute-done | bytes 393248 | tf_op jit(solution)/shard_map/ppermute | solution.py:284
  56.9 1.9 %collective-permute-start.5 = (bf16[512,384]{1,0:T(8,128)(2,1)S(1)}, bf16[512,384]{1,0:T(8,128)(2,1)S(1)}, u32[]{:S(2)}, u32[]{:S(2)}) collective-permute-start(bf16[512,384]{1,0:T(8,128)(2,1)S(1)} %collective-permute-done.4.refs_4_), channel_id=1, source_target_pairs={{0,64},{64,0},{1,65},{65,1},{2,66},{66,2},{3,67},{67,3},{4,68},{68... | collective-permute-start | bytes 1179656 | tf_op jit(solution)/shard_map/ppermute | solution.py:281
  58.8 0.0 collective-permute-done.1.refs_1_
  58.8 0.0 collective-permute-done.3.refs_3_
  58.8 1.7 %collective-permute-done.5.refs_5_ = bf16[512,384]{1,0:T(8,128)(2,1)S(1)} collective-permute-done((bf16[512,384]{1,0:T(8,128)(2,1)S(1)}, bf16[512,384]{1,0:T(8,128)(2,1)S(1)}, u32[]{:S(2)}, u32[]{:S(2)}) %collective-permute-start.5) | collective-permute-done | bytes 393248 | tf_op jit(solution)/shard_map/ppermute | solution.py:281
  60.5 5.1 %plus.1 = (f32[512,768]{1,0:T(8,128)}, f32[256,768]{1,0:T(8,128)S(1)}) custom-call(bf16[2048,384]{1,0:T(8,128)(2,1)} %bitcast.21, bf16[2048,384]{1,0:T(8,128)(2,1)} %bitcast.23, bf16[512,384]{1,0:T(8,128)(2,1)S(1)} %bitcast.20, bf16[512,384]{1,0:T(8,128)(2,1)S(1)} %collective-permute-done.1.refs_1_, bf16[512,384]{1,0:T(8,128)(2,1)S(1)} %collective-permute-done.2.refs_2_, ...), custom_call_target="tpu_custom_call" | custom-call | flops 2000000000 | tf_op jit(solution)/shard_map/plus/pallas_call | solution.py:309
  65.6 0.0 all-to-all-done.1
  65.6 2.0 %collective-permute-start.6 = (bf16[512,384]{1,0:T(8,128)(2,1)S(1)}, bf16[512,384]{1,0:T(8,128)(2,1)S(1)}, u32[]{:S(2)}, u32[]{:S(2)}) collective-permute-start(bf16[512,384]{1,0:T(8,128)(2,1)S(1)} %bitcast.13), channel_id=1, source_target_pairs={{0,64},{64,0},{1,65},{65,1},{2,66},{66,2},{3,67},{67,3},{4,68},{68... | collective-permute-start | bytes 1179656 | tf_op jit(solution)/shard_map/ppermute | solution.py:281
  67.7 1.8 %load.1 = (f32[256,768]{1,0:T(8,128)S(1)}, f32[256,768]{1,0:T(8,128)S(1)}, f32[256,768]{1,0:T(8,128)S(1)}, bf16[512,768]{1,0:T(8,128)(2,1)S(1)}, bf16[384,512]{1,0:T(8,128)(2,1)S(1)}) custom-call(bf16[2048,384]{1,0:T(8,128)(2,1)} %bitcast.22, bf16[2048,384]{1,0:T(8,128)(2,1)} %bitcast.24, bf16[384,2048]{1,0:T(8,128)(2,1)} %bitcast.25, ...), custom_call_target="tpu_custom_call" | custom-call | tf_op jit(solution)/shard_map/load/pallas_call | solution.py:328
  69.5 0.0 collective-permute-done.6.sib
  69.5 1.7 %hidden.1 = (bf16[768,384]{1,0:T(8,128)(2,1)S(1)}, bf16[1024,384]{1,0:T(8,128)(2,1)S(1)}) custom-call(bf16[512,384]{1,0:T(8,128)(2,1)S(1)} %bitcast.14, bf16[512,384]{1,0:T(8,128)(2,1)S(1)} %collective-permute-done.6.sib, f32[256,768]{1,0:T(8,128)S(1)} %get-tuple-element.42.acc_top, f32[256,768]{1,0:T(8,128)S(1)} %get-tuple-element.43.acc_low, ...), custom_call_target="tpu_custom_call" | custom-call | flops 905969664 | tf_op jit(solution)/shard_map/hidden/pallas_call | solution.py:336
  71.2 2.3 %collective-permute-start.7 = (bf16[1024,384]{1,0:T(8,128)(2,1)S(1)}, bf16[1024,384]{1,0:T(8,128)(2,1)S(1)}, u32[]{:S(2)}, u32[]{:S(2)}) collective-permute-start(bf16[1024,384]{1,0:T(8,128)(2,1)S(1)} %get-tuple-element.51), channel_id=1, source_target_pairs={{0,64},{64,0},{1,65},{65,1},{2,66},{66,2},{3,67},{67,3},{4,68},{68... | collective-permute-start | bytes 2359304 | tf_op jit(solution)/shard_map/ppermute | solution.py:281
  73.5 3.6 %rest.1 = (bf16[1024,384]{1,0:T(8,128)(2,1)S(1)}, bf16[512,384]{1,0:T(8,128)(2,1)S(1)}, bf16[512,384]{1,0:T(8,128)(2,1)S(1)}, bf16[512,384]{1,0:T(8,128)(2,1)S(1)}, bf16[512,384]{1,0:T(8,128)(2,1)S(1)}) custom-call(bf16[768,384]{1,0:T(8,128)(2,1)S(1)} %get-tuple-element.47.h, bf16[384,2048]{1,0:T(8,128)(2,1)} %bitcast.26), custom_call_target="tpu_custom_call" | custom-call | flops 905969664 | tf_op jit(solution)/shard_map/rest/pallas_call | solution.py:340
  77.1 0.0 collective-permute-done.7.give
  77.1 0.2 pair.1
  77.3 2.0 %collective-permute-start.8 = (bf16[1024,384]{1,0:T(8,128)(2,1)S(1)}, bf16[1024,384]{1,0:T(8,128)(2,1)S(1)}, u32[]{:S(2)}, u32[]{:S(2)}) collective-permute-start(bf16[1024,384]{1,0:T(8,128)(2,1)S(1)} %get-tuple-element.55), channel_id=1, source_target_pairs={{0,64},{64,0},{1,65},{65,1},{2,66},{66,2},{3,67},{67,3},{4,68},{68... | collective-permute-start | bytes 2359304 | tf_op jit(solution)/shard_map/ppermute | solution.py:281
  79.4 2.9 %collective-permute-start.10 = (bf16[512,384]{1,0:T(8,128)(2,1)S(1)}, bf16[512,384]{1,0:T(8,128)(2,1)S(1)}, u32[]{:S(2)}, u32[]{:S(2)}) collective-permute-start(bf16[512,384]{1,0:T(8,128)(2,1)S(1)} %get-tuple-element.57), channel_id=1, source_target_pairs={{0,384},{128,0},{256,128},{384,256},{1,385},{129,1},{257,129},{385... | collective-permute-start | bytes 1179656 | tf_op jit(solution)/shard_map/ppermute | solution.py:284
  82.2 3.9 %collective-permute-start.9 = (bf16[512,384]{1,0:T(8,128)(2,1)S(1)}, bf16[512,384]{1,0:T(8,128)(2,1)S(1)}, u32[]{:S(2)}, u32[]{:S(2)}) collective-permute-start(bf16[512,384]{1,0:T(8,128)(2,1)S(1)} %get-tuple-element.56), channel_id=1, source_target_pairs={{0,128},{128,256},{256,384},{384,0},{1,129},{129,257},{257,385},{3... | collective-permute-start | bytes 1179656 | tf_op jit(solution)/shard_map/ppermute | solution.py:284
  86.1 0.0 collective-permute-done.8.give
  86.1 0.8 two_sum.1
  87.0 10.9 %all-to-all-start.3 = ((bf16[64,8,384]{2,1,0:T(8,128)(2,1)}), bf16[64,8,384]{2,1,0:T(8,128)(2,1)S(1)}, u32[]{:S(2)}, u32[]{:S(2)}) async-start(bf16[64,8,384]{2,1,0:T(8,128)(2,1)} %bitcast.11), calls=%async_computation.3 | async-start | bytes 786432 | tf_op jit(solution)/shard_map/all_to_all | solution.py:288
  97.9 4.8 %collective-permute-done.10.three = bf16[512,384]{1,0:T(8,128)(2,1)S(1)} collective-permute-done((bf16[512,384]{1,0:T(8,128)(2,1)S(1)}, bf16[512,384]{1,0:T(8,128)(2,1)S(1)}, u32[]{:S(2)}, u32[]{:S(2)}) %collective-permute-start.10) | collective-permute-done | bytes 393248 | tf_op jit(solution)/shard_map/ppermute | solution.py:284
  102.7 3.1 %collective-permute-done.9.one = bf16[512,384]{1,0:T(8,128)(2,1)S(1)} collective-permute-done((bf16[512,384]{1,0:T(8,128)(2,1)S(1)}, bf16[512,384]{1,0:T(8,128)(2,1)S(1)}, u32[]{:S(2)}, u32[]{:S(2)}) %collective-permute-start.9) | collective-permute-done | bytes 393248 | tf_op jit(solution)/shard_map/ppermute | solution.py:284
  105.8 0.0 copy-start
  105.8 0.9 sum.1
  106.7 6.1 %all-to-all-done.3 = bf16[64,8,384]{2,1,0:T(8,128)(2,1)S(1)} async-done(((bf16[64,8,384]{2,1,0:T(8,128)(2,1)}), bf16[64,8,384]{2,1,0:T(8,128)(2,1)S(1)}, u32[]{:S(2)}, u32[]{:S(2)}) %all-to-all-start.3) | async-done | bytes 393248 | tf_op jit(solution)/shard_map/all_to_all | solution.py:288
  112.8 7.3 %all-to-all-start.2 = ((bf16[64,8,384]{2,1,0:T(8,128)(2,1)}), bf16[64,8,384]{2,1,0:T(8,128)(2,1)S(1)}, u32[]{:S(2)}, u32[]{:S(2)}) async-start(bf16[64,8,384]{2,1,0:T(8,128)(2,1)} %bitcast.9), calls=%async_computation.2 | async-start | bytes 786432 | tf_op jit(solution)/shard_map/all_to_all | solution.py:288
  120.1 0.0 copy-done
  120.1 0.4 mix.1
  120.5 5.7 %collective-permute-start.11 = (bf16[64,256]{1,0:T(8,128)(2,1)S(1)}, bf16[64,256]{1,0:T(8,128)(2,1)S(1)}, u32[]{:S(2)}, u32[]{:S(2)}) collective-permute-start(bf16[64,256]{1,0:T(8,128)(2,1)S(1)} %mix.1), channel_id=1, source_target_pairs={{0,256},{128,384},{256,0},{384,128},{1,257},{129,385},{257,1},{385... | collective-permute-start | bytes 98312 | tf_op jit(solution)/shard_map/ppermute | solution.py:284
  126.2 8.2 %all-to-all-done.2 = bf16[64,8,384]{2,1,0:T(8,128)(2,1)S(1)} async-done(((bf16[64,8,384]{2,1,0:T(8,128)(2,1)}), bf16[64,8,384]{2,1,0:T(8,128)(2,1)S(1)}, u32[]{:S(2)}, u32[]{:S(2)}) %all-to-all-start.2) | async-done | bytes 393248 | tf_op jit(solution)/shard_map/all_to_all | solution.py:288
  134.5 0.0 collective-permute-done.11.other
  134.5 1.0 last.1
Async XLA Ops:
  2.3 29.2 %all-to-all-start = ((bf16[64,8,384]{2,1,0:T(8,128)(2,1)}), bf16[64,8,384]{2,1,0:T(8,128)(2,1)S(1)}, u32[]{:S(2)}, u32[]{:S(2)}) async-start(bf16[64,8,384]{2,1,0:T(8,128)(2,1)} %bitcast.27), calls=%async_computation | async-start | bytes 786432 | tf_op jit(solution)/shard_map/all_to_all | solution.py:288
  17.2 10.0 %collective-permute-start = (bf16[64,256]{1,0:T(8,128)(2,1)}, bf16[64,256]{1,0:T(8,128)(2,1)S(1)}, u32[]{:S(2)}, u32[]{:S(2)}) collective-permute-start(bf16[64,256]{1,0:T(8,128)(2,1)} %tokens.1), channel_id=1, source_target_pairs={{0,256},{128,384},{256,0},{384,128},{1,257},{129,385},{257,1},{385... | collective-permute-start | bytes 98312 | tf_op jit(solution)/shard_map/ppermute | solution.py:284
  27.2 1.0 copy-start.1
  31.5 20.0 %collective-permute-start.2 = (bf16[512,384]{1,0:T(8,128)(2,1)S(1)}, bf16[512,384]{1,0:T(8,128)(2,1)S(1)}, u32[]{:S(2)}, u32[]{:S(2)}) collective-permute-start(bf16[512,384]{1,0:T(8,128)(2,1)S(1)} %bitcast.17), channel_id=1, source_target_pairs={{0,128},{128,256},{256,384},{384,0},{1,129},{129,257},{257,385},{3... | collective-permute-start | bytes 1179656 | tf_op jit(solution)/shard_map/ppermute | solution.py:284
  36.0 20.9 %collective-permute-start.4 = (bf16[512,384]{1,0:T(8,128)(2,1)S(1)}, bf16[512,384]{1,0:T(8,128)(2,1)S(1)}, u32[]{:S(2)}, u32[]{:S(2)}) collective-permute-start(bf16[512,384]{1,0:T(8,128)(2,1)S(1)} %bitcast.18), channel_id=1, source_target_pairs={{0,384},{128,0},{256,128},{384,256},{1,385},{129,1},{257,129},{385... | collective-permute-start | bytes 1179656 | tf_op jit(solution)/shard_map/ppermute | solution.py:284
  39.5 26.2 %all-to-all-start.1 = ((bf16[64,8,384]{2,1,0:T(8,128)(2,1)}), bf16[64,8,384]{2,1,0:T(8,128)(2,1)S(1)}, u32[]{:S(2)}, u32[]{:S(2)}) async-start(bf16[64,8,384]{2,1,0:T(8,128)(2,1)} %bitcast.4), calls=%async_computation.1 | async-start | bytes 786432 | tf_op jit(solution)/shard_map/all_to_all | solution.py:288
  48.5 10.3 %collective-permute-start.1 = (bf16[512,384]{1,0:T(8,128)(2,1)S(1)}, bf16[512,384]{1,0:T(8,128)(2,1)S(1)}, u32[]{:S(2)}, u32[]{:S(2)}) collective-permute-start(bf16[512,384]{1,0:T(8,128)(2,1)S(1)} %bitcast.19), channel_id=1, source_target_pairs={{0,64},{64,0},{1,65},{65,1},{2,66},{66,2},{3,67},{67,3},{4,68},{68... | collective-permute-start | bytes 1179656 | tf_op jit(solution)/shard_map/ppermute | solution.py:281
  51.5 7.2 %collective-permute-start.3 = (bf16[512,384]{1,0:T(8,128)(2,1)S(1)}, bf16[512,384]{1,0:T(8,128)(2,1)S(1)}, u32[]{:S(2)}, u32[]{:S(2)}) collective-permute-start(bf16[512,384]{1,0:T(8,128)(2,1)S(1)} %collective-permute-done.2.refs_2_), channel_id=1, source_target_pairs={{0,64},{64,0},{1,65},{65,1},{2,66},{66,2},{3,67},{67,3},{4,68},{68... | collective-permute-start | bytes 1179656 | tf_op jit(solution)/shard_map/ppermute | solution.py:281
  56.9 3.6 %collective-permute-start.5 = (bf16[512,384]{1,0:T(8,128)(2,1)S(1)}, bf16[512,384]{1,0:T(8,128)(2,1)S(1)}, u32[]{:S(2)}, u32[]{:S(2)}) collective-permute-start(bf16[512,384]{1,0:T(8,128)(2,1)S(1)} %collective-permute-done.4.refs_4_), channel_id=1, source_target_pairs={{0,64},{64,0},{1,65},{65,1},{2,66},{66,2},{3,67},{67,3},{4,68},{68... | collective-permute-start | bytes 1179656 | tf_op jit(solution)/shard_map/ppermute | solution.py:281
  65.6 3.9 %collective-permute-start.6 = (bf16[512,384]{1,0:T(8,128)(2,1)S(1)}, bf16[512,384]{1,0:T(8,128)(2,1)S(1)}, u32[]{:S(2)}, u32[]{:S(2)}) collective-permute-start(bf16[512,384]{1,0:T(8,128)(2,1)S(1)} %bitcast.13), channel_id=1, source_target_pairs={{0,64},{64,0},{1,65},{65,1},{2,66},{66,2},{3,67},{67,3},{4,68},{68... | collective-permute-start | bytes 1179656 | tf_op jit(solution)/shard_map/ppermute | solution.py:281
  71.2 5.9 %collective-permute-start.7 = (bf16[1024,384]{1,0:T(8,128)(2,1)S(1)}, bf16[1024,384]{1,0:T(8,128)(2,1)S(1)}, u32[]{:S(2)}, u32[]{:S(2)}) collective-permute-start(bf16[1024,384]{1,0:T(8,128)(2,1)S(1)} %get-tuple-element.51), channel_id=1, source_target_pairs={{0,64},{64,0},{1,65},{65,1},{2,66},{66,2},{3,67},{67,3},{4,68},{68... | collective-permute-start | bytes 2359304 | tf_op jit(solution)/shard_map/ppermute | solution.py:281
  77.3 8.8 %collective-permute-start.8 = (bf16[1024,384]{1,0:T(8,128)(2,1)S(1)}, bf16[1024,384]{1,0:T(8,128)(2,1)S(1)}, u32[]{:S(2)}, u32[]{:S(2)}) collective-permute-start(bf16[1024,384]{1,0:T(8,128)(2,1)S(1)} %get-tuple-element.55), channel_id=1, source_target_pairs={{0,64},{64,0},{1,65},{65,1},{2,66},{66,2},{3,67},{67,3},{4,68},{68... | collective-permute-start | bytes 2359304 | tf_op jit(solution)/shard_map/ppermute | solution.py:281
  79.4 23.3 %collective-permute-start.10 = (bf16[512,384]{1,0:T(8,128)(2,1)S(1)}, bf16[512,384]{1,0:T(8,128)(2,1)S(1)}, u32[]{:S(2)}, u32[]{:S(2)}) collective-permute-start(bf16[512,384]{1,0:T(8,128)(2,1)S(1)} %get-tuple-element.57), channel_id=1, source_target_pairs={{0,384},{128,0},{256,128},{384,256},{1,385},{129,1},{257,129},{385... | collective-permute-start | bytes 1179656 | tf_op jit(solution)/shard_map/ppermute | solution.py:284
  82.2 23.5 %collective-permute-start.9 = (bf16[512,384]{1,0:T(8,128)(2,1)S(1)}, bf16[512,384]{1,0:T(8,128)(2,1)S(1)}, u32[]{:S(2)}, u32[]{:S(2)}) collective-permute-start(bf16[512,384]{1,0:T(8,128)(2,1)S(1)} %get-tuple-element.56), channel_id=1, source_target_pairs={{0,128},{128,256},{256,384},{384,0},{1,129},{129,257},{257,385},{3... | collective-permute-start | bytes 1179656 | tf_op jit(solution)/shard_map/ppermute | solution.py:284
  87.0 25.9 %all-to-all-start.3 = ((bf16[64,8,384]{2,1,0:T(8,128)(2,1)}), bf16[64,8,384]{2,1,0:T(8,128)(2,1)S(1)}, u32[]{:S(2)}, u32[]{:S(2)}) async-start(bf16[64,8,384]{2,1,0:T(8,128)(2,1)} %bitcast.11), calls=%async_computation.3 | async-start | bytes 786432 | tf_op jit(solution)/shard_map/all_to_all | solution.py:288
  105.8 14.4 %copy-start = (bf16[512,192]{1,0:T(8,128)(2,1)S(1)}, bf16[512,192]{1,0:T(8,128)(2,1)}, u32[]{:S(2)}) copy-start(bf16[512,192]{1,0:T(8,128)(2,1)} %get-tuple-element.32.mix) | copy-start | bytes 589828
  112.8 21.6 %all-to-all-start.2 = ((bf16[64,8,384]{2,1,0:T(8,128)(2,1)}), bf16[64,8,384]{2,1,0:T(8,128)(2,1)S(1)}, u32[]{:S(2)}, u32[]{:S(2)}) async-start(bf16[64,8,384]{2,1,0:T(8,128)(2,1)} %bitcast.9), calls=%async_computation.2 | async-start | bytes 786432 | tf_op jit(solution)/shard_map/all_to_all | solution.py:288
  120.5 14.0 %collective-permute-start.11 = (bf16[64,256]{1,0:T(8,128)(2,1)S(1)}, bf16[64,256]{1,0:T(8,128)(2,1)S(1)}, u32[]{:S(2)}, u32[]{:S(2)}) collective-permute-start(bf16[64,256]{1,0:T(8,128)(2,1)S(1)} %mix.1), channel_id=1, source_target_pairs={{0,256},{128,384},{256,0},{384,128},{1,257},{129,385},{257,1},{385... | collective-permute-start | bytes 98312 | tf_op jit(solution)/shard_map/ppermute | solution.py:284

commit v5 on v4

--- a/solution.py
+++ b/solution.py
@@ -15,10 +15,10 @@
 LONG = 40_000_000_000
 SHORT = 2_000_000_000
 PLUS_LIMIT = 50 << 20
-LOAD_LIMIT = 49 << 20
-REST_LIMIT = 50 << 20
+LOAD_LIMIT = 48 << 20
+REST_LIMIT = 32 << 20
 LIMIT = 32 << 20
-PICK_LIMIT = 58 << 20
+PICK_LIMIT = 62 << 20
 DP = {"yh": 4, "core": 2}
 EXPERT = {"z": 8, "yl": 2, "x": 4}
 TRADE = ("yl", "z", "x")
@@ -189,7 +189,7 @@
     back.wait()
 
 
-def load_kernel(wg, wu, wd, acc_near, acc_far, out_top, out_low, out_far, up, give13, sems):
+def load_kernel(wg, wu, wd, acc_near, acc_far, out_top, out_low, out_far, up, give13, give20, keep13, keep20, sems):
     yh, core = place()
     band = up.shape[0] // 2
     fetch = Fetch(sems)
@@ -199,8 +199,10 @@
     fetch(acc_far, out_far)
     fetch.up(wg, wu, up, 0, band_at(yh + 2, core, band))
     fetch.up(wg, wu, up, 1, band_at(yh + 2, 1 - core, band))
-    for slot, k in enumerate((1, 3)):
-        fetch(wd.at[:, band_at(yh + k, 1 - core, band)], give13.at[:, pl.ds(slot * band, band)])
+    downs = ((give13, (1, 3), 1 - core), (give20, (2, 0), 1 - core), (keep13, (1, 3), core), (keep20, (2, 0), core))
+    for down, ks, parity in downs:
+        for slot, k in enumerate(ks):
+            fetch(wd.at[:, band_at(yh + k, parity, band)], down.at[:, pl.ds(slot * band, band)])
     fetch.wait()
 
 
@@ -226,16 +228,9 @@
     pack(h[:n, :], h[n:, :], down, halves(give))
 
 
-def rest_kernel(h, wd, give, keep1, keep3, keep2, keep0, give20, keep13, keep20, sems):
-    yh, core = place()
-    band = give20.shape[1] // 2
-    fetch = Fetch(sems)
-    for down, ks, parity in ((give20, (2, 0), 1 - core), (keep13, (1, 3), core), (keep20, (2, 0), core)):
-        for slot, k in enumerate(ks):
-            fetch(wd.at[:, band_at(yh + k, parity, band)], down.at[:, pl.ds(slot * band, band)])
+def rest_kernel(h, give20, keep13, keep20, give, keep1, keep3, keep2, keep0):
     n = h.shape[0] // SEATS * NEAR
     near, far = h[:n, :], h[n:, :]
-    fetch.wait()
     pack(near, far, keep13, (keep1, keep3))
     pack(near, far, give20, halves(give))
     pack(near, far, keep20, (keep2, keep0))
@@ -325,13 +320,13 @@
     got2, sums0 = tie((got2, sums0))
     sib2 = swap(got2)
     pair = ((wide, 2 * band), BF)
-    top, low, far, up2, give13 = call(
+    top, low, far, up2, give13, give20, keep13, keep20 = call(
         load_kernel,
-        [((experts * FAR, 2 * wide), F32)] * 3 + [((2 * band, 2 * wide), BF), pair],
+        [((experts * FAR, 2 * wide), F32)] * 3 + [((2 * band, 2 * wide), BF)] + [pair] * 4,
         "load",
         [ANY, ANY, ANY, HBM, HBM],
         limit=LOAD_LIMIT,
-        scratch=[sems(9)],
+        scratch=[sems(15)],
     )(wg, wu, wd, *sums0)
     h, give_a = call(
         hidden_kernel, [((experts * SEATS, wide), BF), two], "hidden", [VM] * 7, flops=6 * work
@@ -341,11 +336,10 @@
         rest_kernel,
         [two] + [wire] * 4,
         "rest",
-        [VM, ANY],
+        [VM] * 4,
         limit=REST_LIMIT,
         flops=6 * work,
-        scratch=[pltpu.VMEM(*pair)] * 3 + [sems(6)],
-    )(h, wd)
+    )(h, give20, keep13, keep20)
     one, three = call(pair_kernel, [wire] * 2, "pair", [VM] * 3)(keep1, keep3, give_a)
     one, three, give_b = tie((one, three, give_b))
     one, three = shift(one, 1), shift(three, 3)

time: 136 us -> 135 us (level)
    pallas_call x1, Pallas kernels: 3.59 us -> 2.15 us  [body(): call(rest_kernel, [two] + [wire] * 4, 'rest', [VM] * 4, limit=REST_LIMIT,...]
  transfers between devices with their start and end apart: 16 -> 16, of which waited for: 9 -> 9; matrix products, arithmetic and copies ran while one was open for 0% -> 0% of each run, Pallas kernels for 10% -> 9%
where the time goes in v5:
time: 135 us; the launch traced here: 134 us
  starting transfers between devices  81.5 us (60%)
  waiting for transfers between devices  33.9 us (25%)
  Pallas kernels  17.9 us (13%)
    all_to_all x4, starting transfers between devices, trade(): y = lax.all_to_all(y, TRADE, split_axis=0, concat_axis=0, tiled=True)  42.1 us
    ppermute x6, starting transfers between devices, shift(): return lax.ppermute(x, 'yh', [(i, (i + k) % LINE) for i in range(LINE)])  27.3 us
    all_to_all x4, waiting for transfers between devices, trade(): y = lax.all_to_all(y, TRADE, split_axis=0, concat_axis=0, tiled=True)  16.7 us
    ppermute x6, waiting for transfers between devices, shift(): return lax.ppermute(x, 'yh', [(i, (i + k) % LINE) for i in range(LINE)])  15.6 us
    ppermute x6, starting transfers between devices, swap(): return lax.ppermute(x, 'core', [(0, 1), (1, 0)])  12.1 us
    pallas_call x1, Pallas kernels, body(): call(plus_kernel, sums, 'plus', [ANY] * 8, limit=PLUS_LIMIT, flops=SHORT,...  5.14 us
  transfers between devices with their start and end apart: 16, of which 9 were waited for; matrix products, arithmetic and copies ran while one was open for 0% of the time, Pallas kernels for 9%

profile of v5, /device:TPU:8, one launch (start us, length us, event | category | flops | bytes accessed | tf_op | source)
XLA Modules:
  0.0 134.4 jit_solution(16426761910578793259)
XLA Ops:
  0.0 2.2 %pick.1 = (bf16[512,384]{1,0:T(8,128)(2,1)}, bf16[512,192]{1,0:T(8,128)(2,1)}, bf16[512,192]{1,0:T(8,128)(2,1)}) custom-call(s32[8,64]{1,0:T(8,128)} %bitcast.27, f32[8,64]{1,0:T(8,128)} %bitcast.28, bf16[64,256]{1,0:T(8,128)(2,1)} %tokens.1), custom_call_target="tpu_custom_call" | custom-call | tf_op jit(solution)/shard_map/pick/pallas_call | solution.py:295
  2.3 14.9 %all-to-all-start = ((bf16[64,8,384]{2,1,0:T(8,128)(2,1)}), bf16[64,8,384]{2,1,0:T(8,128)(2,1)S(1)}, u32[]{:S(2)}, u32[]{:S(2)}) async-start(bf16[64,8,384]{2,1,0:T(8,128)(2,1)} %bitcast.26), calls=%async_computation | async-start | bytes 786432 | tf_op jit(solution)/shard_map/all_to_all | solution.py:283
  17.2 6.8 %collective-permute-start = (bf16[64,256]{1,0:T(8,128)(2,1)}, bf16[64,256]{1,0:T(8,128)(2,1)S(1)}, u32[]{:S(2)}, u32[]{:S(2)}) collective-permute-start(bf16[64,256]{1,0:T(8,128)(2,1)} %tokens.1), channel_id=1, source_target_pairs={{0,256},{128,384},{256,0},{384,128},{1,257},{129,385},{257,1},{385... | collective-permute-start | bytes 98312 | tf_op jit(solution)/shard_map/ppermute | solution.py:279
  24.0 3.2 %collective-permute-done.tokens = bf16[64,256]{1,0:T(8,128)(2,1)S(1)} collective-permute-done((bf16[64,256]{1,0:T(8,128)(2,1)}, bf16[64,256]{1,0:T(8,128)(2,1)S(1)}, u32[]{:S(2)}, u32[]{:S(2)}) %collective-permute-start) | collective-permute-done | bytes 32800 | tf_op jit(solution)/shard_map/ppermute | solution.py:279
  27.2 0.0 copy-start.1
  27.2 0.9 copy-done.1
  28.1 1.1 wire.1
  29.2 2.3 %all-to-all-done = bf16[64,8,384]{2,1,0:T(8,128)(2,1)S(1)} async-done(((bf16[64,8,384]{2,1,0:T(8,128)(2,1)}), bf16[64,8,384]{2,1,0:T(8,128)(2,1)S(1)}, u32[]{:S(2)}, u32[]{:S(2)}) %all-to-all-start) | async-done | bytes 393248 | tf_op jit(solution)/shard_map/all_to_all | solution.py:283
  31.5 4.5 %collective-permute-start.2 = (bf16[512,384]{1,0:T(8,128)(2,1)S(1)}, bf16[512,384]{1,0:T(8,128)(2,1)S(1)}, u32[]{:S(2)}, u32[]{:S(2)}) collective-permute-start(bf16[512,384]{1,0:T(8,128)(2,1)S(1)} %bitcast.17), channel_id=1, source_target_pairs={{0,128},{128,256},{256,384},{384,0},{1,129},{129,257},{257,385},{3... | collective-permute-start | bytes 1179656 | tf_op jit(solution)/shard_map/ppermute | solution.py:279
  36.0 3.5 %collective-permute-start.4 = (bf16[512,384]{1,0:T(8,128)(2,1)S(1)}, bf16[512,384]{1,0:T(8,128)(2,1)S(1)}, u32[]{:S(2)}, u32[]{:S(2)}) collective-permute-start(bf16[512,384]{1,0:T(8,128)(2,1)S(1)} %bitcast.18), channel_id=1, source_target_pairs={{0,384},{128,0},{256,128},{384,256},{1,385},{129,1},{257,129},{385... | collective-permute-start | bytes 1179656 | tf_op jit(solution)/shard_map/ppermute | solution.py:279
  39.5 9.0 %all-to-all-start.1 = ((bf16[64,8,384]{2,1,0:T(8,128)(2,1)}), bf16[64,8,384]{2,1,0:T(8,128)(2,1)S(1)}, u32[]{:S(2)}, u32[]{:S(2)}) async-start(bf16[64,8,384]{2,1,0:T(8,128)(2,1)} %bitcast.4), calls=%async_computation.1 | async-start | bytes 786432 | tf_op jit(solution)/shard_map/all_to_all | solution.py:283
  48.5 1.9 %collective-permute-start.1 = (bf16[512,384]{1,0:T(8,128)(2,1)S(1)}, bf16[512,384]{1,0:T(8,128)(2,1)S(1)}, u32[]{:S(2)}, u32[]{:S(2)}) collective-permute-start(bf16[512,384]{1,0:T(8,128)(2,1)S(1)} %bitcast.19), channel_id=1, source_target_pairs={{0,64},{64,0},{1,65},{65,1},{2,66},{66,2},{3,67},{67,3},{4,68},{68... | collective-permute-start | bytes 1179656 | tf_op jit(solution)/shard_map/ppermute | solution.py:276
  50.4 1.1 collective-permute-done.2.refs_2_
  51.5 1.9 %collective-permute-start.3 = (bf16[512,384]{1,0:T(8,128)(2,1)S(1)}, bf16[512,384]{1,0:T(8,128)(2,1)S(1)}, u32[]{:S(2)}, u32[]{:S(2)}) collective-permute-start(bf16[512,384]{1,0:T(8,128)(2,1)S(1)} %collective-permute-done.2.refs_2_), channel_id=1, source_target_pairs={{0,64},{64,0},{1,65},{65,1},{2,66},{66,2},{3,67},{67,3},{4,68},{68... | collective-permute-start | bytes 1179656 | tf_op jit(solution)/shard_map/ppermute | solution.py:276
  53.5 3.4 %collective-permute-done.4.refs_4_ = bf16[512,384]{1,0:T(8,128)(2,1)S(1)} collective-permute-done((bf16[512,384]{1,0:T(8,128)(2,1)S(1)}, bf16[512,384]{1,0:T(8,128)(2,1)S(1)}, u32[]{:S(2)}, u32[]{:S(2)}) %collective-permute-start.4) | collective-permute-done | bytes 393248 | tf_op jit(solution)/shard_map/ppermute | solution.py:279
  56.9 1.9 %collective-permute-start.5 = (bf16[512,384]{1,0:T(8,128)(2,1)S(1)}, bf16[512,384]{1,0:T(8,128)(2,1)S(1)}, u32[]{:S(2)}, u32[]{:S(2)}) collective-permute-start(bf16[512,384]{1,0:T(8,128)(2,1)S(1)} %collective-permute-done.4.refs_4_), channel_id=1, source_target_pairs={{0,64},{64,0},{1,65},{65,1},{2,66},{66,2},{3,67},{67,3},{4,68},{68... | collective-permute-start | bytes 1179656 | tf_op jit(solution)/shard_map/ppermute | solution.py:276
  58.8 0.0 collective-permute-done.1.refs_1_
  58.8 0.0 collective-permute-done.3.refs_3_
  58.8 1.7 %collective-permute-done.5.refs_5_ = bf16[512,384]{1,0:T(8,128)(2,1)S(1)} collective-permute-done((bf16[512,384]{1,0:T(8,128)(2,1)S(1)}, bf16[512,384]{1,0:T(8,128)(2,1)S(1)}, u32[]{:S(2)}, u32[]{:S(2)}) %collective-permute-start.5) | collective-permute-done | bytes 393248 | tf_op jit(solution)/shard_map/ppermute | solution.py:276
  60.5 5.1 %plus.1 = (f32[512,768]{1,0:T(8,128)}, f32[256,768]{1,0:T(8,128)S(1)}) custom-call(bf16[2048,384]{1,0:T(8,128)(2,1)} %bitcast.21, bf16[2048,384]{1,0:T(8,128)(2,1)} %bitcast.23, bf16[512,384]{1,0:T(8,128)(2,1)S(1)} %bitcast.20, bf16[512,384]{1,0:T(8,128)(2,1)S(1)} %collective-permute-done.1.refs_1_, bf16[512,384]{1,0:T(8,128)(2,1)S(1)} %collective-permute-done.2.refs_2_, ...), custom_call_target="tpu_custom_call" | custom-call | flops 2000000000 | tf_op jit(solution)/shard_map/plus/pallas_call | solution.py:304
  65.6 0.0 all-to-all-done.1
  65.6 2.0 %collective-permute-start.6 = (bf16[512,384]{1,0:T(8,128)(2,1)S(1)}, bf16[512,384]{1,0:T(8,128)(2,1)S(1)}, u32[]{:S(2)}, u32[]{:S(2)}) collective-permute-start(bf16[512,384]{1,0:T(8,128)(2,1)S(1)} %bitcast.13), channel_id=1, source_target_pairs={{0,64},{64,0},{1,65},{65,1},{2,66},{66,2},{3,67},{67,3},{4,68},{68... | collective-permute-start | bytes 1179656 | tf_op jit(solution)/shard_map/ppermute | solution.py:276
  67.7 2.2 %load.1 = (f32[256,768]{1,0:T(8,128)S(1)}, f32[256,768]{1,0:T(8,128)S(1)}, f32[256,768]{1,0:T(8,128)S(1)}, bf16[512,768]{1,0:T(8,128)(2,1)S(1)}, bf16[384,512]{1...) custom-call(bf16[2048,384]{1,0:T(8,128)(2,1)} %bitcast.22, ...), custom_call_target="tpu_custom_call" | custom-call | tf_op jit(solution)/shard_map/load/pallas_call | solution.py:323
  69.9 0.0 collective-permute-done.6.sib
  69.9 1.7 %hidden.1 = (bf16[768,384]{1,0:T(8,128)(2,1)S(1)}, bf16[1024,384]{1,0:T(8,128)(2,1)S(1)}) custom-call(bf16[512,384]{1,0:T(8,128)(2,1)S(1)} %bitcast.14, bf16[512,384]{1,0:T(8,128)(2,1)S(1)} %collective-permute-done.6.sib, f32[256,768]{1,0:T(8,128)S(1)} %get-tuple-element.45.acc_top, f32[256,768]{1,0:T(8,128)S(1)} %get-tuple-element.46.acc_low, ...), custom_call_target="tpu_custom_call" | custom-call | flops 905969664 | tf_op jit(solution)/shard_map/hidden/pallas_call | solution.py:331
  71.7 2.3 %collective-permute-start.7 = (bf16[1024,384]{1,0:T(8,128)(2,1)S(1)}, bf16[1024,384]{1,0:T(8,128)(2,1)S(1)}, u32[]{:S(2)}, u32[]{:S(2)}) collective-permute-start(bf16[1024,384]{1,0:T(8,128)(2,1)S(1)} %get-tuple-element.57), channel_id=1, source_target_pairs={{0,64},{64,0},{1,65},{65,1},{2,66},{66,2},{3,67},{67,3},{4,68},{68... | collective-permute-start | bytes 2359304 | tf_op jit(solution)/shard_map/ppermute | solution.py:276
  73.9 2.2 %rest.1 = (bf16[1024,384]{1,0:T(8,128)(2,1)S(1)}, bf16[512,384]{1,0:T(8,128)(2,1)S(1)}, bf16[512,384]{1,0:T(8,128)(2,1)S(1)}, bf16[512,384]{1,0:T(8,128)(2,1)S(1)}, bf16[512,384]{1,0:T(8,128)(2,1)S(1)}) custom-call(bf16[768,384]{1,0:T(8,128)(2,1)S(1)} %get-tuple-element.50.h, bf16[384,512]{1,0:T(8,128)(2,1)S(1)} %get-tuple-element.51.give20, ...), custom_call_target="tpu_custom_call" | custom-call | flops 905969664 | tf_op jit(solution)/shard_map/rest/pallas_call | solution.py:335
  76.1 0.0 collective-permute-done.7.give
  76.1 0.2 pair.1
  76.3 2.0 %collective-permute-start.8 = (bf16[1024,384]{1,0:T(8,128)(2,1)S(1)}, bf16[1024,384]{1,0:T(8,128)(2,1)S(1)}, u32[]{:S(2)}, u32[]{:S(2)}) collective-permute-start(bf16[1024,384]{1,0:T(8,128)(2,1)S(1)} %get-tuple-element.61), channel_id=1, source_target_pairs={{0,64},{64,0},{1,65},{65,1},{2,66},{66,2},{3,67},{67,3},{4,68},{68... | collective-permute-start | bytes 2359304 | tf_op jit(solution)/shard_map/ppermute | solution.py:276
  78.4 2.8 %collective-permute-start.10 = (bf16[512,384]{1,0:T(8,128)(2,1)S(1)}, bf16[512,384]{1,0:T(8,128)(2,1)S(1)}, u32[]{:S(2)}, u32[]{:S(2)}) collective-permute-start(bf16[512,384]{1,0:T(8,128)(2,1)S(1)} %get-tuple-element.63), channel_id=1, source_target_pairs={{0,384},{128,0},{256,128},{384,256},{1,385},{129,1},{257,129},{385... | collective-permute-start | bytes 1179656 | tf_op jit(solution)/shard_map/ppermute | solution.py:279
  81.2 3.9 %collective-permute-start.9 = (bf16[512,384]{1,0:T(8,128)(2,1)S(1)}, bf16[512,384]{1,0:T(8,128)(2,1)S(1)}, u32[]{:S(2)}, u32[]{:S(2)}) collective-permute-start(bf16[512,384]{1,0:T(8,128)(2,1)S(1)} %get-tuple-element.62), channel_id=1, source_target_pairs={{0,128},{128,256},{256,384},{384,0},{1,129},{129,257},{257,385},{3... | collective-permute-start | bytes 1179656 | tf_op jit(solution)/shard_map/ppermute | solution.py:279
  85.1 0.0 collective-permute-done.8.give
  85.1 0.8 two_sum.1
  86.0 10.9 %all-to-all-start.3 = ((bf16[64,8,384]{2,1,0:T(8,128)(2,1)}), bf16[64,8,384]{2,1,0:T(8,128)(2,1)S(1)}, u32[]{:S(2)}, u32[]{:S(2)}) async-start(bf16[64,8,384]{2,1,0:T(8,128)(2,1)} %bitcast.11), calls=%async_computation.3 | async-start | bytes 786432 | tf_op jit(solution)/shard_map/all_to_all | solution.py:283
  96.9 4.8 %collective-permute-done.10.three = bf16[512,384]{1,0:T(8,128)(2,1)S(1)} collective-permute-done((bf16[512,384]{1,0:T(8,128)(2,1)S(1)}, bf16[512,384]{1,0:T(8,128)(2,1)S(1)}, u32[]{:S(2)}, u32[]{:S(2)}) %collective-permute-start.10) | collective-permute-done | bytes 393248 | tf_op jit(solution)/shard_map/ppermute | solution.py:279
  101.7 3.1 %collective-permute-done.9.one = bf16[512,384]{1,0:T(8,128)(2,1)S(1)} collective-permute-done((bf16[512,384]{1,0:T(8,128)(2,1)S(1)}, bf16[512,384]{1,0:T(8,128)(2,1)S(1)}, u32[]{:S(2)}, u32[]{:S(2)}) %collective-permute-start.9) | collective-permute-done | bytes 393248 | tf_op jit(solution)/shard_map/ppermute | solution.py:279
  104.8 0.0 copy-start
  104.8 0.9 sum.1
  105.7 6.2 %all-to-all-done.3 = bf16[64,8,384]{2,1,0:T(8,128)(2,1)S(1)} async-done(((bf16[64,8,384]{2,1,0:T(8,128)(2,1)}), bf16[64,8,384]{2,1,0:T(8,128)(2,1)S(1)}, u32[]{:S(2)}, u32[]{:S(2)}) %all-to-all-start.3) | async-done | bytes 393248 | tf_op jit(solution)/shard_map/all_to_all | solution.py:283
  111.8 7.3 %all-to-all-start.2 = ((bf16[64,8,384]{2,1,0:T(8,128)(2,1)}), bf16[64,8,384]{2,1,0:T(8,128)(2,1)S(1)}, u32[]{:S(2)}, u32[]{:S(2)}) async-start(bf16[64,8,384]{2,1,0:T(8,128)(2,1)} %bitcast.9), calls=%async_computation.2 | async-start | bytes 786432 | tf_op jit(solution)/shard_map/all_to_all | solution.py:283
  119.1 0.0 copy-done
  119.1 0.4 mix.1
  119.5 5.7 %collective-permute-start.11 = (bf16[64,256]{1,0:T(8,128)(2,1)S(1)}, bf16[64,256]{1,0:T(8,128)(2,1)S(1)}, u32[]{:S(2)}, u32[]{:S(2)}) collective-permute-start(bf16[64,256]{1,0:T(8,128)(2,1)S(1)} %mix.1), channel_id=1, source_target_pairs={{0,256},{128,384},{256,0},{384,128},{1,257},{129,385},{257,1},{385... | collective-permute-start | bytes 98312 | tf_op jit(solution)/shard_map/ppermute | solution.py:279
  125.2 8.2 %all-to-all-done.2 = bf16[64,8,384]{2,1,0:T(8,128)(2,1)S(1)} async-done(((bf16[64,8,384]{2,1,0:T(8,128)(2,1)}), bf16[64,8,384]{2,1,0:T(8,128)(2,1)S(1)}, u32[]{:S(2)}, u32[]{:S(2)}) %all-to-all-start.2) | async-done | bytes 393248 | tf_op jit(solution)/shard_map/all_to_all | solution.py:283
  133.5 0.0 collective-permute-done.11.other
  133.5 1.0 last.1
Async XLA Ops:
  2.3 29.2 %all-to-all-start = ((bf16[64,8,384]{2,1,0:T(8,128)(2,1)}), bf16[64,8,384]{2,1,0:T(8,128)(2,1)S(1)}, u32[]{:S(2)}, u32[]{:S(2)}) async-start(bf16[64,8,384]{2,1,0:T(8,128)(2,1)} %bitcast.26), calls=%async_computation | async-start | bytes 786432 | tf_op jit(solution)/shard_map/all_to_all | solution.py:283
  17.2 10.0 %collective-permute-start = (bf16[64,256]{1,0:T(8,128)(2,1)}, bf16[64,256]{1,0:T(8,128)(2,1)S(1)}, u32[]{:S(2)}, u32[]{:S(2)}) collective-permute-start(bf16[64,256]{1,0:T(8,128)(2,1)} %tokens.1), channel_id=1, source_target_pairs={{0,256},{128,384},{256,0},{384,128},{1,257},{129,385},{257,1},{385... | collective-permute-start | bytes 98312 | tf_op jit(solution)/shard_map/ppermute | solution.py:279
  27.2 1.0 copy-start.1
  31.5 20.0 %collective-permute-start.2 = (bf16[512,384]{1,0:T(8,128)(2,1)S(1)}, bf16[512,384]{1,0:T(8,128)(2,1)S(1)}, u32[]{:S(2)}, u32[]{:S(2)}) collective-permute-start(bf16[512,384]{1,0:T(8,128)(2,1)S(1)} %bitcast.17), channel_id=1, source_target_pairs={{0,128},{128,256},{256,384},{384,0},{1,129},{129,257},{257,385},{3... | collective-permute-start | bytes 1179656 | tf_op jit(solution)/shard_map/ppermute | solution.py:279
  36.0 20.9 %collective-permute-start.4 = (bf16[512,384]{1,0:T(8,128)(2,1)S(1)}, bf16[512,384]{1,0:T(8,128)(2,1)S(1)}, u32[]{:S(2)}, u32[]{:S(2)}) collective-permute-start(bf16[512,384]{1,0:T(8,128)(2,1)S(1)} %bitcast.18), channel_id=1, source_target_pairs={{0,384},{128,0},{256,128},{384,256},{1,385},{129,1},{257,129},{385... | collective-permute-start | bytes 1179656 | tf_op jit(solution)/shard_map/ppermute | solution.py:279
  39.5 26.2 %all-to-all-start.1 = ((bf16[64,8,384]{2,1,0:T(8,128)(2,1)}), bf16[64,8,384]{2,1,0:T(8,128)(2,1)S(1)}, u32[]{:S(2)}, u32[]{:S(2)}) async-start(bf16[64,8,384]{2,1,0:T(8,128)(2,1)} %bitcast.4), calls=%async_computation.1 | async-start | bytes 786432 | tf_op jit(solution)/shard_map/all_to_all | solution.py:283
  48.5 10.3 %collective-permute-start.1 = (bf16[512,384]{1,0:T(8,128)(2,1)S(1)}, bf16[512,384]{1,0:T(8,128)(2,1)S(1)}, u32[]{:S(2)}, u32[]{:S(2)}) collective-permute-start(bf16[512,384]{1,0:T(8,128)(2,1)S(1)} %bitcast.19), channel_id=1, source_target_pairs={{0,64},{64,0},{1,65},{65,1},{2,66},{66,2},{3,67},{67,3},{4,68},{68... | collective-permute-start | bytes 1179656 | tf_op jit(solution)/shard_map/ppermute | solution.py:276
  51.5 7.2 %collective-permute-start.3 = (bf16[512,384]{1,0:T(8,128)(2,1)S(1)}, bf16[512,384]{1,0:T(8,128)(2,1)S(1)}, u32[]{:S(2)}, u32[]{:S(2)}) collective-permute-start(bf16[512,384]{1,0:T(8,128)(2,1)S(1)} %collective-permute-done.2.refs_2_), channel_id=1, source_target_pairs={{0,64},{64,0},{1,65},{65,1},{2,66},{66,2},{3,67},{67,3},{4,68},{68... | collective-permute-start | bytes 1179656 | tf_op jit(solution)/shard_map/ppermute | solution.py:276
  56.9 3.6 %collective-permute-start.5 = (bf16[512,384]{1,0:T(8,128)(2,1)S(1)}, bf16[512,384]{1,0:T(8,128)(2,1)S(1)}, u32[]{:S(2)}, u32[]{:S(2)}) collective-permute-start(bf16[512,384]{1,0:T(8,128)(2,1)S(1)} %collective-permute-done.4.refs_4_), channel_id=1, source_target_pairs={{0,64},{64,0},{1,65},{65,1},{2,66},{66,2},{3,67},{67,3},{4,68},{68... | collective-permute-start | bytes 1179656 | tf_op jit(solution)/shard_map/ppermute | solution.py:276
  65.6 4.3 %collective-permute-start.6 = (bf16[512,384]{1,0:T(8,128)(2,1)S(1)}, bf16[512,384]{1,0:T(8,128)(2,1)S(1)}, u32[]{:S(2)}, u32[]{:S(2)}) collective-permute-start(bf16[512,384]{1,0:T(8,128)(2,1)S(1)} %bitcast.13), channel_id=1, source_target_pairs={{0,64},{64,0},{1,65},{65,1},{2,66},{66,2},{3,67},{67,3},{4,68},{68... | collective-permute-start | bytes 1179656 | tf_op jit(solution)/shard_map/ppermute | solution.py:276
  71.7 4.5 %collective-permute-start.7 = (bf16[1024,384]{1,0:T(8,128)(2,1)S(1)}, bf16[1024,384]{1,0:T(8,128)(2,1)S(1)}, u32[]{:S(2)}, u32[]{:S(2)}) collective-permute-start(bf16[1024,384]{1,0:T(8,128)(2,1)S(1)} %get-tuple-element.57), channel_id=1, source_target_pairs={{0,64},{64,0},{1,65},{65,1},{2,66},{66,2},{3,67},{67,3},{4,68},{68... | collective-permute-start | bytes 2359304 | tf_op jit(solution)/shard_map/ppermute | solution.py:276
  76.3 8.8 %collective-permute-start.8 = (bf16[1024,384]{1,0:T(8,128)(2,1)S(1)}, bf16[1024,384]{1,0:T(8,128)(2,1)S(1)}, u32[]{:S(2)}, u32[]{:S(2)}) collective-permute-start(bf16[1024,384]{1,0:T(8,128)(2,1)S(1)} %get-tuple-element.61), channel_id=1, source_target_pairs={{0,64},{64,0},{1,65},{65,1},{2,66},{66,2},{3,67},{67,3},{4,68},{68... | collective-permute-start | bytes 2359304 | tf_op jit(solution)/shard_map/ppermute | solution.py:276
  78.4 23.3 %collective-permute-start.10 = (bf16[512,384]{1,0:T(8,128)(2,1)S(1)}, bf16[512,384]{1,0:T(8,128)(2,1)S(1)}, u32[]{:S(2)}, u32[]{:S(2)}) collective-permute-start(bf16[512,384]{1,0:T(8,128)(2,1)S(1)} %get-tuple-element.63), channel_id=1, source_target_pairs={{0,384},{128,0},{256,128},{384,256},{1,385},{129,1},{257,129},{385... | collective-permute-start | bytes 1179656 | tf_op jit(solution)/shard_map/ppermute | solution.py:279
  81.2 23.5 %collective-permute-start.9 = (bf16[512,384]{1,0:T(8,128)(2,1)S(1)}, bf16[512,384]{1,0:T(8,128)(2,1)S(1)}, u32[]{:S(2)}, u32[]{:S(2)}) collective-permute-start(bf16[512,384]{1,0:T(8,128)(2,1)S(1)} %get-tuple-element.62), channel_id=1, source_target_pairs={{0,128},{128,256},{256,384},{384,0},{1,129},{129,257},{257,385},{3... | collective-permute-start | bytes 1179656 | tf_op jit(solution)/shard_map/ppermute | solution.py:279
  86.0 25.9 %all-to-all-start.3 = ((bf16[64,8,384]{2,1,0:T(8,128)(2,1)}), bf16[64,8,384]{2,1,0:T(8,128)(2,1)S(1)}, u32[]{:S(2)}, u32[]{:S(2)}) async-start(bf16[64,8,384]{2,1,0:T(8,128)(2,1)} %bitcast.11), calls=%async_computation.3 | async-start | bytes 786432 | tf_op jit(solution)/shard_map/all_to_all | solution.py:283
  104.8 14.4 %copy-start = (bf16[512,192]{1,0:T(8,128)(2,1)S(1)}, bf16[512,192]{1,0:T(8,128)(2,1)}, u32[]{:S(2)}) copy-start(bf16[512,192]{1,0:T(8,128)(2,1)} %get-tuple-element.35.mix) | copy-start | bytes 589828
  111.8 21.6 %all-to-all-start.2 = ((bf16[64,8,384]{2,1,0:T(8,128)(2,1)}), bf16[64,8,384]{2,1,0:T(8,128)(2,1)S(1)}, u32[]{:S(2)}, u32[]{:S(2)}) async-start(bf16[64,8,384]{2,1,0:T(8,128)(2,1)} %bitcast.9), calls=%async_computation.2 | async-start | bytes 786432 | tf_op jit(solution)/shard_map/all_to_all | solution.py:283
  119.5 14.0 %collective-permute-start.11 = (bf16[64,256]{1,0:T(8,128)(2,1)S(1)}, bf16[64,256]{1,0:T(8,128)(2,1)S(1)}, u32[]{:S(2)}, u32[]{:S(2)}) collective-permute-start(bf16[64,256]{1,0:T(8,128)(2,1)S(1)} %mix.1), channel_id=1, source_target_pairs={{0,256},{128,384},{256,0},{384,128},{1,257},{129,385},{257,1},{385... | collective-permute-start | bytes 98312 | tf_op jit(solution)/shard_map/ppermute | solution.py:279

commit v6 on v5

--- a/solution.py
+++ b/solution.py
@@ -57,7 +57,7 @@
     wire[:, band:] = dot(pick[:, rows:], halves).astype(BF)
 
 
-def pick_kernel(ids, probs, tokens, wire, pick, mix):
+def lists_kernel(ids, probs, pick, mix):
     fanout, rows = ids.shape
     experts = pick.shape[0] // NEAR
     at = lax.broadcasted_iota(jnp.int32, (experts, rows), 0)
@@ -90,7 +90,12 @@
     far = seats == place % FAR + NEAR
     for i, hit in enumerate((seats == place, far & (place < FAR), far & (place >= FAR))):
         pick[:, i * rows : (i + 1) * rows] = hit.astype(F32).astype(BF)
-        mix[:, i * rows : (i + 1) * rows] = jnp.where(hit, weights, 0.0).astype(BF)
+        if mix is not None:
+            mix[:, i * rows : (i + 1) * rows] = jnp.where(hit, weights, 0.0).astype(BF)
+
+
+def pick_kernel(ids, probs, tokens, wire, pick):
+    lists_kernel(ids, probs, pick, None)
     fill(pick, tokens, wire)
 
 
@@ -292,9 +297,11 @@
     work = 2 * experts * SEATS * band * wide
     sems = lambda n: pltpu.SemaphoreType.DMA((n,))
     other = shift(tokens, 2)
-    wire0, pick, mix = call(pick_kernel, [wire, lists, lists], "pick", [VM] * 3, limit=PICK_LIMIT)(
+    (wire0,) = call(pick_kernel, [wire], "pick", [VM] * 3, limit=PICK_LIMIT, scratch=[pltpu.VMEM(*lists)])(
         expert_ids.T, router_probs.T, tokens
     )
+    ids, wire0 = tie((expert_ids.T, wire0))
+    pick, mix = call(lists_kernel, [lists] * 2, "lists", [VM] * 2, limit=PICK_LIMIT)(ids, router_probs.T)
     got0 = trade(wire0)
     (wire2,) = call(fill, [wire], "wire", [VM] * 2)(pick, other)
     got0, wire2 = tie((got0, wire2))

time: 135 us -> 135 us (level)
  waiting for transfers between devices: 33.9 us -> 32 us
  Pallas kernels: 17.9 us -> 19.7 us
    ppermute x6, waiting for transfers between devices: 15.6 us -> 13.6 us  [shift(): return lax.ppermute(x, 'yh', [(i, (i + k) % LINE) for i in range(LINE)])]
    pallas_call x1 -> x2, Pallas kernels: 2.25 us -> 4.03 us  [the longest x1 2.12 us: body(): call(pick_kernel, [wire], 'pick', [VM] * 3, limit=PICK_LIMIT, scratch=[pl...]
  transfers between devices with their start and end apart: 16 -> 16, of which waited for: 9 -> 9; matrix products, arithmetic and copies ran while one was open for 0% -> 0% of each run, Pallas kernels for 9% -> 11%
where the time goes in v6:
time: 135 us; the launch traced here: 134 us
  starting transfers between devices  81.5 us (60%)
  waiting for transfers between devices  32 us (24%)
  Pallas kernels  19.7 us (15%)
    all_to_all x4, starting transfers between devices, trade(): y = lax.all_to_all(y, TRADE, split_axis=0, concat_axis=0, tiled=True)  42.1 us
    ppermute x6, starting transfers between devices, shift(): return lax.ppermute(x, 'yh', [(i, (i + k) % LINE) for i in range(LINE)])  27.3 us
    all_to_all x4, waiting for transfers between devices, trade(): y = lax.all_to_all(y, TRADE, split_axis=0, concat_axis=0, tiled=True)  16.7 us
    ppermute x6, waiting for transfers between devices, shift(): return lax.ppermute(x, 'yh', [(i, (i + k) % LINE) for i in range(LINE)])  13.6 us
    ppermute x6, starting transfers between devices, swap(): return lax.ppermute(x, 'core', [(0, 1), (1, 0)])  12.1 us
    pallas_call x1, Pallas kernels, body(): call(plus_kernel, sums, 'plus', [ANY] * 8, limit=PLUS_LIMIT, flops=SHORT,...  5.14 us
  transfers between devices with their start and end apart: 16, of which 9 were waited for; matrix products, arithmetic and copies ran while one was open for 0% of the time, Pallas kernels for 11%

profile of v6, /device:TPU:8, one launch (start us, length us, event | category | flops | bytes accessed | tf_op | source)
XLA Modules:
  0.0 134.3 jit_solution(5624953793589564383)
XLA Ops:
  0.0 2.1 %pick.1 = bf16[512,384]{1,0:T(8,128)(2,1)} custom-call(s32[8,64]{1,0:T(8,128)} %bitcast.27, f32[8,64]{1,0:T(8,128)} %bitcast.29, bf16[64,256]{1,0:T(8,128)(2,1)} %tokens.1), custom_call_target="tpu_custom_call" | custom-call | tf_op jit(solution)/shard_map/pick/pallas_call | solution.py:300
  2.1 14.9 %all-to-all-start = ((bf16[64,8,384]{2,1,0:T(8,128)(2,1)}), bf16[64,8,384]{2,1,0:T(8,128)(2,1)S(1)}, u32[]{:S(2)}, u32[]{:S(2)}) async-start(bf16[64,8,384]{2,1,0:T(8,128)(2,1)} %bitcast.26), calls=%async_computation | async-start | bytes 786432 | tf_op jit(solution)/shard_map/all_to_all | solution.py:288
  17.0 6.8 %collective-permute-start = (bf16[64,256]{1,0:T(8,128)(2,1)}, bf16[64,256]{1,0:T(8,128)(2,1)S(1)}, u32[]{:S(2)}, u32[]{:S(2)}) collective-permute-start(bf16[64,256]{1,0:T(8,128)(2,1)} %tokens.1), channel_id=1, source_target_pairs={{0,256},{128,384},{256,0},{384,128},{1,257},{129,385},{257,1},{385... | collective-permute-start | bytes 98312 | tf_op jit(solution)/shard_map/ppermute | solution.py:284
  23.9 1.9 %lists.1 = (bf16[512,192]{1,0:T(8,128)(2,1)}, bf16[512,192]{1,0:T(8,128)(2,1)}) custom-call(s32[8,64]{1,0:T(8,128)} %bitcast.28, f32[8,64]{1,0:T(8,128)} %bitcast.30), custom_call_target="tpu_custom_call" | custom-call | tf_op jit(solution)/shard_map/lists/pallas_call | solution.py:304
  25.8 1.3 collective-permute-done.tokens
  27.1 0.0 copy-start.1
  27.1 0.9 copy-done.1
  28.0 1.1 wire.1
  29.1 2.3 %all-to-all-done = bf16[64,8,384]{2,1,0:T(8,128)(2,1)S(1)} async-done(((bf16[64,8,384]{2,1,0:T(8,128)(2,1)}), bf16[64,8,384]{2,1,0:T(8,128)(2,1)S(1)}, u32[]{:S(2)}, u32[]{:S(2)}) %all-to-all-start) | async-done | bytes 393248 | tf_op jit(solution)/shard_map/all_to_all | solution.py:288
  31.4 4.5 %collective-permute-start.2 = (bf16[512,384]{1,0:T(8,128)(2,1)S(1)}, bf16[512,384]{1,0:T(8,128)(2,1)S(1)}, u32[]{:S(2)}, u32[]{:S(2)}) collective-permute-start(bf16[512,384]{1,0:T(8,128)(2,1)S(1)} %bitcast.17), channel_id=1, source_target_pairs={{0,128},{128,256},{256,384},{384,0},{1,129},{129,257},{257,385},{3... | collective-permute-start | bytes 1179656 | tf_op jit(solution)/shard_map/ppermute | solution.py:284
  35.9 3.5 %collective-permute-start.4 = (bf16[512,384]{1,0:T(8,128)(2,1)S(1)}, bf16[512,384]{1,0:T(8,128)(2,1)S(1)}, u32[]{:S(2)}, u32[]{:S(2)}) collective-permute-start(bf16[512,384]{1,0:T(8,128)(2,1)S(1)} %bitcast.18), channel_id=1, source_target_pairs={{0,384},{128,0},{256,128},{384,256},{1,385},{129,1},{257,129},{385... | collective-permute-start | bytes 1179656 | tf_op jit(solution)/shard_map/ppermute | solution.py:284
  39.3 9.0 %all-to-all-start.1 = ((bf16[64,8,384]{2,1,0:T(8,128)(2,1)}), bf16[64,8,384]{2,1,0:T(8,128)(2,1)S(1)}, u32[]{:S(2)}, u32[]{:S(2)}) async-start(bf16[64,8,384]{2,1,0:T(8,128)(2,1)} %bitcast.4), calls=%async_computation.1 | async-start | bytes 786432 | tf_op jit(solution)/shard_map/all_to_all | solution.py:288
  48.3 1.9 %collective-permute-start.1 = (bf16[512,384]{1,0:T(8,128)(2,1)S(1)}, bf16[512,384]{1,0:T(8,128)(2,1)S(1)}, u32[]{:S(2)}, u32[]{:S(2)}) collective-permute-start(bf16[512,384]{1,0:T(8,128)(2,1)S(1)} %bitcast.19), channel_id=1, source_target_pairs={{0,64},{64,0},{1,65},{65,1},{2,66},{66,2},{3,67},{67,3},{4,68},{68... | collective-permute-start | bytes 1179656 | tf_op jit(solution)/shard_map/ppermute | solution.py:281
  50.3 1.1 collective-permute-done.2.refs_2_
  51.4 1.9 %collective-permute-start.3 = (bf16[512,384]{1,0:T(8,128)(2,1)S(1)}, bf16[512,384]{1,0:T(8,128)(2,1)S(1)}, u32[]{:S(2)}, u32[]{:S(2)}) collective-permute-start(bf16[512,384]{1,0:T(8,128)(2,1)S(1)} %collective-permute-done.2.refs_2_), channel_id=1, source_target_pairs={{0,64},{64,0},{1,65},{65,1},{2,66},{66,2},{3,67},{67,3},{4,68},{68... | collective-permute-start | bytes 1179656 | tf_op jit(solution)/shard_map/ppermute | solution.py:281
  53.3 3.4 %collective-permute-done.4.refs_4_ = bf16[512,384]{1,0:T(8,128)(2,1)S(1)} collective-permute-done((bf16[512,384]{1,0:T(8,128)(2,1)S(1)}, bf16[512,384]{1,0:T(8,128)(2,1)S(1)}, u32[]{:S(2)}, u32[]{:S(2)}) %collective-permute-start.4) | collective-permute-done | bytes 393248 | tf_op jit(solution)/shard_map/ppermute | solution.py:284
  56.7 1.9 %collective-permute-start.5 = (bf16[512,384]{1,0:T(8,128)(2,1)S(1)}, bf16[512,384]{1,0:T(8,128)(2,1)S(1)}, u32[]{:S(2)}, u32[]{:S(2)}) collective-permute-start(bf16[512,384]{1,0:T(8,128)(2,1)S(1)} %collective-permute-done.4.refs_4_), channel_id=1, source_target_pairs={{0,64},{64,0},{1,65},{65,1},{2,66},{66,2},{3,67},{67,3},{4,68},{68... | collective-permute-start | bytes 1179656 | tf_op jit(solution)/shard_map/ppermute | solution.py:281
  58.6 0.0 collective-permute-done.1.refs_1_
  58.7 0.0 collective-permute-done.3.refs_3_
  58.7 1.7 %collective-permute-done.5.refs_5_ = bf16[512,384]{1,0:T(8,128)(2,1)S(1)} collective-permute-done((bf16[512,384]{1,0:T(8,128)(2,1)S(1)}, bf16[512,384]{1,0:T(8,128)(2,1)S(1)}, u32[]{:S(2)}, u32[]{:S(2)}) %collective-permute-start.5) | collective-permute-done | bytes 393248 | tf_op jit(solution)/shard_map/ppermute | solution.py:281
  60.3 5.1 %plus.1 = (f32[512,768]{1,0:T(8,128)}, f32[256,768]{1,0:T(8,128)S(1)}) custom-call(bf16[2048,384]{1,0:T(8,128)(2,1)} %bitcast.21, bf16[2048,384]{1,0:T(8,128)(2,1)} %bitcast.23, bf16[512,384]{1,0:T(8,128)(2,1)S(1)} %bitcast.20, bf16[512,384]{1,0:T(8,128)(2,1)S(1)} %collective-permute-done.1.refs_1_, bf16[512,384]{1,0:T(8,128)(2,1)S(1)} %collective-permute-done.2.refs_2_, ...), custom_call_target="tpu_custom_call" | custom-call | flops 2000000000 | tf_op jit(solution)/shard_map/plus/pallas_call | solution.py:311
  65.5 0.0 all-to-all-done.1
  65.5 2.0 %collective-permute-start.6 = (bf16[512,384]{1,0:T(8,128)(2,1)S(1)}, bf16[512,384]{1,0:T(8,128)(2,1)S(1)}, u32[]{:S(2)}, u32[]{:S(2)}) collective-permute-start(bf16[512,384]{1,0:T(8,128)(2,1)S(1)} %bitcast.13), channel_id=1, source_target_pairs={{0,64},{64,0},{1,65},{65,1},{2,66},{66,2},{3,67},{67,3},{4,68},{68... | collective-permute-start | bytes 1179656 | tf_op jit(solution)/shard_map/ppermute | solution.py:281
  67.5 2.2 %load.1 = (f32[256,768]{1,0:T(8,128)S(1)}, f32[256,768]{1,0:T(8,128)S(1)}, f32[256,768]{1,0:T(8,128)S(1)}, bf16[512,768]{1,0:T(8,128)(2,1)S(1)}, bf16[384,512]{1...) custom-call(bf16[2048,384]{1,0:T(8,128)(2,1)} %bitcast.22, ...), custom_call_target="tpu_custom_call" | custom-call | tf_op jit(solution)/shard_map/load/pallas_call | solution.py:330
  69.8 0.0 collective-permute-done.6.sib
  69.8 1.7 %hidden.1 = (bf16[768,384]{1,0:T(8,128)(2,1)S(1)}, bf16[1024,384]{1,0:T(8,128)(2,1)S(1)}) custom-call(bf16[512,384]{1,0:T(8,128)(2,1)S(1)} %bitcast.14, bf16[512,384]{1,0:T(8,128)(2,1)S(1)} %collective-permute-done.6.sib, f32[256,768]{1,0:T(8,128)S(1)} %get-tuple-element.47.acc_top, f32[256,768]{1,0:T(8,128)S(1)} %get-tuple-element.48.acc_low, ...), custom_call_target="tpu_custom_call" | custom-call | flops 905969664 | tf_op jit(solution)/shard_map/hidden/pallas_call | solution.py:338
  71.5 2.3 %collective-permute-start.7 = (bf16[1024,384]{1,0:T(8,128)(2,1)S(1)}, bf16[1024,384]{1,0:T(8,128)(2,1)S(1)}, u32[]{:S(2)}, u32[]{:S(2)}) collective-permute-start(bf16[1024,384]{1,0:T(8,128)(2,1)S(1)} %get-tuple-element.59), channel_id=1, source_target_pairs={{0,64},{64,0},{1,65},{65,1},{2,66},{66,2},{3,67},{67,3},{4,68},{68... | collective-permute-start | bytes 2359304 | tf_op jit(solution)/shard_map/ppermute | solution.py:281
  73.8 2.2 %rest.1 = (bf16[1024,384]{1,0:T(8,128)(2,1)S(1)}, bf16[512,384]{1,0:T(8,128)(2,1)S(1)}, bf16[512,384]{1,0:T(8,128)(2,1)S(1)}, bf16[512,384]{1,0:T(8,128)(2,1)S(1)}, bf16[512,384]{1,0:T(8,128)(2,1)S(1)}) custom-call(bf16[768,384]{1,0:T(8,128)(2,1)S(1)} %get-tuple-element.52.h, bf16[384,512]{1,0:T(8,128)(2,1)S(1)} %get-tuple-element.53.give20, ...), custom_call_target="tpu_custom_call" | custom-call | flops 905969664 | tf_op jit(solution)/shard_map/rest/pallas_call | solution.py:342
  76.0 0.0 collective-permute-done.7.give
  76.0 0.2 pair.1
  76.2 2.0 %collective-permute-start.8 = (bf16[1024,384]{1,0:T(8,128)(2,1)S(1)}, bf16[1024,384]{1,0:T(8,128)(2,1)S(1)}, u32[]{:S(2)}, u32[]{:S(2)}) collective-permute-start(bf16[1024,384]{1,0:T(8,128)(2,1)S(1)} %get-tuple-element.63), channel_id=1, source_target_pairs={{0,64},{64,0},{1,65},{65,1},{2,66},{66,2},{3,67},{67,3},{4,68},{68... | collective-permute-start | bytes 2359304 | tf_op jit(solution)/shard_map/ppermute | solution.py:281
  78.2 2.9 %collective-permute-start.10 = (bf16[512,384]{1,0:T(8,128)(2,1)S(1)}, bf16[512,384]{1,0:T(8,128)(2,1)S(1)}, u32[]{:S(2)}, u32[]{:S(2)}) collective-permute-start(bf16[512,384]{1,0:T(8,128)(2,1)S(1)} %get-tuple-element.65), channel_id=1, source_target_pairs={{0,384},{128,0},{256,128},{384,256},{1,385},{129,1},{257,129},{385... | collective-permute-start | bytes 1179656 | tf_op jit(solution)/shard_map/ppermute | solution.py:284
  81.1 3.9 %collective-permute-start.9 = (bf16[512,384]{1,0:T(8,128)(2,1)S(1)}, bf16[512,384]{1,0:T(8,128)(2,1)S(1)}, u32[]{:S(2)}, u32[]{:S(2)}) collective-permute-start(bf16[512,384]{1,0:T(8,128)(2,1)S(1)} %get-tuple-element.64), channel_id=1, source_target_pairs={{0,128},{128,256},{256,384},{384,0},{1,129},{129,257},{257,385},{3... | collective-permute-start | bytes 1179656 | tf_op jit(solution)/shard_map/ppermute | solution.py:284
  85.0 0.0 collective-permute-done.8.give
  85.0 0.8 two_sum.1
  85.9 10.9 %all-to-all-start.3 = ((bf16[64,8,384]{2,1,0:T(8,128)(2,1)}), bf16[64,8,384]{2,1,0:T(8,128)(2,1)S(1)}, u32[]{:S(2)}, u32[]{:S(2)}) async-start(bf16[64,8,384]{2,1,0:T(8,128)(2,1)} %bitcast.11), calls=%async_computation.3 | async-start | bytes 786432 | tf_op jit(solution)/shard_map/all_to_all | solution.py:288
  96.8 4.7 %collective-permute-done.10.three = bf16[512,384]{1,0:T(8,128)(2,1)S(1)} collective-permute-done((bf16[512,384]{1,0:T(8,128)(2,1)S(1)}, bf16[512,384]{1,0:T(8,128)(2,1)S(1)}, u32[]{:S(2)}, u32[]{:S(2)}) %collective-permute-start.10) | collective-permute-done | bytes 393248 | tf_op jit(solution)/shard_map/ppermute | solution.py:284
  101.5 3.0 %collective-permute-done.9.one = bf16[512,384]{1,0:T(8,128)(2,1)S(1)} collective-permute-done((bf16[512,384]{1,0:T(8,128)(2,1)S(1)}, bf16[512,384]{1,0:T(8,128)(2,1)S(1)}, u32[]{:S(2)}, u32[]{:S(2)}) %collective-permute-start.9) | collective-permute-done | bytes 393248 | tf_op jit(solution)/shard_map/ppermute | solution.py:284
  104.6 0.0 copy-start
  104.6 0.9 sum.1
  105.5 6.2 %all-to-all-done.3 = bf16[64,8,384]{2,1,0:T(8,128)(2,1)S(1)} async-done(((bf16[64,8,384]{2,1,0:T(8,128)(2,1)}), bf16[64,8,384]{2,1,0:T(8,128)(2,1)S(1)}, u32[]{:S(2)}, u32[]{:S(2)}) %all-to-all-start.3) | async-done | bytes 393248 | tf_op jit(solution)/shard_map/all_to_all | solution.py:288
  111.7 7.3 %all-to-all-start.2 = ((bf16[64,8,384]{2,1,0:T(8,128)(2,1)}), bf16[64,8,384]{2,1,0:T(8,128)(2,1)S(1)}, u32[]{:S(2)}, u32[]{:S(2)}) async-start(bf16[64,8,384]{2,1,0:T(8,128)(2,1)} %bitcast.9), calls=%async_computation.2 | async-start | bytes 786432 | tf_op jit(solution)/shard_map/all_to_all | solution.py:288
  119.0 0.0 copy-done
  119.0 0.4 mix.1
  119.4 5.7 %collective-permute-start.11 = (bf16[64,256]{1,0:T(8,128)(2,1)S(1)}, bf16[64,256]{1,0:T(8,128)(2,1)S(1)}, u32[]{:S(2)}, u32[]{:S(2)}) collective-permute-start(bf16[64,256]{1,0:T(8,128)(2,1)S(1)} %mix.1), channel_id=1, source_target_pairs={{0,256},{128,384},{256,0},{384,128},{1,257},{129,385},{257,1},{385... | collective-permute-start | bytes 98312 | tf_op jit(solution)/shard_map/ppermute | solution.py:284
  125.1 8.2 %all-to-all-done.2 = bf16[64,8,384]{2,1,0:T(8,128)(2,1)S(1)} async-done(((bf16[64,8,384]{2,1,0:T(8,128)(2,1)}), bf16[64,8,384]{2,1,0:T(8,128)(2,1)S(1)}, u32[]{:S(2)}, u32[]{:S(2)}) %all-to-all-start.2) | async-done | bytes 393248 | tf_op jit(solution)/shard_map/all_to_all | solution.py:288
  133.3 0.0 collective-permute-done.11.other
  133.3 1.0 last.1
Async XLA Ops:
  2.1 29.2 %all-to-all-start = ((bf16[64,8,384]{2,1,0:T(8,128)(2,1)}), bf16[64,8,384]{2,1,0:T(8,128)(2,1)S(1)}, u32[]{:S(2)}, u32[]{:S(2)}) async-start(bf16[64,8,384]{2,1,0:T(8,128)(2,1)} %bitcast.26), calls=%async_computation | async-start | bytes 786432 | tf_op jit(solution)/shard_map/all_to_all | solution.py:288
  17.0 10.0 %collective-permute-start = (bf16[64,256]{1,0:T(8,128)(2,1)}, bf16[64,256]{1,0:T(8,128)(2,1)S(1)}, u32[]{:S(2)}, u32[]{:S(2)}) collective-permute-start(bf16[64,256]{1,0:T(8,128)(2,1)} %tokens.1), channel_id=1, source_target_pairs={{0,256},{128,384},{256,0},{384,128},{1,257},{129,385},{257,1},{385... | collective-permute-start | bytes 98312 | tf_op jit(solution)/shard_map/ppermute | solution.py:284
  27.1 1.0 copy-start.1
  31.4 20.0 %collective-permute-start.2 = (bf16[512,384]{1,0:T(8,128)(2,1)S(1)}, bf16[512,384]{1,0:T(8,128)(2,1)S(1)}, u32[]{:S(2)}, u32[]{:S(2)}) collective-permute-start(bf16[512,384]{1,0:T(8,128)(2,1)S(1)} %bitcast.17), channel_id=1, source_target_pairs={{0,128},{128,256},{256,384},{384,0},{1,129},{129,257},{257,385},{3... | collective-permute-start | bytes 1179656 | tf_op jit(solution)/shard_map/ppermute | solution.py:284
  35.9 20.9 %collective-permute-start.4 = (bf16[512,384]{1,0:T(8,128)(2,1)S(1)}, bf16[512,384]{1,0:T(8,128)(2,1)S(1)}, u32[]{:S(2)}, u32[]{:S(2)}) collective-permute-start(bf16[512,384]{1,0:T(8,128)(2,1)S(1)} %bitcast.18), channel_id=1, source_target_pairs={{0,384},{128,0},{256,128},{384,256},{1,385},{129,1},{257,129},{385... | collective-permute-start | bytes 1179656 | tf_op jit(solution)/shard_map/ppermute | solution.py:284
  39.3 26.2 %all-to-all-start.1 = ((bf16[64,8,384]{2,1,0:T(8,128)(2,1)}), bf16[64,8,384]{2,1,0:T(8,128)(2,1)S(1)}, u32[]{:S(2)}, u32[]{:S(2)}) async-start(bf16[64,8,384]{2,1,0:T(8,128)(2,1)} %bitcast.4), calls=%async_computation.1 | async-start | bytes 786432 | tf_op jit(solution)/shard_map/all_to_all | solution.py:288
  48.3 10.3 %collective-permute-start.1 = (bf16[512,384]{1,0:T(8,128)(2,1)S(1)}, bf16[512,384]{1,0:T(8,128)(2,1)S(1)}, u32[]{:S(2)}, u32[]{:S(2)}) collective-permute-start(bf16[512,384]{1,0:T(8,128)(2,1)S(1)} %bitcast.19), channel_id=1, source_target_pairs={{0,64},{64,0},{1,65},{65,1},{2,66},{66,2},{3,67},{67,3},{4,68},{68... | collective-permute-start | bytes 1179656 | tf_op jit(solution)/shard_map/ppermute | solution.py:281
  51.4 7.2 %collective-permute-start.3 = (bf16[512,384]{1,0:T(8,128)(2,1)S(1)}, bf16[512,384]{1,0:T(8,128)(2,1)S(1)}, u32[]{:S(2)}, u32[]{:S(2)}) collective-permute-start(bf16[512,384]{1,0:T(8,128)(2,1)S(1)} %collective-permute-done.2.refs_2_), channel_id=1, source_target_pairs={{0,64},{64,0},{1,65},{65,1},{2,66},{66,2},{3,67},{67,3},{4,68},{68... | collective-permute-start | bytes 1179656 | tf_op jit(solution)/shard_map/ppermute | solution.py:281
  56.7 3.6 %collective-permute-start.5 = (bf16[512,384]{1,0:T(8,128)(2,1)S(1)}, bf16[512,384]{1,0:T(8,128)(2,1)S(1)}, u32[]{:S(2)}, u32[]{:S(2)}) collective-permute-start(bf16[512,384]{1,0:T(8,128)(2,1)S(1)} %collective-permute-done.4.refs_4_), channel_id=1, source_target_pairs={{0,64},{64,0},{1,65},{65,1},{2,66},{66,2},{3,67},{67,3},{4,68},{68... | collective-permute-start | bytes 1179656 | tf_op jit(solution)/shard_map/ppermute | solution.py:281
  65.5 4.3 %collective-permute-start.6 = (bf16[512,384]{1,0:T(8,128)(2,1)S(1)}, bf16[512,384]{1,0:T(8,128)(2,1)S(1)}, u32[]{:S(2)}, u32[]{:S(2)}) collective-permute-start(bf16[512,384]{1,0:T(8,128)(2,1)S(1)} %bitcast.13), channel_id=1, source_target_pairs={{0,64},{64,0},{1,65},{65,1},{2,66},{66,2},{3,67},{67,3},{4,68},{68... | collective-permute-start | bytes 1179656 | tf_op jit(solution)/shard_map/ppermute | solution.py:281
  71.5 4.4 %collective-permute-start.7 = (bf16[1024,384]{1,0:T(8,128)(2,1)S(1)}, bf16[1024,384]{1,0:T(8,128)(2,1)S(1)}, u32[]{:S(2)}, u32[]{:S(2)}) collective-permute-start(bf16[1024,384]{1,0:T(8,128)(2,1)S(1)} %get-tuple-element.59), channel_id=1, source_target_pairs={{0,64},{64,0},{1,65},{65,1},{2,66},{66,2},{3,67},{67,3},{4,68},{68... | collective-permute-start | bytes 2359304 | tf_op jit(solution)/shard_map/ppermute | solution.py:281
  76.2 8.8 %collective-permute-start.8 = (bf16[1024,384]{1,0:T(8,128)(2,1)S(1)}, bf16[1024,384]{1,0:T(8,128)(2,1)S(1)}, u32[]{:S(2)}, u32[]{:S(2)}) collective-permute-start(bf16[1024,384]{1,0:T(8,128)(2,1)S(1)} %get-tuple-element.63), channel_id=1, source_target_pairs={{0,64},{64,0},{1,65},{65,1},{2,66},{66,2},{3,67},{67,3},{4,68},{68... | collective-permute-start | bytes 2359304 | tf_op jit(solution)/shard_map/ppermute | solution.py:281
  78.2 23.3 %collective-permute-start.10 = (bf16[512,384]{1,0:T(8,128)(2,1)S(1)}, bf16[512,384]{1,0:T(8,128)(2,1)S(1)}, u32[]{:S(2)}, u32[]{:S(2)}) collective-permute-start(bf16[512,384]{1,0:T(8,128)(2,1)S(1)} %get-tuple-element.65), channel_id=1, source_target_pairs={{0,384},{128,0},{256,128},{384,256},{1,385},{129,1},{257,129},{385... | collective-permute-start | bytes 1179656 | tf_op jit(solution)/shard_map/ppermute | solution.py:284
  81.1 23.5 %collective-permute-start.9 = (bf16[512,384]{1,0:T(8,128)(2,1)S(1)}, bf16[512,384]{1,0:T(8,128)(2,1)S(1)}, u32[]{:S(2)}, u32[]{:S(2)}) collective-permute-start(bf16[512,384]{1,0:T(8,128)(2,1)S(1)} %get-tuple-element.64), channel_id=1, source_target_pairs={{0,128},{128,256},{256,384},{384,0},{1,129},{129,257},{257,385},{3... | collective-permute-start | bytes 1179656 | tf_op jit(solution)/shard_map/ppermute | solution.py:284
  85.9 25.9 %all-to-all-start.3 = ((bf16[64,8,384]{2,1,0:T(8,128)(2,1)}), bf16[64,8,384]{2,1,0:T(8,128)(2,1)S(1)}, u32[]{:S(2)}, u32[]{:S(2)}) async-start(bf16[64,8,384]{2,1,0:T(8,128)(2,1)} %bitcast.11), calls=%async_computation.3 | async-start | bytes 786432 | tf_op jit(solution)/shard_map/all_to_all | solution.py:288
  104.6 14.4 %copy-start = (bf16[512,192]{1,0:T(8,128)(2,1)S(1)}, bf16[512,192]{1,0:T(8,128)(2,1)}, u32[]{:S(2)}) copy-start(bf16[512,192]{1,0:T(8,128)(2,1)} %get-tuple-element.37.mix) | copy-start | bytes 589828
  111.7 21.6 %all-to-all-start.2 = ((bf16[64,8,384]{2,1,0:T(8,128)(2,1)}), bf16[64,8,384]{2,1,0:T(8,128)(2,1)S(1)}, u32[]{:S(2)}, u32[]{:S(2)}) async-start(bf16[64,8,384]{2,1,0:T(8,128)(2,1)} %bitcast.9), calls=%async_computation.2 | async-start | bytes 786432 | tf_op jit(solution)/shard_map/all_to_all | solution.py:288
  119.4 14.0 %collective-permute-start.11 = (bf16[64,256]{1,0:T(8,128)(2,1)S(1)}, bf16[64,256]{1,0:T(8,128)(2,1)S(1)}, u32[]{:S(2)}, u32[]{:S(2)}) collective-permute-start(bf16[64,256]{1,0:T(8,128)(2,1)S(1)} %mix.1), channel_id=1, source_target_pairs={{0,256},{128,384},{256,0},{384,128},{1,257},{129,385},{257,1},{385... | collective-permute-start | bytes 98312 | tf_op jit(solution)/shard_map/ppermute | solution.py:284
